TPU v7x, 512 devices: a whole 4x8x8 slice. The times are simulated.
512 devices in a mesh: dp: 2 (over y_hi), segment: 8 (over x, core), tile: 32 (over y_lo, z).
Axes of the slice: x: 4, y: 8 (y_hi: 2, y_lo: 4; y = y_hi * 4 + y_lo), z: 8, core: 2. Of those that a mesh axis runs over, the one named last changes fastest.
Arguments:
- inputs: bfloat16 [4, 32, 32, 32, 128], P('dp', 'tile'), may hold values from -6 to 6
- neighbor: int32 [32, 4], replicated, may hold values from 0 to 31, as said below
- edge_of: int32 [32, 4], replicated, may hold values from 0 to 3
- reverse: int32 [32, 4], replicated, may hold values from 0 to 1, as said below
- weights: bfloat16 [8, 1152, 128], P('segment'), may hold values from -0.1875 to 0.1875
- cotangent: bfloat16 [8, 4, 32, 32, 32, 128], P('segment', 'dp', 'tile'), may hold values from -6 to 6
Outputs:
- levels: bfloat16 [8, 4, 32, 32, 32, 128], P('segment', 'dp', 'tile')
- grads: float32 [8, 1152, 128], P('segment')
Inputs may be any that keep to these rules, and one draw needn't show every extreme that they name: The seams pair the edges: every (tile, edge) slot is named by exactly one slot, and if (t, d) names (neighbor[t, d], edge_of[t, d]) = (u, e), then (u, e) names (t, d). reverse[t, d] equals reverse at the partner slot (neighbor[t, d], edge_of[t, d]).
All inputs are finite; a program needn't handle non-finite values.
Results may differ from a plain program's by a relative error of at most 0.017.
Values may be sent and summed in bfloat16 or wider, within the bound.
No kernel may reach another device: no remote copies, remote signals or barrier semaphores. Data moves between devices by JAX's collectives and lax.ppermute only.
A program may use at most 64 MiB of HBM per device.

v0:
```python
import jax
import jax.numpy as jnp
from jax import lax
from jax.sharding import PartitionSpec as P


def from_behind(shard, axis, by):
    count = lax.axis_size(axis)
    pairs = [(i, i + by) for i in range(count) if 0 <= i + by < count]
    return lax.ppermute(shard, axis, pairs)


def make_patches(padded, side):
    parts = []
    for k in range(9):
        dy = k // 3
        dx = k % 3
        parts.append(padded[dy : dy + side, dx : dx + side, :])
    return jnp.concatenate(parts, axis=-1)


def silu_slope(value):
    sigma = jax.nn.sigmoid(value)
    return sigma * (1.0 + value * (1.0 - sigma))


def pad_tile(state, strips):
    corner = jnp.zeros((1, 1, state.shape[2]), state.dtype)
    top = jnp.concatenate([corner, strips[0][None], corner], axis=1)
    bottom = jnp.concatenate([corner, strips[2][None], corner], axis=1)
    middle = jnp.concatenate([strips[3][:, None], state, strips[1][:, None]], axis=1)
    return jnp.concatenate([top, middle, bottom], axis=0)


def local(inputs, neighbor, edge_of, reverse, weights, cotangent):
    samples = inputs.shape[0]
    side = inputs.shape[2]
    chans = inputs.shape[4]
    segment_count = lax.axis_size("segment")
    segment = lax.axis_index("segment")
    tile = lax.axis_index("tile")
    source = lax.dynamic_index_in_dim(neighbor, tile, 0, False) * 4 + lax.dynamic_index_in_dim(
        edge_of, tile, 0, False
    )
    flips = lax.dynamic_index_in_dim(reverse, tile, 0, False)
    kernel = weights[0]
    firsts = inputs[:, 0]
    cotans = cotangent[0, :, 0]

    def seam_strips(state):
        edges = jnp.stack(
            [state[0, :, :], state[:, side - 1, :], state[side - 1, :, :], state[:, 0, :]], axis=0
        )[None]
        gathered = lax.all_gather(edges, "tile", axis=0, tiled=True)
        count = gathered.shape[0] * 4
        onehot = (source[:, None] == jnp.arange(count, dtype=jnp.int32)[None, :]).astype(
            jnp.bfloat16
        )
        picked = jnp.dot(
            onehot, gathered.reshape(count, side * chans), preferred_element_type=jnp.float32
        )
        strips = picked.astype(jnp.bfloat16).reshape(4, side, chans)
        return jnp.where(flips[:, None, None] == 1, strips[:, ::-1, :], strips)

    def tick(step, carry):
        current, outputs, kernel_sum = carry
        index = step - segment
        valid = (index >= 0) & (index < samples)
        clipped = jnp.clip(index, 0, samples - 1)
        first = lax.dynamic_index_in_dim(firsts, clipped, 0, False)
        state = jnp.where(segment == 0, first, current)
        strips = seam_strips(state)
        padded = pad_tile(state, strips)
        patches = make_patches(padded, side).reshape(side * side, 9 * chans)
        pre_act = jnp.dot(patches, kernel, preferred_element_type=jnp.float32)
        new_flat = (
            state.reshape(side * side, chans).astype(jnp.float32) + jax.nn.silu(pre_act)
        ).astype(jnp.bfloat16)
        new_state = new_flat.reshape(side, side, chans)
        cotan = lax.dynamic_index_in_dim(cotans, clipped, 0, False).reshape(side * side, chans)
        delta = (cotan.astype(jnp.float32) * silu_slope(pre_act)).astype(jnp.bfloat16)
        term = lax.dot_general(
            patches, delta, (((0,), (0,)), ((), ())), preferred_element_type=jnp.float32
        )
        kernel_sum = kernel_sum + jnp.where(valid, term, jnp.zeros_like(term))
        previous = lax.dynamic_index_in_dim(outputs, clipped, 0, False)
        outputs = lax.dynamic_update_index_in_dim(
            outputs, jnp.where(valid, new_state, previous), clipped, 0
        )
        current = from_behind(new_state, "segment", 1)
        return (current, outputs, kernel_sum)

    start = (
        jnp.zeros((side, side, chans), jnp.bfloat16),
        jnp.zeros((samples, side, side, chans), jnp.bfloat16),
        jnp.zeros((9 * chans, chans), jnp.float32),
    )
    current, outputs, kernel_sum = lax.fori_loop(0, samples + segment_count - 1, tick, start)
    total = lax.psum(kernel_sum, ("dp", "tile"))
    return (outputs[None, :, None], total[None])


def solution(mesh):
    placed = (
        P("dp", "tile", None, None, None),
        P(),
        P(),
        P(),
        P("segment", None, None),
        P("segment", "dp", "tile", None, None, None),
    )
    return jax.shard_map(
        local,
        mesh=mesh,
        in_specs=placed,
        out_specs=(P("segment", "dp", "tile", None, None, None), P("segment", None, None)),
        check_vma=False,
    )
```

profile of v0, /device:TPU:2, one launch (start us, length us, event | category | flops | bytes accessed | tf_op | source)
XLA Modules:
  0.0 1655.6 jit_solution(16945184397781068950)
XLA Ops:
  9.1 1480.7 %while.19 = (s32[]{:T(128)}, bf16[32,32,128]{2,1,0:T(8,128)(2,1)S(1)}, bf16[2,32,32,128]{3,2,1,0:T(8,128)(2,1)S(1)}, f32[1152,128]{1,0:T(8,128)S(1)}, pred[]{:T(...) while((s32[]{:T(128)}, ...), condition=%wide.region_1.2_spmd.clone, body=%wide.region_0.1_spmd.clone.sunk | while | flops 615684608 | bytes 22792052 | solution.py:98
  11.8 158.9 %all-gather.6.cloned.1.call-done = bf16[128,32,128]{2,1,0:T(8,128)(2,1)} async-done(((bf16[4,32,128]{2,1,0:T(8,128)(2,1)}), bf16[128,32,128]{2,1,0:T(8,128)(2,1)}) %all-gather.6.cloned.1.call-update) | async-done | bytes 1048592 | tf_op jit(solution)/shard_map/while/body/eval_jaxpr/all_gather | solution.py:54
  174.6 1.9 collective-permute-start
  177.7 4.6 collective-permute-done
  185.0 149.3 %all-gather.6.cloned.1.call-done = bf16[128,32,128]{2,1,0:T(8,128)(2,1)} async-done(((bf16[4,32,128]{2,1,0:T(8,128)(2,1)}), bf16[128,32,128]{2,1,0:T(8,128)(2,1)}) %all-gather.6.cloned.1.call-update) | async-done | bytes 1048592 | tf_op jit(solution)/shard_map/while/body/eval_jaxpr/all_gather | solution.py:54
  338.1 1.9 collective-permute-start
  341.2 4.6 collective-permute-done
  348.5 149.3 %all-gather.6.cloned.1.call-done = bf16[128,32,128]{2,1,0:T(8,128)(2,1)} async-done(((bf16[4,32,128]{2,1,0:T(8,128)(2,1)}), bf16[128,32,128]{2,1,0:T(8,128)(2,1)}) %all-gather.6.cloned.1.call-update) | async-done | bytes 1048592 | tf_op jit(solution)/shard_map/while/body/eval_jaxpr/all_gather | solution.py:54
  501.7 1.9 collective-permute-start
  504.8 4.6 collective-permute-done
  512.1 149.0 %all-gather.6.cloned.1.call-done = bf16[128,32,128]{2,1,0:T(8,128)(2,1)} async-done(((bf16[4,32,128]{2,1,0:T(8,128)(2,1)}), bf16[128,32,128]{2,1,0:T(8,128)(2,1)}) %all-gather.6.cloned.1.call-update) | async-done | bytes 1048592 | tf_op jit(solution)/shard_map/while/body/eval_jaxpr/all_gather | solution.py:54
  668.0 4.6 collective-permute-done
  675.3 149.0 %all-gather.6.cloned.1.call-done = bf16[128,32,128]{2,1,0:T(8,128)(2,1)} async-done(((bf16[4,32,128]{2,1,0:T(8,128)(2,1)}), bf16[128,32,128]{2,1,0:T(8,128)(2,1)}) %all-gather.6.cloned.1.call-update) | async-done | bytes 1048592 | tf_op jit(solution)/shard_map/while/body/eval_jaxpr/all_gather | solution.py:54
  831.3 4.6 collective-permute-done
  838.6 149.0 %all-gather.6.cloned.1.call-done = bf16[128,32,128]{2,1,0:T(8,128)(2,1)} async-done(((bf16[4,32,128]{2,1,0:T(8,128)(2,1)}), bf16[128,32,128]{2,1,0:T(8,128)(2,1)}) %all-gather.6.cloned.1.call-update) | async-done | bytes 1048592 | tf_op jit(solution)/shard_map/while/body/eval_jaxpr/all_gather | solution.py:54
  991.4 1.9 collective-permute-start
  994.5 4.6 collective-permute-done
  1001.8 149.3 %all-gather.6.cloned.1.call-done = bf16[128,32,128]{2,1,0:T(8,128)(2,1)} async-done(((bf16[4,32,128]{2,1,0:T(8,128)(2,1)}), bf16[128,32,128]{2,1,0:T(8,128)(2,1)}) %all-gather.6.cloned.1.call-update) | async-done | bytes 1048592 | tf_op jit(solution)/shard_map/while/body/eval_jaxpr/all_gather | solution.py:54
  1158.1 4.6 collective-permute-done
  1165.4 149.3 %all-gather.6.cloned.1.call-done = bf16[128,32,128]{2,1,0:T(8,128)(2,1)} async-done(((bf16[4,32,128]{2,1,0:T(8,128)(2,1)}), bf16[128,32,128]{2,1,0:T(8,128)(2,1)}) %all-gather.6.cloned.1.call-update) | async-done | bytes 1048592 | tf_op jit(solution)/shard_map/while/body/eval_jaxpr/all_gather | solution.py:54
  1321.6 4.6 collective-permute-done
  1328.9 149.3 %all-gather.6.cloned.1.call-done = bf16[128,32,128]{2,1,0:T(8,128)(2,1)} async-done(((bf16[4,32,128]{2,1,0:T(8,128)(2,1)}), bf16[128,32,128]{2,1,0:T(8,128)(2,1)}) %all-gather.6.cloned.1.call-update) | async-done | bytes 1048592 | tf_op jit(solution)/shard_map/while/body/eval_jaxpr/all_gather | solution.py:54
  1485.2 4.6 collective-permute-done
  1490.6 155.9 %all-reduce.2.cloned.1.call-done = f32[1,1152,128]{2,1,0:T(8,128)} async-done(((f32[1,1152,128]{2,1,0:T(8,128)}), f32[1,1152,128]{2,1,0:T(8,128)}) %all-reduce.2.cloned.1.call-update) | async-done | bytes 589840 | tf_op jit(solution)/shard_map/psum | solution.py:99
  (304 shorter events, 81.5 us)
Async XLA Ops:
  9.1 161.6 %all-gather.6.cloned.1.call-start = ((), (), s32[]{:S(2)}) async-start(), calls=%async_computation.1 | async-start | bytes 1081344 | tf_op jit(solution)/shard_map/while/body/eval_jaxpr/all_gather | solution.py:54
  172.8 1.0 copy-start.2
  174.6 7.7 collective-permute-start
  182.3 152.0 %all-gather.6.cloned.1.call-start = ((), (), s32[]{:S(2)}) async-start(), calls=%async_computation.1 | async-start | bytes 1081344 | tf_op jit(solution)/shard_map/while/body/eval_jaxpr/all_gather | solution.py:54
  336.3 1.0 copy-start.2
  338.1 7.7 collective-permute-start
  345.8 152.0 %all-gather.6.cloned.1.call-start = ((), (), s32[]{:S(2)}) async-start(), calls=%async_computation.1 | async-start | bytes 1081344 | tf_op jit(solution)/shard_map/while/body/eval_jaxpr/all_gather | solution.py:54
  501.7 7.7 collective-permute-start
  509.4 151.7 %all-gather.6.cloned.1.call-start = ((), (), s32[]{:S(2)}) async-start(), calls=%async_computation.1 | async-start | bytes 1081344 | tf_op jit(solution)/shard_map/while/body/eval_jaxpr/all_gather | solution.py:54
  663.1 1.0 copy-start.2
  664.9 7.7 collective-permute-start
  672.6 151.7 %all-gather.6.cloned.1.call-start = ((), (), s32[]{:S(2)}) async-start(), calls=%async_computation.1 | async-start | bytes 1081344 | tf_op jit(solution)/shard_map/while/body/eval_jaxpr/all_gather | solution.py:54
  826.4 1.0 copy-start.2
  828.2 7.7 collective-permute-start
  835.9 151.7 %all-gather.6.cloned.1.call-start = ((), (), s32[]{:S(2)}) async-start(), calls=%async_computation.1 | async-start | bytes 1081344 | tf_op jit(solution)/shard_map/while/body/eval_jaxpr/all_gather | solution.py:54
  991.4 7.7 collective-permute-start
  999.1 152.0 %all-gather.6.cloned.1.call-start = ((), (), s32[]{:S(2)}) async-start(), calls=%async_computation.1 | async-start | bytes 1081344 | tf_op jit(solution)/shard_map/while/body/eval_jaxpr/all_gather | solution.py:54
  1155.0 7.7 collective-permute-start
  1162.7 152.0 %all-gather.6.cloned.1.call-start = ((), (), s32[]{:S(2)}) async-start(), calls=%async_computation.1 | async-start | bytes 1081344 | tf_op jit(solution)/shard_map/while/body/eval_jaxpr/all_gather | solution.py:54
  1318.5 7.7 collective-permute-start
  1326.2 152.0 %all-gather.6.cloned.1.call-start = ((), (), s32[]{:S(2)}) async-start(), calls=%async_computation.1 | async-start | bytes 1081344 | tf_op jit(solution)/shard_map/while/body/eval_jaxpr/all_gather | solution.py:54
  1482.1 7.7 collective-permute-start
  1489.8 158.7 %copy-start = (bf16[2,32,32,128]{3,2,1,0:T(8,128)(2,1)}, bf16[2,32,32,128]{3,2,1,0:T(8,128)(2,1)S(1)}, u32[]{:S(2)}) copy-start(bf16[2,32,32,128]{3,2,1,0:T(8,128)(2,1)S(1)} %get-tuple-element.217) | copy-start | bytes 1572868
  1489.8 156.8 %all-reduce.2.cloned.1.call-start = ((), (), s32[]{:S(2)}) async-start(), calls=%async_computation | async-start | bytes 1179648 | tf_op jit(solution)/shard_map/psum | solution.py:99
  (6 other events, 5.6 us)
Sparse Core Ops, SparseCore 0:
  12.6 158.1 all-gather.5
  185.7 148.5 all-gather.5
  349.3 148.5 all-gather.5
  512.5 148.5 all-gather.5
  675.8 148.5 all-gather.5
  839.0 148.5 all-gather.5
  1002.6 148.5 all-gather.5
  1166.1 148.5 all-gather.5
  1329.7 148.5 all-gather.5
Sparse Core Ops, SparseCore 1:
  1494.1 152.4 all-reduce.1
where the time goes:
time: 1660 us
  waiting for transfers between devices  1550 us (93%)
  matrix products  31.6 us (2%)
  other arithmetic  21.5 us (1%)
  local copies, waits for them, and re-layouts  18.5 us (1%)
  starting transfers between devices  17.3 us (1%)
    all_gather x9, waiting for transfers between devices, seam_strips(): gathered = lax.all_gather(edges, 'tile', axis=0, tiled=True)  1350 us
    psum x1, waiting for transfers between devices, local(): total = lax.psum(kernel_sum, ('dp', 'tile'))  156 us
    ppermute x9, waiting for transfers between devices, from_behind(): return lax.ppermute(shard, axis, pairs)  41.2 us
  transfers between devices with their start and end apart: 19, of which 19 were waited for; matrix products, arithmetic and copies ran while one was open for 1% of the time, Pallas kernels for 0%

commit v1 on v0

--- a/solution.py
+++ b/solution.py
@@ -32,6 +32,17 @@
     return jnp.concatenate([top, middle, bottom], axis=0)
 
 
+def sum_terms(term):
+    axes = ("dp", "tile")
+    count = lax.axis_size(axes)
+    rows = term.shape[0] // count
+    pieces = term.astype(jnp.bfloat16).reshape(count, rows, term.shape[1])
+    pieces = lax.all_to_all(pieces, axes, 0, 0)
+    piece = jnp.sum(pieces.astype(jnp.float32), axis=0).astype(jnp.bfloat16)
+    pieces = lax.all_to_all(jnp.broadcast_to(piece[None], pieces.shape), axes, 0, 0)
+    return pieces.reshape(term.shape).astype(jnp.float32)
+
+
 def local(inputs, neighbor, edge_of, reverse, weights, cotangent):
     samples = inputs.shape[0]
     side = inputs.shape[2]
@@ -51,7 +62,9 @@
         edges = jnp.stack(
             [state[0, :, :], state[:, side - 1, :], state[side - 1, :, :], state[:, 0, :]], axis=0
         )[None]
-        gathered = lax.all_gather(edges, "tile", axis=0, tiled=True)
+        tiles = lax.axis_size("tile")
+        copies = jnp.broadcast_to(edges, (tiles,) + edges.shape[1:])
+        gathered = lax.all_to_all(copies, "tile", 0, 0)
         count = gathered.shape[0] * 4
         onehot = (source[:, None] == jnp.arange(count, dtype=jnp.int32)[None, :]).astype(
             jnp.bfloat16
@@ -96,7 +109,7 @@
         jnp.zeros((9 * chans, chans), jnp.float32),
     )
     current, outputs, kernel_sum = lax.fori_loop(0, samples + segment_count - 1, tick, start)
-    total = lax.psum(kernel_sum, ("dp", "tile"))
+    total = sum_terms(kernel_sum)
     return (outputs[None, :, None], total[None])
 
 

time: 1660 us -> 453 us (0.27)
  waiting for transfers between devices: 1550 us -> 272 us
  starting transfers between devices: 17.3 us -> 78.8 us
  blocking collectives: 0 us -> 41.5 us
    all_gather x9 -> x0, waiting for transfers between devices: 1350 us -> none  [seam_strips(): gathered = lax.all_gather(edges, 'tile', axis=0, tiled=True)]
    all_to_all x0 -> x9, waiting for transfers between devices: none -> 231 us  [seam_strips(): gathered = lax.all_to_all(copies, 'tile', 0, 0)]
    psum x1 -> x0, waiting for transfers between devices: 156 us -> none  [local(): total = lax.psum(kernel_sum, ('dp', 'tile'))]
    all_to_all x0 -> x9, starting transfers between devices: none -> 61.5 us  [seam_strips(): gathered = lax.all_to_all(copies, 'tile', 0, 0)]
    all_to_all x0 -> x2, blocking collectives: none -> 41.5 us  [the longest x1 22.5 us: sum_terms(): pieces = lax.all_to_all(pieces, axes, 0, 0)]
  transfers between devices with their start and end apart: 19 -> 18, of which waited for: 19 -> 18; matrix products, arithmetic and copies ran while one was open for 1% -> 2% of each run, Pallas kernels for 0% -> 0%
where the time goes in v1:
time: 453 us; the launch traced here: 452 us
  waiting for transfers between devices  272 us (60%)
  starting transfers between devices  78.8 us (17%)
  blocking collectives  41.5 us (9%)
  matrix products  20.8 us (5%)
  local copies, waits for them, and re-layouts  19.2 us (4%)
  other arithmetic  16.9 us (4%)
    all_to_all x9, waiting for transfers between devices, seam_strips(): gathered = lax.all_to_all(copies, 'tile', 0, 0)  231 us
    all_to_all x9, starting transfers between devices, seam_strips(): gathered = lax.all_to_all(copies, 'tile', 0, 0)  61.5 us
    ppermute x9, waiting for transfers between devices, from_behind(): return lax.ppermute(shard, axis, pairs)  41.1 us
    all_to_all x1, blocking collectives, sum_terms(): pieces = lax.all_to_all(pieces, axes, 0, 0)  22.5 us
    all_to_all x1, blocking collectives, sum_terms(): lax.all_to_all(jnp.broadcast_to(piece[None], pieces.shape), axes, 0, 0)  18.9 us
    ppermute x9, starting transfers between devices, from_behind(): return lax.ppermute(shard, axis, pairs)  17.3 us
    broadcast_in_dim x9, local copies, waits for them, and re-layouts, seam_strips(): copies = jnp.broadcast_to(edges, (tiles,) + edges.shape[1:])  10.9 us
    dot_general x9, matrix products, tick(): lax.dot_general(patches, delta, (((0,), (0,)), ((), ())), preferred_eleme...  9.77 us
  transfers between devices with their start and end apart: 18, of which 18 were waited for; matrix products, arithmetic and copies ran while one was open for 2% of the time, Pallas kernels for 0%

profile of v1, /device:TPU:2, one launch (start us, length us, event | category | flops | bytes accessed | tf_op | source)
XLA Modules:
  0.0 451.5 jit_solution(10074294668727381467)
XLA Ops:
  1.7 407.2 %while.19 = (s32[]{:T(128)}, bf16[32,32,128]{2,1,0:T(8,128)(2,1)S(1)}, bf16[2,32,32,128]{3,2,1,0:T(8,128)(2,1)S(1)}, f32[1152,128]{1,0:T(8,128)S(1)}, pred[]{:T(...) while((s32[]{:T(128)}, ...), condition=%wide.region_1.2_spmd.clone, body=%wide.region_0.1_spmd.clone.sunk | while | flops 615684608 | bytes 25872264 | solution.py:111
  4.1 13.7 %all-to-all-start = ((bf16[32,4,32,128]{3,2,1,0:T(8,128)(2,1)}), bf16[32,4,32,128]{3,2,1,0:T(8,128)(2,1)S(1)}, u32[]{:S(2)}, u32[]{:S(2)}) async-start(bf16[32,4,32,128]{3,2,1,0:T(8,128)(2,1)} %broadcast_in_dim.76), calls=%async_computation | async-start | bytes 2097152 | tf_op jit(solution)/shard_map/while/body/eval_jaxpr/all_to_all | solution.py:67
  17.9 27.5 %all-to-all-done = bf16[32,4,32,128]{3,2,1,0:T(8,128)(2,1)S(1)} async-done(((bf16[32,4,32,128]{3,2,1,0:T(8,128)(2,1)}), bf16[32,4,32,128]{3,2,1,0:T(8,128)(2,1)S(1)}, u32[]{:S(2)}, u32[]{:S(2)}) %all-to-all-start) | async-done | bytes 1048608 | tf_op jit(solution)/shard_map/while/body/eval_jaxpr/all_to_all | solution.py:67
  51.2 4.6 %collective-permute-done = bf16[32,32,128]{2,1,0:T(8,128)(2,1)S(1)} collective-permute-done((bf16[32,32,128]{2,1,0:T(8,128)(2,1)S(1)}, bf16[32,32,128]{2,1,0:T(8,128)(2,1)S(1)}, u32[]{:S(2)}, u32[]{:S(2)}) %collective-permute-start) | collective-permute-done | bytes 262176 | tf_op jit(solution)/shard_map/while/body/eval_jaxpr/ppermute | solution.py:10
  58.1 5.8 %all-to-all-start = ((bf16[32,4,32,128]{3,2,1,0:T(8,128)(2,1)}), bf16[32,4,32,128]{3,2,1,0:T(8,128)(2,1)S(1)}, u32[]{:S(2)}, u32[]{:S(2)}) async-start(bf16[32,4,32,128]{3,2,1,0:T(8,128)(2,1)} %broadcast_in_dim.76), calls=%async_computation | async-start | bytes 2097152 | tf_op jit(solution)/shard_map/while/body/eval_jaxpr/all_to_all | solution.py:67
  63.9 26.6 %all-to-all-done = bf16[32,4,32,128]{3,2,1,0:T(8,128)(2,1)S(1)} async-done(((bf16[32,4,32,128]{3,2,1,0:T(8,128)(2,1)}), bf16[32,4,32,128]{3,2,1,0:T(8,128)(2,1)S(1)}, u32[]{:S(2)}, u32[]{:S(2)}) %all-to-all-start) | async-done | bytes 1048608 | tf_op jit(solution)/shard_map/while/body/eval_jaxpr/all_to_all | solution.py:67
  103.2 6.0 %all-to-all-start = ((bf16[32,4,32,128]{3,2,1,0:T(8,128)(2,1)}), bf16[32,4,32,128]{3,2,1,0:T(8,128)(2,1)S(1)}, u32[]{:S(2)}, u32[]{:S(2)}) async-start(bf16[32,4,32,128]{3,2,1,0:T(8,128)(2,1)} %broadcast_in_dim.76), calls=%async_computation | async-start | bytes 2097152 | tf_op jit(solution)/shard_map/while/body/eval_jaxpr/all_to_all | solution.py:67
  109.3 26.7 %all-to-all-done = bf16[32,4,32,128]{3,2,1,0:T(8,128)(2,1)S(1)} async-done(((bf16[32,4,32,128]{3,2,1,0:T(8,128)(2,1)}), bf16[32,4,32,128]{3,2,1,0:T(8,128)(2,1)S(1)}, u32[]{:S(2)}, u32[]{:S(2)}) %all-to-all-start) | async-done | bytes 1048608 | tf_op jit(solution)/shard_map/while/body/eval_jaxpr/all_to_all | solution.py:67
  148.6 6.1 %all-to-all-start = ((bf16[32,4,32,128]{3,2,1,0:T(8,128)(2,1)}), bf16[32,4,32,128]{3,2,1,0:T(8,128)(2,1)S(1)}, u32[]{:S(2)}, u32[]{:S(2)}) async-start(bf16[32,4,32,128]{3,2,1,0:T(8,128)(2,1)} %broadcast_in_dim.76), calls=%async_computation | async-start | bytes 2097152 | tf_op jit(solution)/shard_map/while/body/eval_jaxpr/all_to_all | solution.py:67
  154.8 25.8 %all-to-all-done = bf16[32,4,32,128]{3,2,1,0:T(8,128)(2,1)S(1)} async-done(((bf16[32,4,32,128]{3,2,1,0:T(8,128)(2,1)}), bf16[32,4,32,128]{3,2,1,0:T(8,128)(2,1)S(1)}, u32[]{:S(2)}, u32[]{:S(2)}) %all-to-all-start) | async-done | bytes 1048608 | tf_op jit(solution)/shard_map/while/body/eval_jaxpr/all_to_all | solution.py:67
  193.3 5.4 %all-to-all-start = ((bf16[32,4,32,128]{3,2,1,0:T(8,128)(2,1)}), bf16[32,4,32,128]{3,2,1,0:T(8,128)(2,1)S(1)}, u32[]{:S(2)}, u32[]{:S(2)}) async-start(bf16[32,4,32,128]{3,2,1,0:T(8,128)(2,1)} %broadcast_in_dim.76), calls=%async_computation | async-start | bytes 2097152 | tf_op jit(solution)/shard_map/while/body/eval_jaxpr/all_to_all | solution.py:67
  198.8 25.1 %all-to-all-done = bf16[32,4,32,128]{3,2,1,0:T(8,128)(2,1)S(1)} async-done(((bf16[32,4,32,128]{3,2,1,0:T(8,128)(2,1)}), bf16[32,4,32,128]{3,2,1,0:T(8,128)(2,1)S(1)}, u32[]{:S(2)}, u32[]{:S(2)}) %all-to-all-start) | async-done | bytes 1048608 | tf_op jit(solution)/shard_map/while/body/eval_jaxpr/all_to_all | solution.py:67
  236.5 5.9 %all-to-all-start = ((bf16[32,4,32,128]{3,2,1,0:T(8,128)(2,1)}), bf16[32,4,32,128]{3,2,1,0:T(8,128)(2,1)S(1)}, u32[]{:S(2)}, u32[]{:S(2)}) async-start(bf16[32,4,32,128]{3,2,1,0:T(8,128)(2,1)} %broadcast_in_dim.76), calls=%async_computation | async-start | bytes 2097152 | tf_op jit(solution)/shard_map/while/body/eval_jaxpr/all_to_all | solution.py:67
  242.5 24.9 %all-to-all-done = bf16[32,4,32,128]{3,2,1,0:T(8,128)(2,1)S(1)} async-done(((bf16[32,4,32,128]{3,2,1,0:T(8,128)(2,1)}), bf16[32,4,32,128]{3,2,1,0:T(8,128)(2,1)S(1)}, u32[]{:S(2)}, u32[]{:S(2)}) %all-to-all-start) | async-done | bytes 1048608 | tf_op jit(solution)/shard_map/while/body/eval_jaxpr/all_to_all | solution.py:67
  273.2 4.6 %collective-permute-done = bf16[32,32,128]{2,1,0:T(8,128)(2,1)S(1)} collective-permute-done((bf16[32,32,128]{2,1,0:T(8,128)(2,1)S(1)}, bf16[32,32,128]{2,1,0:T(8,128)(2,1)S(1)}, u32[]{:S(2)}, u32[]{:S(2)}) %collective-permute-start) | collective-permute-done | bytes 262176 | tf_op jit(solution)/shard_map/while/body/eval_jaxpr/ppermute | solution.py:10
  280.1 6.2 %all-to-all-start = ((bf16[32,4,32,128]{3,2,1,0:T(8,128)(2,1)}), bf16[32,4,32,128]{3,2,1,0:T(8,128)(2,1)S(1)}, u32[]{:S(2)}, u32[]{:S(2)}) async-start(bf16[32,4,32,128]{3,2,1,0:T(8,128)(2,1)} %broadcast_in_dim.76), calls=%async_computation | async-start | bytes 2097152 | tf_op jit(solution)/shard_map/while/body/eval_jaxpr/all_to_all | solution.py:67
  286.4 24.8 %all-to-all-done = bf16[32,4,32,128]{3,2,1,0:T(8,128)(2,1)S(1)} async-done(((bf16[32,4,32,128]{3,2,1,0:T(8,128)(2,1)}), bf16[32,4,32,128]{3,2,1,0:T(8,128)(2,1)S(1)}, u32[]{:S(2)}, u32[]{:S(2)}) %all-to-all-start) | async-done | bytes 1048608 | tf_op jit(solution)/shard_map/while/body/eval_jaxpr/all_to_all | solution.py:67
  323.9 6.1 %all-to-all-start = ((bf16[32,4,32,128]{3,2,1,0:T(8,128)(2,1)}), bf16[32,4,32,128]{3,2,1,0:T(8,128)(2,1)S(1)}, u32[]{:S(2)}, u32[]{:S(2)}) async-start(bf16[32,4,32,128]{3,2,1,0:T(8,128)(2,1)} %broadcast_in_dim.76), calls=%async_computation | async-start | bytes 2097152 | tf_op jit(solution)/shard_map/while/body/eval_jaxpr/all_to_all | solution.py:67
  330.1 24.8 %all-to-all-done = bf16[32,4,32,128]{3,2,1,0:T(8,128)(2,1)S(1)} async-done(((bf16[32,4,32,128]{3,2,1,0:T(8,128)(2,1)}), bf16[32,4,32,128]{3,2,1,0:T(8,128)(2,1)S(1)}, u32[]{:S(2)}, u32[]{:S(2)}) %all-to-all-start) | async-done | bytes 1048608 | tf_op jit(solution)/shard_map/while/body/eval_jaxpr/all_to_all | solution.py:67
  367.5 6.2 %all-to-all-start = ((bf16[32,4,32,128]{3,2,1,0:T(8,128)(2,1)}), bf16[32,4,32,128]{3,2,1,0:T(8,128)(2,1)S(1)}, u32[]{:S(2)}, u32[]{:S(2)}) async-start(bf16[32,4,32,128]{3,2,1,0:T(8,128)(2,1)} %broadcast_in_dim.76), calls=%async_computation | async-start | bytes 2097152 | tf_op jit(solution)/shard_map/while/body/eval_jaxpr/all_to_all | solution.py:67
  373.7 24.8 %all-to-all-done = bf16[32,4,32,128]{3,2,1,0:T(8,128)(2,1)S(1)} async-done(((bf16[32,4,32,128]{3,2,1,0:T(8,128)(2,1)}), bf16[32,4,32,128]{3,2,1,0:T(8,128)(2,1)S(1)}, u32[]{:S(2)}, u32[]{:S(2)}) %all-to-all-start) | async-done | bytes 1048608 | tf_op jit(solution)/shard_map/while/body/eval_jaxpr/all_to_all | solution.py:67
  404.3 4.6 %collective-permute-done = bf16[32,32,128]{2,1,0:T(8,128)(2,1)S(1)} collective-permute-done((bf16[32,32,128]{2,1,0:T(8,128)(2,1)S(1)}, bf16[32,32,128]{2,1,0:T(8,128)(2,1)S(1)}, u32[]{:S(2)}, u32[]{:S(2)}) %collective-permute-start) | collective-permute-done | bytes 262176 | tf_op jit(solution)/shard_map/while/body/eval_jaxpr/ppermute | solution.py:10
  409.0 22.5 %all_to_all.22 = bf16[64,18,128]{2,1,0:T(8,128)(2,1)S(1)} all-to-all(bf16[64,18,128]{2,1,0:T(8,128)(2,1)S(1)} %reshape.88), channel_id=1, replica_groups=mesh['dp'=2,'segment'=8,'tile'=32] {'dp','tile'}, dimensions={0} | all-to-all | bytes 589824 | tf_op jit(solution)/shard_map/all_to_all | solution.py:40
  431.7 18.9 %all_to_all.23 = bf16[64,18,128]{2,1,0:T(8,128)(2,1)S(1)} all-to-all(bf16[64,18,128]{2,1,0:T(8,128)(2,1)S(1)} %broadcast_in_dim.69), channel_id=1, replica_groups=mesh['dp'=2,'segment'=8,'tile'=32] {'dp','tile'}, dimensions={0} | all-to-all | bytes 589824 | tf_op jit(solution)/shard_map/all_to_all | solution.py:42
  (323 shorter events, 101.6 us)
Async XLA Ops:
  1.7 16.1 %copy-start.1 = (bf16[2,32,32,128]{3,2,1,0:T(8,128)(2,1)S(1)}, bf16[2,32,32,128]{3,2,1,0:T(8,128)(2,1)}, u32[]{:S(2)}) copy-start(bf16[2,32,32,128]{3,2,1,0:T(8,128)(2,1)} %get-tuple-element.428) | copy-start | bytes 1572868 | tf_op jit(solution)/shard_map/while
  4.1 41.3 %all-to-all-start = ((bf16[32,4,32,128]{3,2,1,0:T(8,128)(2,1)}), bf16[32,4,32,128]{3,2,1,0:T(8,128)(2,1)S(1)}, u32[]{:S(2)}, u32[]{:S(2)}) async-start(bf16[32,4,32,128]{3,2,1,0:T(8,128)(2,1)} %broadcast_in_dim.76), calls=%async_computation | async-start | bytes 2097152 | tf_op jit(solution)/shard_map/while/body/eval_jaxpr/all_to_all | solution.py:67
  48.0 7.7 %collective-permute-start = (bf16[32,32,128]{2,1,0:T(8,128)(2,1)S(1)}, bf16[32,32,128]{2,1,0:T(8,128)(2,1)S(1)}, u32[]{:S(2)}, u32[]{:S(2)}) collective-permute-start(bf16[32,32,128]{2,1,0:T(8,128)(2,1)S(1)} %bitcast.69), channel_id=1, source_target_pairs={{0,32},{32,64},{64,96},{96,128},{128,160},{160,192},{192,224},{1,3... | collective-permute-start | bytes 786440 | tf_op jit(solution)/shard_map/while/body/eval_jaxpr/ppermute | solution.py:10
  58.1 32.5 %all-to-all-start = ((bf16[32,4,32,128]{3,2,1,0:T(8,128)(2,1)}), bf16[32,4,32,128]{3,2,1,0:T(8,128)(2,1)S(1)}, u32[]{:S(2)}, u32[]{:S(2)}) async-start(bf16[32,4,32,128]{3,2,1,0:T(8,128)(2,1)} %broadcast_in_dim.76), calls=%async_computation | async-start | bytes 2097152 | tf_op jit(solution)/shard_map/while/body/eval_jaxpr/all_to_all | solution.py:67
  93.2 7.7 %collective-permute-start = (bf16[32,32,128]{2,1,0:T(8,128)(2,1)S(1)}, bf16[32,32,128]{2,1,0:T(8,128)(2,1)S(1)}, u32[]{:S(2)}, u32[]{:S(2)}) collective-permute-start(bf16[32,32,128]{2,1,0:T(8,128)(2,1)S(1)} %bitcast.69), channel_id=1, source_target_pairs={{0,32},{32,64},{64,96},{96,128},{128,160},{160,192},{192,224},{1,3... | collective-permute-start | bytes 786440 | tf_op jit(solution)/shard_map/while/body/eval_jaxpr/ppermute | solution.py:10
  103.2 32.8 %all-to-all-start = ((bf16[32,4,32,128]{3,2,1,0:T(8,128)(2,1)}), bf16[32,4,32,128]{3,2,1,0:T(8,128)(2,1)S(1)}, u32[]{:S(2)}, u32[]{:S(2)}) async-start(bf16[32,4,32,128]{3,2,1,0:T(8,128)(2,1)} %broadcast_in_dim.76), calls=%async_computation | async-start | bytes 2097152 | tf_op jit(solution)/shard_map/while/body/eval_jaxpr/all_to_all | solution.py:67
  138.6 7.7 %collective-permute-start = (bf16[32,32,128]{2,1,0:T(8,128)(2,1)S(1)}, bf16[32,32,128]{2,1,0:T(8,128)(2,1)S(1)}, u32[]{:S(2)}, u32[]{:S(2)}) collective-permute-start(bf16[32,32,128]{2,1,0:T(8,128)(2,1)S(1)} %bitcast.69), channel_id=1, source_target_pairs={{0,32},{32,64},{64,96},{96,128},{128,160},{160,192},{192,224},{1,3... | collective-permute-start | bytes 786440 | tf_op jit(solution)/shard_map/while/body/eval_jaxpr/ppermute | solution.py:10
  146.3 8.4 %copy-start.1 = (bf16[2,32,32,128]{3,2,1,0:T(8,128)(2,1)S(1)}, bf16[2,32,32,128]{3,2,1,0:T(8,128)(2,1)}, u32[]{:S(2)}) copy-start(bf16[2,32,32,128]{3,2,1,0:T(8,128)(2,1)} %get-tuple-element.428) | copy-start | bytes 1572868 | tf_op jit(solution)/shard_map/while
  148.6 32.0 %all-to-all-start = ((bf16[32,4,32,128]{3,2,1,0:T(8,128)(2,1)}), bf16[32,4,32,128]{3,2,1,0:T(8,128)(2,1)S(1)}, u32[]{:S(2)}, u32[]{:S(2)}) async-start(bf16[32,4,32,128]{3,2,1,0:T(8,128)(2,1)} %broadcast_in_dim.76), calls=%async_computation | async-start | bytes 2097152 | tf_op jit(solution)/shard_map/while/body/eval_jaxpr/all_to_all | solution.py:67
  183.2 7.7 %collective-permute-start = (bf16[32,32,128]{2,1,0:T(8,128)(2,1)S(1)}, bf16[32,32,128]{2,1,0:T(8,128)(2,1)S(1)}, u32[]{:S(2)}, u32[]{:S(2)}) collective-permute-start(bf16[32,32,128]{2,1,0:T(8,128)(2,1)S(1)} %bitcast.69), channel_id=1, source_target_pairs={{0,32},{32,64},{64,96},{96,128},{128,160},{160,192},{192,224},{1,3... | collective-permute-start | bytes 786440 | tf_op jit(solution)/shard_map/while/body/eval_jaxpr/ppermute | solution.py:10
  193.3 30.6 %all-to-all-start = ((bf16[32,4,32,128]{3,2,1,0:T(8,128)(2,1)}), bf16[32,4,32,128]{3,2,1,0:T(8,128)(2,1)S(1)}, u32[]{:S(2)}, u32[]{:S(2)}) async-start(bf16[32,4,32,128]{3,2,1,0:T(8,128)(2,1)} %broadcast_in_dim.76), calls=%async_computation | async-start | bytes 2097152 | tf_op jit(solution)/shard_map/while/body/eval_jaxpr/all_to_all | solution.py:67
  226.5 7.7 %collective-permute-start = (bf16[32,32,128]{2,1,0:T(8,128)(2,1)S(1)}, bf16[32,32,128]{2,1,0:T(8,128)(2,1)S(1)}, u32[]{:S(2)}, u32[]{:S(2)}) collective-permute-start(bf16[32,32,128]{2,1,0:T(8,128)(2,1)S(1)} %bitcast.69), channel_id=1, source_target_pairs={{0,32},{32,64},{64,96},{96,128},{128,160},{160,192},{192,224},{1,3... | collective-permute-start | bytes 786440 | tf_op jit(solution)/shard_map/while/body/eval_jaxpr/ppermute | solution.py:10
  236.5 30.9 %all-to-all-start = ((bf16[32,4,32,128]{3,2,1,0:T(8,128)(2,1)}), bf16[32,4,32,128]{3,2,1,0:T(8,128)(2,1)S(1)}, u32[]{:S(2)}, u32[]{:S(2)}) async-start(bf16[32,4,32,128]{3,2,1,0:T(8,128)(2,1)} %broadcast_in_dim.76), calls=%async_computation | async-start | bytes 2097152 | tf_op jit(solution)/shard_map/while/body/eval_jaxpr/all_to_all | solution.py:67
  270.0 7.7 %collective-permute-start = (bf16[32,32,128]{2,1,0:T(8,128)(2,1)S(1)}, bf16[32,32,128]{2,1,0:T(8,128)(2,1)S(1)}, u32[]{:S(2)}, u32[]{:S(2)}) collective-permute-start(bf16[32,32,128]{2,1,0:T(8,128)(2,1)S(1)} %bitcast.69), channel_id=1, source_target_pairs={{0,32},{32,64},{64,96},{96,128},{128,160},{160,192},{192,224},{1,3... | collective-permute-start | bytes 786440 | tf_op jit(solution)/shard_map/while/body/eval_jaxpr/ppermute | solution.py:10
  277.7 8.6 %copy-start.1 = (bf16[2,32,32,128]{3,2,1,0:T(8,128)(2,1)S(1)}, bf16[2,32,32,128]{3,2,1,0:T(8,128)(2,1)}, u32[]{:S(2)}) copy-start(bf16[2,32,32,128]{3,2,1,0:T(8,128)(2,1)} %get-tuple-element.428) | copy-start | bytes 1572868 | tf_op jit(solution)/shard_map/while
  280.1 31.1 %all-to-all-start = ((bf16[32,4,32,128]{3,2,1,0:T(8,128)(2,1)}), bf16[32,4,32,128]{3,2,1,0:T(8,128)(2,1)S(1)}, u32[]{:S(2)}, u32[]{:S(2)}) async-start(bf16[32,4,32,128]{3,2,1,0:T(8,128)(2,1)} %broadcast_in_dim.76), calls=%async_computation | async-start | bytes 2097152 | tf_op jit(solution)/shard_map/while/body/eval_jaxpr/all_to_all | solution.py:67
  313.8 7.7 %collective-permute-start = (bf16[32,32,128]{2,1,0:T(8,128)(2,1)S(1)}, bf16[32,32,128]{2,1,0:T(8,128)(2,1)S(1)}, u32[]{:S(2)}, u32[]{:S(2)}) collective-permute-start(bf16[32,32,128]{2,1,0:T(8,128)(2,1)S(1)} %bitcast.69), channel_id=1, source_target_pairs={{0,32},{32,64},{64,96},{96,128},{128,160},{160,192},{192,224},{1,3... | collective-permute-start | bytes 786440 | tf_op jit(solution)/shard_map/while/body/eval_jaxpr/ppermute | solution.py:10
  321.5 8.5 %copy-start.1 = (bf16[2,32,32,128]{3,2,1,0:T(8,128)(2,1)S(1)}, bf16[2,32,32,128]{3,2,1,0:T(8,128)(2,1)}, u32[]{:S(2)}) copy-start(bf16[2,32,32,128]{3,2,1,0:T(8,128)(2,1)} %get-tuple-element.428) | copy-start | bytes 1572868 | tf_op jit(solution)/shard_map/while
  323.9 31.0 %all-to-all-start = ((bf16[32,4,32,128]{3,2,1,0:T(8,128)(2,1)}), bf16[32,4,32,128]{3,2,1,0:T(8,128)(2,1)S(1)}, u32[]{:S(2)}, u32[]{:S(2)}) async-start(bf16[32,4,32,128]{3,2,1,0:T(8,128)(2,1)} %broadcast_in_dim.76), calls=%async_computation | async-start | bytes 2097152 | tf_op jit(solution)/shard_map/while/body/eval_jaxpr/all_to_all | solution.py:67
  357.5 7.7 %collective-permute-start = (bf16[32,32,128]{2,1,0:T(8,128)(2,1)S(1)}, bf16[32,32,128]{2,1,0:T(8,128)(2,1)S(1)}, u32[]{:S(2)}, u32[]{:S(2)}) collective-permute-start(bf16[32,32,128]{2,1,0:T(8,128)(2,1)S(1)} %bitcast.69), channel_id=1, source_target_pairs={{0,32},{32,64},{64,96},{96,128},{128,160},{160,192},{192,224},{1,3... | collective-permute-start | bytes 786440 | tf_op jit(solution)/shard_map/while/body/eval_jaxpr/ppermute | solution.py:10
  365.1 8.5 %copy-start.1 = (bf16[2,32,32,128]{3,2,1,0:T(8,128)(2,1)S(1)}, bf16[2,32,32,128]{3,2,1,0:T(8,128)(2,1)}, u32[]{:S(2)}) copy-start(bf16[2,32,32,128]{3,2,1,0:T(8,128)(2,1)} %get-tuple-element.428) | copy-start | bytes 1572868 | tf_op jit(solution)/shard_map/while
  367.5 31.1 %all-to-all-start = ((bf16[32,4,32,128]{3,2,1,0:T(8,128)(2,1)}), bf16[32,4,32,128]{3,2,1,0:T(8,128)(2,1)S(1)}, u32[]{:S(2)}, u32[]{:S(2)}) async-start(bf16[32,4,32,128]{3,2,1,0:T(8,128)(2,1)} %broadcast_in_dim.76), calls=%async_computation | async-start | bytes 2097152 | tf_op jit(solution)/shard_map/while/body/eval_jaxpr/all_to_all | solution.py:67
  401.2 7.7 %collective-permute-start = (bf16[32,32,128]{2,1,0:T(8,128)(2,1)S(1)}, bf16[32,32,128]{2,1,0:T(8,128)(2,1)S(1)}, u32[]{:S(2)}, u32[]{:S(2)}) collective-permute-start(bf16[32,32,128]{2,1,0:T(8,128)(2,1)S(1)} %bitcast.69), channel_id=1, source_target_pairs={{0,32},{32,64},{64,96},{96,128},{128,160},{160,192},{192,224},{1,3... | collective-permute-start | bytes 786440 | tf_op jit(solution)/shard_map/while/body/eval_jaxpr/ppermute | solution.py:10
  408.9 42.7 %copy-start = (bf16[2,32,32,128]{3,2,1,0:T(8,128)(2,1)}, bf16[2,32,32,128]{3,2,1,0:T(8,128)(2,1)S(1)}, u32[]{:S(2)}) copy-start(bf16[2,32,32,128]{3,2,1,0:T(8,128)(2,1)S(1)} %get-tuple-element.217) | copy-start | bytes 1572868
  (13 other events, 41.3 us)

commit v2 on v0

v2 whole, which is shorter than its diff:
```python
import jax
import jax.numpy as jnp
from jax import lax
from jax.experimental import pallas as pl
from jax.experimental.pallas import tpu as pltpu
from jax.sharding import PartitionSpec as P

SIDE = 32
CELLS = SIDE * SIDE
RING = 4 * SIDE
C = 128
TAPS = 9
SPLIT = 4
PART = SIDE // SPLIT
PICK = 8 * PART + 16
VMEM_BYTES = 40 * 1024 * 1024


def iota(shape, axis):
    return lax.broadcasted_iota(jnp.int32, shape, axis)


def onehot(target, columns):
    return (target[:, None] == iota((target.shape[0], columns), 1)).astype(jnp.bfloat16)


def lookup(table, index):
    flat = table.reshape(-1)
    hit = index[..., None] == jnp.arange(flat.shape[0], dtype=jnp.int32)
    return jnp.sum(jnp.where(hit, flat, 0), axis=-1)


def rim_cell(edge, depth, place):
    last = SIDE - 1
    return jnp.where(
        edge == 0,
        depth * SIDE + place,
        jnp.where(
            edge == 1,
            place * SIDE + last - depth,
            jnp.where(edge == 2, (last - depth) * SIDE + place, place * SIDE + depth),
        ),
    )


def selections(neighbor, edge_of, reverse, tile, part):
    d4 = jnp.arange(4, dtype=jnp.int32)
    own = tile * 4 + d4
    nbr, edge, flip = lookup(neighbor, own), lookup(edge_of, own), lookup(reverse, own)
    tiles = neighbor.shape[0]
    row = jnp.arange(8 * PART, dtype=jnp.int32)
    share = rim_cell(row // (2 * PART), row // PART % 2, part * PART + row % PART)
    rim = onehot(share, CELLS)
    width = 8 * PART
    row = jnp.arange(8 * PART, dtype=jnp.int32)
    d = row // (2 * PART)
    strips = lookup(nbr, d) * width + lookup(edge, d) * (2 * PART) + row % (2 * PART)
    row = jnp.arange(16, dtype=jnp.int32)
    d, end, depth = row // 4, row // 2 % 2, row % 2
    e = lookup(edge, d)
    side = jnp.where(e % 2 == 0, 3 - 2 * end, 2 * end)
    slot = lookup(nbr, d) * 4 + side
    place = jnp.where((e == 0) | (e == 3), depth, SIDE - 1 - depth)
    place = jnp.where(lookup(reverse, slot) == 1, SIDE - 1 - place, place)
    ends = lookup(neighbor, slot) * width + lookup(edge_of, slot) * (2 * PART) + place % PART
    ends = jnp.where(place // PART == part, ends, -1)
    pick = onehot(jnp.concatenate([strips, ends]), tiles * width)
    row = jnp.arange(RING, dtype=jnp.int32)
    d, place = row // SIDE, row % SIDE
    turned = jnp.where(lookup(flip, d) == 1, SIDE - 1 - place, place)

    def picked(where, depth):
        return where // PART * PICK + d * (2 * PART) + depth * PART + where % PART

    end = jnp.where(place == 0, 0, jnp.where(place == SIDE - 1, 1, -1))
    column = iota((RING, SPLIT * PICK), 1) % PICK

    def beyond(depth):
        target = jnp.where(end < 0, -1, 8 * PART + d * 4 + end * 2 + depth)
        return (target[:, None] == column).astype(jnp.bfloat16)

    ring = jnp.concatenate(
        [
            onehot(picked(turned, 0), SPLIT * PICK),
            onehot(picked(place, 0), SPLIT * PICK),
            onehot(picked(place, 1), SPLIT * PICK),
            beyond(0),
            beyond(1),
        ]
    )
    facing = onehot(rim_cell(d, 0, turned), CELLS)
    turn = onehot(d * SIDE + turned, RING)
    return edge, rim, pick, ring, facing, turn


def sigmoid(value):
    return 1.0 / (1.0 + jnp.exp(-value))


def fill_patches(state, padded, patches):
    padded[1 : SIDE + 1, 8 : SIDE + 8, :] = (
        state[0:CELLS, :].astype(jnp.float32).reshape(SIDE, SIDE, C)
    )
    halo = state[CELLS : CELLS + RING, :].astype(jnp.float32)
    empty = jnp.zeros((8, C), jnp.float32)
    for row, first in ((0, 0), (SIDE + 1, 2 * SIDE)):
        padded[row, 0:8, :] = empty
        padded[row, 8 : SIDE + 8, :] = halo[first : first + SIDE]
        padded[row, SIDE + 8 : SIDE + 16, :] = empty
    padded[1 : SIDE + 1, SIDE + 8, :] = halo[SIDE : 2 * SIDE]
    padded[1 : SIDE + 1, 7, :] = halo[3 * SIDE : 4 * SIDE]
    for dx in range(3):
        shifted = padded[:, 7 + dx : 7 + dx + SIDE, :].astype(jnp.bfloat16)
        shifted = shifted.reshape((SIDE + 2) * SIDE, C)
        for dy in range(3):
            k = dy * 3 + dx
            patches[:, k * C : (k + 1) * C] = shifted[dy * SIDE : dy * SIDE + CELLS]


def next_state(state, pre_act):
    return (state + pre_act * sigmoid(pre_act)).astype(jnp.bfloat16)


def dot(a, b):
    return jnp.dot(a, b, preferred_element_type=jnp.float32)


def round_kernel(
    edge, start, gathered, weights, rim, ring, facing, turn, first, second, out, share, padded, patches, side_patches
):
    strips = dot(ring[...], gathered[...])
    first[0:CELLS, :] = start[...]
    first[CELLS : CELLS + RING, :] = strips[0:RING].astype(jnp.bfloat16)
    near, far = strips[RING : 2 * RING], strips[2 * RING : 3 * RING]
    near_ends, far_ends = strips[3 * RING : 4 * RING], strips[4 * RING : 5 * RING]
    mine = dot(facing[...], start[...])
    place = iota((RING, C), 0) % SIDE
    for a, (cells, ends) in enumerate(((mine, jnp.zeros_like(mine)), (near, near_ends), (far, far_ends))):
        below = jnp.where(place == 0, ends, pltpu.roll(cells, 1, 0))
        above = jnp.where(place == SIDE - 1, ends, pltpu.roll(cells, RING - 1, 0))
        for b, moved in enumerate((below, cells, above)):
            moved = moved.astype(jnp.bfloat16)
            for d in range(4):
                e = edge[d]
                across = jnp.where((e == 0) | (e == 3), a, 2 - a)
                tap = jnp.where(e % 2 == 0, 3 * across + b, 3 * b + across)
                side_patches[d * SIDE : (d + 1) * SIDE, pl.ds(pl.multiple_of(tap * C, C), C)] = moved[
                    d * SIDE : (d + 1) * SIDE
                ]
    new_side = next_state(near, dot(side_patches[...], weights[0]))
    fill_patches(first, padded, patches)
    second[0:CELLS, :] = next_state(start[...].astype(jnp.float32), dot(patches[...], weights[0]))
    second[CELLS : CELLS + RING, :] = dot(turn[...], new_side).astype(jnp.bfloat16)
    fill_patches(second, padded, patches)
    new = next_state(second[0:CELLS, :].astype(jnp.float32), dot(patches[...], weights[1]))
    out[...] = new
    share[...] = dot(rim[...], new).astype(jnp.bfloat16)


def two_sections(edge, start, gathered, weights, rim, ring, facing, turn):
    vmem = pl.BlockSpec(memory_space=pltpu.VMEM)
    bf16 = jnp.bfloat16
    return pl.pallas_call(
        round_kernel,
        out_shape=(
            jax.ShapeDtypeStruct((CELLS + RING, C), bf16),
            jax.ShapeDtypeStruct((CELLS + RING, C), bf16),
            jax.ShapeDtypeStruct((CELLS, C), bf16),
            jax.ShapeDtypeStruct((8 * PART, C), bf16),
        ),
        in_specs=[pl.BlockSpec(memory_space=pltpu.SMEM)] + [vmem] * 7,
        out_specs=(vmem,) * 4,
        scratch_shapes=[
            pltpu.VMEM((SIDE + 2, SIDE + 16, C), jnp.float32),
            pltpu.VMEM((CELLS, TAPS * C), bf16),
            pltpu.VMEM((RING, TAPS * C), bf16),
        ],
        compiler_params=pltpu.CompilerParams(vmem_limit_bytes=VMEM_BYTES),
        cost_estimate=pl.CostEstimate(
            flops=2 * 2 * CELLS * TAPS * C * C, bytes_accessed=4 << 20, transcendentals=2 * CELLS * C
        ),
        name="two_sections",
    )(edge, start, gathered, weights, rim, ring, facing, turn)


def choose_kernel(index, *refs):
    states, (kept, sent), sems = refs[:8], refs[8:10], refs[10]
    for slot, target in ((0, kept), (1, sent)):
        for s in range(8):

            @pl.when(index[slot] == s)
            def _(s=s, slot=slot, target=target):
                copy = pltpu.make_async_copy(states[s], target, sems.at[slot])
                copy.start()
                copy.wait()


def choose(index, states):
    shape = jax.ShapeDtypeStruct(states[0].shape, states[0].dtype)
    return pl.pallas_call(
        choose_kernel,
        out_shape=(shape, shape),
        in_specs=[pl.BlockSpec(memory_space=pltpu.SMEM)] + [pl.BlockSpec(memory_space=pl.ANY)] * 8,
        out_specs=(pl.BlockSpec(memory_space=pl.ANY),) * 2,
        scratch_shapes=[pltpu.SemaphoreType.DMA((2,))],
        name="choose",
    )(index, *states)


def gradient_kernel(state, cotangent, weights, before, level, term, padded, patches):
    fill_patches(state, padded, patches)
    pre_act = dot(patches[...], weights[...])
    gate = sigmoid(pre_act)
    level[...] = (state[0:CELLS, :].astype(jnp.float32) + pre_act * gate).astype(jnp.bfloat16)
    slope = gate * (1.0 + pre_act * (1.0 - gate))
    delta = (cotangent[...].astype(jnp.float32) * slope).astype(jnp.bfloat16)
    added = lax.dot_general(
        patches[...], delta, (((0,), (0,)), ((), ())), preferred_element_type=jnp.float32
    )
    term[...] = (before[...] + added).astype(term.dtype)


def gradient(state, cotangent, weights, before, dtype):
    vmem = pl.BlockSpec(memory_space=pltpu.VMEM)
    return pl.pallas_call(
        gradient_kernel,
        out_shape=(
            jax.ShapeDtypeStruct((CELLS, C), jnp.bfloat16),
            jax.ShapeDtypeStruct((TAPS * C, C), dtype),
        ),
        in_specs=[vmem] * 4,
        out_specs=(vmem,) * 2,
        scratch_shapes=[
            pltpu.VMEM((SIDE + 2, SIDE + 16, C), jnp.float32),
            pltpu.VMEM((CELLS, TAPS * C), jnp.bfloat16),
        ],
        compiler_params=pltpu.CompilerParams(vmem_limit_bytes=VMEM_BYTES),
        cost_estimate=pl.CostEstimate(
            flops=2 * 2 * CELLS * TAPS * C * C, bytes_accessed=3 << 20, transcendentals=CELLS * C
        ),
        name="gradient",
    )(state, cotangent, weights, before)


def share_out(block, axis, groups=None):
    count = lax.axis_size(axis) if groups is None else len(groups[0])
    return lax.all_to_all(
        jnp.broadcast_to(block[None], (count,) + block.shape), axis, 0, 0, axis_index_groups=groups
    )


def sum_terms(term):
    axes = ("dp", "tile")
    count = lax.axis_size(axes)
    rows = term.shape[0] // count
    pieces = lax.all_to_all(term.reshape(count, rows, term.shape[1]), axes, 0, 0)
    piece = jnp.sum(pieces.astype(jnp.float32), axis=0).astype(jnp.bfloat16)
    return share_out(piece, axes).reshape(term.shape).astype(jnp.float32)


def local(inputs, neighbor, edge_of, reverse, weights, cotangent):
    segment = lax.axis_index("segment")
    sample, part = segment // SPLIT, segment % SPLIT
    teams = [[t * SPLIT + p for p in range(SPLIT)] for t in range(2)]
    kernels = lax.all_gather(weights, "segment", axis=0, tiled=True)
    edge, rim, pick, ring, facing, turn = selections(
        neighbor, edge_of, reverse, lax.axis_index("tile"), part
    )
    state = lax.dynamic_index_in_dim(inputs[:, 0], sample, 0, False).reshape(CELLS, C)
    share = dot(rim, state).astype(jnp.bfloat16)
    states = []
    for step in range(4):
        rims = share_out(share, "tile").reshape(-1, C)
        picked = dot(pick, rims).astype(jnp.bfloat16)
        gathered = share_out(picked, "segment", teams).reshape(-1, C)
        pair = kernels[2 * step : 2 * step + 2]
        first, second, state, share = two_sections(edge, state, gathered, pair, rim, ring, facing, turn)
        states += [first, second]
    partner = segment ^ SPLIT
    kept, sent = choose(jnp.stack([segment, partner]).astype(jnp.int32), states)
    other = lax.ppermute(sent, "segment", [(s, s ^ SPLIT) for s in range(8)])
    cotans = cotangent[0, :, 0].reshape(2, CELLS, C)
    mine = lax.dynamic_index_in_dim(cotans, sample, 0, False)
    theirs = lax.dynamic_index_in_dim(cotans, 1 - sample, 0, False)
    zero = jnp.zeros((TAPS * C, C), jnp.float32)
    level_mine, term = gradient(kept, mine, weights[0], zero, jnp.float32)
    level_other, term = gradient(other, theirs, weights[0], term, jnp.bfloat16)
    total = sum_terms(term)
    low = jnp.where(sample == 0, level_mine, level_other)
    high = jnp.where(sample == 0, level_other, level_mine)
    levels = jnp.stack([low, high]).reshape(1, 2, 1, SIDE, SIDE, C)
    return levels, total[None]


def solution(mesh):
    placed = (
        P("dp", "tile", None, None, None),
        P(),
        P(),
        P(),
        P("segment", None, None),
        P("segment", "dp", "tile", None, None, None),
    )
    return jax.shard_map(
        local,
        mesh=mesh,
        in_specs=placed,
        out_specs=(P("segment", "dp", "tile", None, None, None), P("segment", None, None)),
        check_vma=False,
    )
```

time: 1660 us -> 265 us (0.16)
  the two profiles are of different devices: /device:TPU:2 before, /device:TPU:4 now
where the time goes in v2:
time: 265 us; the launch traced here: 264 us
  blocking collectives  85.7 us (32%)
  waiting for transfers between devices  64.2 us (24%)
  Pallas kernels  41.8 us (16%)
  starting transfers between devices  34.1 us (13%)
  local copies, waits for them, and re-layouts  17.7 us (7%)
  between operations  14.6 us (6%)
  other arithmetic  4.12 us (2%)
    all_to_all x4, blocking collectives, share_out(): lax.all_to_all(jnp.broadcast_to(block[None], (count,) + block.shape), axi...  62.5 us
    all_to_all x5, waiting for transfers between devices, share_out(): lax.all_to_all(jnp.broadcast_to(block[None], (count,) + block.shape), axi...  48.4 us
    all_to_all x5, starting transfers between devices, share_out(): lax.all_to_all(jnp.broadcast_to(block[None], (count,) + block.shape), axi...  31.2 us
    all_to_all x1, blocking collectives, sum_terms(): lax.all_to_all(term.reshape(count, rows, term.shape[1]), axes, 0, 0)  23.2 us
    pallas_call x1, Pallas kernels, choose(): pl.pallas_call(choose_kernel, out_shape=(shape, shape), in_specs=[pl.Bloc...  20.9 us
    pallas_call x4, Pallas kernels, two_sections(): pl.pallas_call(round_kernel, out_shape=(jax.ShapeDtypeStruct((CELLS + RIN...  16.1 us
    all_gather x1, waiting for transfers between devices, local(): kernels = lax.all_gather(weights, 'segment', axis=0, tiled=True)  10.5 us
    unnamed x45, local copies, waits for them, and re-layouts  9.3 us
  transfers between devices with their start and end apart: 7, of which 6 were waited for; matrix products, arithmetic and copies ran while one was open for 3% of the time, Pallas kernels for 1%

profile of v2, /device:TPU:4, one launch (start us, length us, event | category | flops | bytes accessed | tf_op | source)
XLA Modules:
  0.0 263.7 jit_solution(13283027289475908207)
XLA Ops:
  10.1 13.7 %all-to-all-start = ((bf16[32,64,128]{2,1,0:T(8,128)(2,1)}), bf16[32,64,128]{2,1,0:T(8,128)(2,1)S(1)}, u32[]{:S(2)}, u32[]{:S(2)}) async-start(bf16[32,64,128]{2,1,0:T(8,128)(2,1)} %broadcast_in_dim.177), calls=%async_computation | async-start | bytes 1048576 | tf_op jit(solution)/shard_map/all_to_all | solution.py:247
  27.8 12.8 %all-to-all-done = bf16[32,64,128]{2,1,0:T(8,128)(2,1)S(1)} async-done(((bf16[32,64,128]{2,1,0:T(8,128)(2,1)}), bf16[32,64,128]{2,1,0:T(8,128)(2,1)S(1)}, u32[]{:S(2)}, u32[]{:S(2)}) %all-to-all-start) | async-done | bytes 524320 | tf_op jit(solution)/shard_map/all_to_all | solution.py:247
  41.6 3.9 %all-to-all-start.1 = ((bf16[4,80,128]{2,1,0:T(8,128)(2,1)}), bf16[4,80,128]{2,1,0:T(8,128)(2,1)}, u32[]{:S(2)}, u32[]{:S(2)}) async-start(bf16[4,80,128]{2,1,0:T(8,128)(2,1)} %broadcast_in_dim.178), calls=%async_computation.1 | async-start | bytes 163840 | tf_op jit(solution)/shard_map/all_to_all | solution.py:247
  45.5 10.5 %all-gather.2.cloned.1.call-done = bf16[8,1152,128]{2,1,0:T(8,128)(2,1)} async-done(((bf16[1,1152,128]{2,1,0:T(8,128)(2,1)}), bf16[8,1152,128]{2,1,0:T(8,128)(2,1)}) %all-gather.2.cloned.1.call-update) | async-done | bytes 2359312 | tf_op jit(solution)/shard_map/all_gather | solution.py:265
  59.7 4.2 %two_sections.4 = (bf16[1152,128]{1,0:T(8,128)(2,1)S(1)}, bf16[1152,128]{1,0:T(8,128)(2,1)S(1)}, bf16[1024,128]{1,0:T(8,128)(2,1)S(1)}, bf16[64,128]{1,0:T(8,128)(2,1)S(1)}) custom-call(s32[4]{0:T(128)S(1)} %get-tuple-element.44.edge, bf16[1024,128]{1,0:T(8,128)(2,1)S(1)} %bitcast.27, bf16[320,128]{1,0:T(8,128)(2,1)} %bitcast.4.gathered, ...), custom_call_target="tpu_custom_call" | custom-call | flops 603979776 | bytes 4194304 | tf_op jit(solution)/shard_map/two_sections/pallas_call | solution.py:163
  65.4 27.0 %all_to_all.50 = bf16[32,64,128]{2,1,0:T(8,128)(2,1)S(1)} all-to-all(bf16[32,64,128]{2,1,0:T(8,128)(2,1)S(1)} %broadcast_in_dim.182), channel_id=1, replica_groups=mesh['dp'=2,'segment'=8,'tile'=32] {'tile'}, dimensions={0} | all-to-all | bytes 1048576 | tf_op jit(solution)/shard_map/all_to_all | solution.py:247
  92.8 6.9 %all_to_all.51 = bf16[4,80,128]{2,1,0:T(8,128)(2,1)S(1)} all-to-all(bf16[4,80,128]{2,1,0:T(8,128)(2,1)S(1)} %broadcast_in_dim.183), channel_id=1, replica_groups={{0,32,64,96},{128,160,192,224},{1,33,65,97},{129,161,193,225},{2,34,66,..., dimensions={0} | all-to-all | bytes 163840 | tf_op jit(solution)/shard_map/all_to_all | solution.py:247
  99.7 3.8 %two_sections.5 = (bf16[1152,128]{1,0:T(8,128)(2,1)S(1)}, bf16[1152,128]{1,0:T(8,128)(2,1)S(1)}, bf16[1024,128]{1,0:T(8,128)(2,1)S(1)}, bf16[64,128]{1,0:T(8,128)(2,1)S(1)}) custom-call(s32[4]{0:T(128)S(1)} %get-tuple-element.44.edge, bf16[1024,128]{1,0:T(8,128)(2,1)S(1)} %get-tuple-element.24.start, bf16[320,128]{1,0:T(8,128)(2,1)S(1)} %bitcast.29, ...), custom_call_target="tpu_custom_call" | custom-call | flops 603979776 | bytes 4194304 | tf_op jit(solution)/shard_map/two_sections/pallas_call | solution.py:163
  103.6 22.0 %all_to_all.52 = bf16[32,64,128]{2,1,0:T(8,128)(2,1)S(1)} all-to-all(bf16[32,64,128]{2,1,0:T(8,128)(2,1)S(1)} %broadcast_in_dim.184), channel_id=1, replica_groups=mesh['dp'=2,'segment'=8,'tile'=32] {'tile'}, dimensions={0} | all-to-all | bytes 1048576 | tf_op jit(solution)/shard_map/all_to_all | solution.py:247
  125.9 6.6 %all_to_all.53 = bf16[4,80,128]{2,1,0:T(8,128)(2,1)S(1)} all-to-all(bf16[4,80,128]{2,1,0:T(8,128)(2,1)S(1)} %broadcast_in_dim.185), channel_id=1, replica_groups={{0,32,64,96},{128,160,192,224},{1,33,65,97},{129,161,193,225},{2,34,66,..., dimensions={0} | all-to-all | bytes 163840 | tf_op jit(solution)/shard_map/all_to_all | solution.py:247
  132.5 3.8 %two_sections.6 = (bf16[1152,128]{1,0:T(8,128)(2,1)S(1)}, bf16[1152,128]{1,0:T(8,128)(2,1)S(1)}, bf16[1024,128]{1,0:T(8,128)(2,1)S(1)}, bf16[64,128]{1,0:T(8,128)(2,1)S(1)}) custom-call(s32[4]{0:T(128)S(1)} %get-tuple-element.44.edge, bf16[1024,128]{1,0:T(8,128)(2,1)S(1)} %get-tuple-element.28.start, bf16[320,128]{1,0:T(8,128)(2,1)S(1)} %bitcast.30, ...), custom_call_target="tpu_custom_call" | custom-call | flops 603979776 | bytes 4194304 | tf_op jit(solution)/shard_map/two_sections/pallas_call | solution.py:163
  138.0 5.4 %all-to-all-start.6 = ((bf16[32,64,128]{2,1,0:T(8,128)(2,1)}), bf16[32,64,128]{2,1,0:T(8,128)(2,1)S(1)}, u32[]{:S(2)}, u32[]{:S(2)}) async-start(bf16[32,64,128]{2,1,0:T(8,128)(2,1)} %broadcast_in_dim.186), calls=%async_computation.6 | async-start | bytes 1048576 | tf_op jit(solution)/shard_map/all_to_all | solution.py:247
  143.4 16.6 %all-to-all-done.6 = bf16[32,64,128]{2,1,0:T(8,128)(2,1)S(1)} async-done(((bf16[32,64,128]{2,1,0:T(8,128)(2,1)}), bf16[32,64,128]{2,1,0:T(8,128)(2,1)S(1)}, u32[]{:S(2)}, u32[]{:S(2)}) %all-to-all-start.6) | async-done | bytes 524320 | tf_op jit(solution)/shard_map/all_to_all | solution.py:247
  160.9 3.5 %all-to-all-start.7 = ((bf16[4,80,128]{2,1,0:T(8,128)(2,1)}), bf16[4,80,128]{2,1,0:T(8,128)(2,1)S(1)}, u32[]{:S(2)}, u32[]{:S(2)}) async-start(bf16[4,80,128]{2,1,0:T(8,128)(2,1)} %broadcast_in_dim.187), calls=%async_computation.7 | async-start | bytes 163840 | tf_op jit(solution)/shard_map/all_to_all | solution.py:247
  165.1 3.3 %all-to-all-done.7 = bf16[4,80,128]{2,1,0:T(8,128)(2,1)S(1)} async-done(((bf16[4,80,128]{2,1,0:T(8,128)(2,1)}), bf16[4,80,128]{2,1,0:T(8,128)(2,1)S(1)}, u32[]{:S(2)}, u32[]{:S(2)}) %all-to-all-start.7) | async-done | bytes 81952 | tf_op jit(solution)/shard_map/all_to_all | solution.py:247
  169.4 4.4 %two_sections.7 = (bf16[1152,128]{1,0:T(8,128)(2,1)S(1)}, bf16[1152,128]{1,0:T(8,128)(2,1)S(1)}, bf16[1024,128]{1,0:T(8,128)(2,1)}, bf16[64,128]{1,0:T(8,128)(2,1)}) custom-call(s32[4]{0:T(128)S(1)} %get-tuple-element.44.edge, bf16[1024,128]{1,0:T(8,128)(2,1)S(1)} %copy-done.17, bf16[320,128]{1,0:T(8,128)(2,1)S(1)} %bitcast.28, ...), custom_call_target="tpu_custom_call" | custom-call | flops 603979776 | bytes 4194304 | tf_op jit(solution)/shard_map/two_sections/pallas_call | solution.py:163
  175.2 20.9 %choose.1 = (bf16[1152,128]{1,0:T(8,128)(2,1)}, bf16[1152,128]{1,0:T(8,128)(2,1)}) custom-call(s32[2]{0:T(128)} %pad_add_fusion.index, bf16[1152,128]{1,0:T(8,128)(2,1)} %copy-done.1, bf16[1152,128]{1,0:T(8,128)(2,1)} %copy-done.2, bf16[1152,128]{1,0:T(8,128)(2,1)} %copy-done.3, bf16[1152,128]{1,0:T(8,128)(2,1)} %copy-done.4, bf16[1152,128]{1,0:T(8,128)(2,1)} %copy-done.5, ...), custom_call_target="tpu_custom_call" | custom-call | tf_op jit(solution)/shard_map/choose/pallas_call | solution.py:200
  196.1 2.9 %collective-permute-start = (bf16[1152,128]{1,0:T(8,128)(2,1)}, bf16[1152,128]{1,0:T(8,128)(2,1)S(1)}, u32[]{:S(2)}, u32[]{:S(2)}) collective-permute-start(bf16[1152,128]{1,0:T(8,128)(2,1)} %get-tuple-element.38), channel_id=1, source_target_pairs={{0,128},{32,160},{64,192},{96,224},{128,0},{160,32},{192,64},{224,... | collective-permute-start | bytes 884744 | tf_op jit(solution)/shard_map/ppermute | solution.py:281
  201.1 2.4 gradient.2
  203.5 4.7 %collective-permute-done.state = bf16[1152,128]{1,0:T(8,128)(2,1)S(1)} collective-permute-done((bf16[1152,128]{1,0:T(8,128)(2,1)}, bf16[1152,128]{1,0:T(8,128)(2,1)S(1)}, u32[]{:S(2)}, u32[]{:S(2)}) %collective-permute-start) | collective-permute-done | bytes 294944 | tf_op jit(solution)/shard_map/ppermute | solution.py:281
  208.2 2.4 gradient.3
  210.7 23.2 %all_to_all.54 = bf16[64,18,128]{2,1,0:T(8,128)(2,1)S(1)} all-to-all(bf16[64,18,128]{2,1,0:T(8,128)(2,1)S(1)} %reshape.342), channel_id=1, replica_groups=mesh['dp'=2,'segment'=8,'tile'=32] {'dp','tile'}, dimensions={0} | all-to-all | bytes 589824 | tf_op jit(solution)/shard_map/all_to_all | solution.py:256
  234.8 4.6 %all-to-all-start.9 = ((bf16[64,18,128]{2,1,0:T(8,128)(2,1)}), bf16[64,18,128]{2,1,0:T(8,128)(2,1)S(1)}, u32[]{:S(2)}, u32[]{:S(2)}) async-start(bf16[64,18,128]{2,1,0:T(8,128)(2,1)} %broadcast_in_dim.189), calls=%async_computation.9 | async-start | bytes 786432 | tf_op jit(solution)/shard_map/all_to_all | solution.py:247
  240.3 15.6 %all-to-all-done.9 = bf16[64,18,128]{2,1,0:T(8,128)(2,1)S(1)} async-done(((bf16[64,18,128]{2,1,0:T(8,128)(2,1)}), bf16[64,18,128]{2,1,0:T(8,128)(2,1)S(1)}, u32[]{:S(2)}, u32[]{:S(2)}) %all-to-all-start.9) | async-done | bytes 294944 | tf_op jit(solution)/shard_map/all_to_all | solution.py:247
  (104 shorter events, 24.0 us)
Async XLA Ops:
  7.2 1.0 copy-start
  7.2 17.5 %copy-start.18 = (s32[32,4]{0,1:T(4,128)S(1)}, s32[32,4]{0,1:T(4,128)}, u32[]{:S(2)}) copy-start(s32[32,4]{0,1:T(4,128)} %param.9) | copy-start | bytes 1540
  7.2 17.7 %copy-start.19 = (s32[32,4]{0,1:T(4,128)S(1)}, s32[32,4]{0,1:T(4,128)}, u32[]{:S(2)}) copy-start(s32[32,4]{0,1:T(4,128)} %param.7) | copy-start | bytes 1540
  7.2 17.9 %copy-start.20 = (s32[32,4]{0,1:T(4,128)S(1)}, s32[32,4]{0,1:T(4,128)}, u32[]{:S(2)}) copy-start(s32[32,4]{0,1:T(4,128)} %param.8) | copy-start | bytes 1540
  10.1 30.6 %all-to-all-start = ((bf16[32,64,128]{2,1,0:T(8,128)(2,1)}), bf16[32,64,128]{2,1,0:T(8,128)(2,1)S(1)}, u32[]{:S(2)}, u32[]{:S(2)}) async-start(bf16[32,64,128]{2,1,0:T(8,128)(2,1)} %broadcast_in_dim.177), calls=%async_computation | async-start | bytes 1048576 | tf_op jit(solution)/shard_map/all_to_all | solution.py:247
  23.8 32.2 %all-gather.2.cloned.1.call-start = ((), (), s32[]{:S(2)}) async-start(), calls=%async_computation.10 | async-start | bytes 2654208 | tf_op jit(solution)/shard_map/all_gather | solution.py:265
  41.6 16.2 %all-to-all-start.1 = ((bf16[4,80,128]{2,1,0:T(8,128)(2,1)}), bf16[4,80,128]{2,1,0:T(8,128)(2,1)}, u32[]{:S(2)}, u32[]{:S(2)}) async-start(bf16[4,80,128]{2,1,0:T(8,128)(2,1)} %broadcast_in_dim.178), calls=%async_computation.1 | async-start | bytes 163840 | tf_op jit(solution)/shard_map/all_to_all | solution.py:247
  57.8 1.0 copy-start.11
  58.7 0.9 copy-start.12
  59.7 40.0 %copy-start.13 = (bf16[128,1024]{1,0:T(8,128)(2,1)S(1)}, bf16[128,1024]{1,0:T(8,128)(2,1)}, u32[]{:S(2)}) copy-start(bf16[128,1024]{1,0:T(8,128)(2,1)} %fusion.facing) | copy-start | bytes 786436
  63.9 0.7 copy-start.1
  103.5 32.8 %copy-start.3 = (bf16[1152,128]{1,0:T(8,128)(2,1)}, bf16[1152,128]{1,0:T(8,128)(2,1)S(1)}, u32[]{:S(2)}) copy-start(bf16[1152,128]{1,0:T(8,128)(2,1)S(1)} %get-tuple-element.26.refs_2_) | copy-start | bytes 884740
  103.5 34.5 %copy-start.4 = (bf16[1152,128]{1,0:T(8,128)(2,1)}, bf16[1152,128]{1,0:T(8,128)(2,1)S(1)}, u32[]{:S(2)}) copy-start(bf16[1152,128]{1,0:T(8,128)(2,1)S(1)} %get-tuple-element.27.refs_3_) | copy-start | bytes 884740
  132.5 35.9 %copy-start.14 = (bf16[128,1024]{1,0:T(8,128)(2,1)S(1)}, bf16[128,1024]{1,0:T(8,128)(2,1)}, u32[]{:S(2)}) copy-start(bf16[128,1024]{1,0:T(8,128)(2,1)} %fusion.facing) | copy-start | bytes 786436
  137.0 38.2 %copy-start.5 = (bf16[1152,128]{1,0:T(8,128)(2,1)}, bf16[1152,128]{1,0:T(8,128)(2,1)S(1)}, u32[]{:S(2)}) copy-start(bf16[1152,128]{1,0:T(8,128)(2,1)S(1)} %get-tuple-element.30.refs_4_) | copy-start | bytes 884740
  137.0 38.2 %copy-start.6 = (bf16[1152,128]{1,0:T(8,128)(2,1)}, bf16[1152,128]{1,0:T(8,128)(2,1)S(1)}, u32[]{:S(2)}) copy-start(bf16[1152,128]{1,0:T(8,128)(2,1)S(1)} %get-tuple-element.31.refs_5_) | copy-start | bytes 884740
  138.0 22.0 %all-to-all-start.6 = ((bf16[32,64,128]{2,1,0:T(8,128)(2,1)}), bf16[32,64,128]{2,1,0:T(8,128)(2,1)S(1)}, u32[]{:S(2)}, u32[]{:S(2)}) async-start(bf16[32,64,128]{2,1,0:T(8,128)(2,1)} %broadcast_in_dim.186), calls=%async_computation.6 | async-start | bytes 1048576 | tf_op jit(solution)/shard_map/all_to_all | solution.py:247
  160.9 7.5 %all-to-all-start.7 = ((bf16[4,80,128]{2,1,0:T(8,128)(2,1)}), bf16[4,80,128]{2,1,0:T(8,128)(2,1)S(1)}, u32[]{:S(2)}, u32[]{:S(2)}) async-start(bf16[4,80,128]{2,1,0:T(8,128)(2,1)} %broadcast_in_dim.187), calls=%async_computation.7 | async-start | bytes 163840 | tf_op jit(solution)/shard_map/all_to_all | solution.py:247
  168.4 1.0 copy-start.17
  174.4 0.7 copy-start.8
  175.2 25.0 %copy-start.9 = (bf16[1,1152,128]{2,1,0:T(8,128)(2,1)S(1)}, bf16[1,1152,128]{2,1,0:T(8,128)(2,1)}, u32[]{:S(2)}) copy-start(bf16[1,1152,128]{2,1,0:T(8,128)(2,1)} %param.10) | copy-start | bytes 884740
  196.1 12.1 %collective-permute-start = (bf16[1152,128]{1,0:T(8,128)(2,1)}, bf16[1152,128]{1,0:T(8,128)(2,1)S(1)}, u32[]{:S(2)}, u32[]{:S(2)}) collective-permute-start(bf16[1152,128]{1,0:T(8,128)(2,1)} %get-tuple-element.38), channel_id=1, source_target_pairs={{0,128},{32,160},{64,192},{96,224},{128,0},{160,32},{192,64},{224,... | collective-permute-start | bytes 884744 | tf_op jit(solution)/shard_map/ppermute | solution.py:281
  200.1 1.0 copy-start.15
  234.8 21.1 %all-to-all-start.9 = ((bf16[64,18,128]{2,1,0:T(8,128)(2,1)}), bf16[64,18,128]{2,1,0:T(8,128)(2,1)S(1)}, u32[]{:S(2)}, u32[]{:S(2)}) async-start(bf16[64,18,128]{2,1,0:T(8,128)(2,1)} %broadcast_in_dim.189), calls=%async_computation.9 | async-start | bytes 786432 | tf_op jit(solution)/shard_map/all_to_all | solution.py:247
  (4 other events, 2.8 us)
Sparse Core Ops, SparseCore 0:
  26.8 29.1 all-gather.1

commit v3 on v2

v3 whole, which is shorter than its diff:
```python
import jax
import jax.numpy as jnp
from jax import lax
from jax.experimental import pallas as pl
from jax.experimental.pallas import tpu as pltpu
from jax.sharding import PartitionSpec as P

SIDE = 32
CELLS = SIDE * SIDE
RING = 4 * SIDE
C = 128
TAPS = 9
DEPTH = 4
SPLIT = 4
PART = SIDE // SPLIT
EDGE = DEPTH * PART
SHARE = 4 * EDGE
BLOCKS = [[(x, c) for x in range(DEPTH + 1 - j) for c in range(DEPTH - j)] for j in range(1, DEPTH)]
SLOTS = sum(len(block) for block in BLOCKS)
FANS = 8
PICK = SHARE + FANS * SLOTS
VMEM_BYTES = 48 * 1024 * 1024


def iota(shape, axis):
    return lax.broadcasted_iota(jnp.int32, shape, axis)


def onehot(target, columns):
    return (target[:, None] == iota((target.shape[0], columns), 1)).astype(jnp.bfloat16)


def lookup(table, index):
    flat = table.reshape(-1)
    hit = index[..., None] == jnp.arange(flat.shape[0], dtype=jnp.int32)
    return jnp.sum(jnp.where(hit, flat, 0), axis=-1)


def rim_cell(edge, depth, place):
    last = SIDE - 1
    return jnp.where(
        edge == 0,
        depth * SIDE + place,
        jnp.where(
            edge == 1,
            place * SIDE + last - depth,
            jnp.where(edge == 2, (last - depth) * SIDE + place, place * SIDE + depth),
        ),
    )


def walk(tables, tile, edge, end):
    neighbor, edge_of, reverse = tables
    slot = tile * 4 + jnp.where(edge % 2 == 0, 3 - 2 * end, 2 * end)
    corner = jnp.where((edge == 0) | (edge == 3), 0, 1)
    corner = jnp.where(lookup(reverse, slot) == 1, 1 - corner, corner)
    return lookup(neighbor, slot), lookup(edge_of, slot), corner


def spread(columns, counts):
    return jnp.concatenate(
        [jnp.broadcast_to(col[:, None], (FANS, n)) for col, n in zip(columns, counts)], axis=1
    )


def static(values):
    row = jnp.zeros((len(values),), jnp.int32)
    for i, value in enumerate(values):
        row = jnp.where(jnp.arange(len(values), dtype=jnp.int32) == i, value, row)
    return row


def tap_columns(edges, ends, block_of, x, c):
    k = iota((TAPS, 1, 1), 0)
    dy, dx = k // 3 - 1, k % 3 - 1
    edges, ends = edges[None], ends[None]
    down = jnp.where(edges == 0, dy, jnp.where(edges == 2, -dy, jnp.where(edges == 3, dx, -dx)))
    along = jnp.where(edges % 2 == 0, dx, dy)
    along = jnp.where(ends == 1, -along, along)
    return x + along, c + down


def selections(neighbor, edge_of, reverse, tile, part):
    tables = (neighbor, edge_of, reverse)
    own = tile * 4 + jnp.arange(4, dtype=jnp.int32)
    nbr, edge, flip = lookup(neighbor, own), lookup(edge_of, own), lookup(reverse, own)
    tiles = neighbor.shape[0]
    row = jnp.arange(SHARE, dtype=jnp.int32)
    share = rim_cell(row // EDGE, row // PART % DEPTH, part * PART + row % PART)
    rim = onehot(share, CELLS)
    fan = jnp.arange(FANS, dtype=jnp.int32)
    chain = [(lookup(nbr, fan // 2), lookup(edge, fan // 2), fan % 2)]
    for j in range(1, DEPTH):
        chain.append(walk(tables, *chain[-1]))
    around, edges, ends = zip(*chain[1:])
    strips = lookup(nbr, row // EDGE) * SHARE + lookup(edge, row // EDGE) * EDGE + row % EDGE
    counts = [len(block) for block in BLOCKS]
    x = static([cell[0] for block in BLOCKS for cell in block])
    c = static([cell[1] for block in BLOCKS for cell in block])
    place = jnp.where(spread(ends, counts) == 1, SIDE - 1 - x, x)
    cells = spread(around, counts) * SHARE + spread(edges, counts) * EDGE + c * PART + place % PART
    cells = jnp.where(place // PART == part, cells, -1)
    pick = onehot(jnp.concatenate([strips, cells.reshape(-1)]), tiles * SHARE)
    d, place = row // SIDE, row % SIDE
    end = jnp.where(place == 0, 0, jnp.where(place == SIDE - 1, 1, -1))
    beyond = []
    for slots, stride, rows in ((SLOTS, 3, 4), (8, 2, 3), (2, 1, 2)):
        target = (d * 2 + end)[None] * slots + stride * jnp.arange(rows, dtype=jnp.int32)[:, None]
        target = jnp.where(end[None] < 0, -1, target)
        beyond.append(onehot(target.reshape(-1), FANS * slots))
    fan3 = iota((1, FANS, 1), 1)
    at_end = fan3 // 2 * SIDE + fan3 % 2 * (SIDE - 1)
    x = static([0, 0, 1, 1, 2, 2, 0, 1])
    c = static([0, 1, 0, 1, 0, 1, 0, 0])
    near = jnp.arange(8, dtype=jnp.int32) < 6
    x, c = tap_columns(spread(edges[:2], (6, 2)), spread(ends[:2], (6, 2)), near, x, c)
    base = DEPTH * RING + fan3 * SLOTS
    first = jnp.where(
        c < 0,
        jnp.where(near, x * RING + at_end, base + x),
        jnp.where(
            x < 0,
            jnp.where(near, base + 12 + 2 * c, base + 18 + c),
            jnp.where(near, base + 3 * x + c, base + 12 + 2 * x + c),
        ),
    )
    first = onehot(jnp.where((c < 0) & (x < 0), -1, first).reshape(-1), DEPTH * RING + FANS * SLOTS)
    x, c = tap_columns(spread(edges[:1], (2,)), spread(ends[:1], (2,)), None, static([0, 1]), static([0, 0]))
    base = (DEPTH - 1) * RING + fan3 * 8
    second = jnp.where(c < 0, x * RING + at_end, jnp.where(x < 0, base + 6 + c, base + 2 * x + c))
    second = onehot(jnp.where((c < 0) & (x < 0), -1, second).reshape(-1), (DEPTH - 1) * RING + FANS * 8)
    turned = jnp.where(lookup(flip, d) == 1, SIDE - 1 - place, place)
    facing = onehot(rim_cell(d, 0, turned), CELLS)
    turn = onehot(d * SIDE + turned, RING)
    return edge, rim, pick, (*beyond, first, second, facing, turn)


def sigmoid(value):
    return 1.0 / (1.0 + jnp.exp(-value))


def fill_patches(state, padded, patches):
    padded[1 : SIDE + 1, 8 : SIDE + 8, :] = (
        state[0:CELLS, :].astype(jnp.float32).reshape(SIDE, SIDE, C)
    )
    halo = state[CELLS : CELLS + RING, :].astype(jnp.float32)
    empty = jnp.zeros((8, C), jnp.float32)
    for row, first in ((0, 0), (SIDE + 1, 2 * SIDE)):
        padded[row, 0:8, :] = empty
        padded[row, 8 : SIDE + 8, :] = halo[first : first + SIDE]
        padded[row, SIDE + 8 : SIDE + 16, :] = empty
    padded[1 : SIDE + 1, SIDE + 8, :] = halo[SIDE : 2 * SIDE]
    padded[1 : SIDE + 1, 7, :] = halo[3 * SIDE : 4 * SIDE]
    for dx in range(3):
        shifted = padded[:, 7 + dx : 7 + dx + SIDE, :].astype(jnp.bfloat16)
        shifted = shifted.reshape((SIDE + 2) * SIDE, C)
        for dy in range(3):
            k = dy * 3 + dx
            patches[:, k * C : (k + 1) * C] = shifted[dy * SIDE : dy * SIDE + CELLS]


def next_state(state, pre_act):
    return (state + pre_act * sigmoid(pre_act)).astype(jnp.bfloat16)


def dot(a, b):
    return jnp.dot(a, b, preferred_element_type=jnp.float32)


def update_strips(edge, level, strips, ends, mine, weights, side_patches):
    rows = len(strips) - 1
    place = iota((RING, C), 0) % SIDE
    moved = []
    for cells, beyond in [(mine, jnp.zeros_like(mine))] + list(zip(strips, ends)):
        below = jnp.where(place == 0, beyond, pltpu.roll(cells, 1, 0))
        above = jnp.where(place == SIDE - 1, beyond, pltpu.roll(cells, RING - 1, 0))
        moved.append([v.astype(jnp.bfloat16) for v in (below, cells, above)])
    for d in range(4):
        e = edge[d]
        for a in range(3):
            across = jnp.where((e == 0) | (e == 3), a, 2 - a)
            for b in range(3):
                tap = jnp.where(e % 2 == 0, 3 * across + b, 3 * b + across)
                lanes = pl.ds(pl.multiple_of(tap * C, C), C)
                for r in range(rows):
                    first = r * RING + d * SIDE
                    side_patches[first : first + SIDE, lanes] = moved[r + a][b][d * SIDE : (d + 1) * SIDE]
    before = jnp.concatenate(strips[:rows], axis=0)
    after = next_state(before, dot(side_patches[0 : rows * RING, :], weights)).astype(jnp.float32)
    return [after[r * RING : (r + 1) * RING] for r in range(rows)]


def update_fans(taps, strips, fans, weights):
    pool = jnp.concatenate([v.astype(jnp.bfloat16) for v in strips + [fans]], axis=0)
    found = dot(taps[...], pool)
    n = found.shape[0] // TAPS
    parts = [found[k * n : (k + 1) * n] for k in range(TAPS)]
    side = jnp.concatenate([v.astype(jnp.bfloat16) for v in parts], axis=1)
    return next_state(parts[4], dot(side, weights)).astype(jnp.float32)


def round_kernel(step, last, *refs):
    index, edge, start, gathered, all_weights, rim, e0, e1, e2, taps1, taps2, facing, turn = refs[:13]
    refs = refs[13 + (2 if step else 0) :]
    (kept, sent), refs = refs[:2], refs[2:]
    if not last:
        (out, share), refs = refs[:2], refs[2:]
    states, padded, patches, side_patches, weights, weight_sems, sems = refs
    loads = [
        pltpu.make_async_copy(all_weights.at[step * DEPTH + i], weights.at[i], weight_sems.at[i])
        for i in range(DEPTH)
    ]
    for load in loads:
        load.start()
    states[0, 0:CELLS, :] = start[...]
    cells = gathered[...].astype(jnp.float32)
    strips = [
        jnp.concatenate(
            [
                cells[q * PICK + d * EDGE + r * PART : q * PICK + d * EDGE + (r + 1) * PART]
                for d in range(4)
                for q in range(SPLIT)
            ],
            axis=0,
        )
        for r in range(DEPTH)
    ]
    fans = cells[SHARE:PICK]
    for q in range(1, SPLIT):
        fans = fans + cells[q * PICK + SHARE : (q + 1) * PICK]

    def deliver(i, act):
        for slot, target in ((0, kept), (1, sent)):

            @pl.when(index[slot] == step * DEPTH + i)
            def _():
                act(pltpu.make_async_copy(states.at[i], target, sems.at[slot]))

    for i in range(DEPTH):
        state = states.at[i]
        state[CELLS : CELLS + RING, :] = dot(turn[...], strips[0].astype(jnp.bfloat16)).astype(jnp.bfloat16)
        deliver(i, lambda copy: copy.start())
        tile = state[0:CELLS, :]
        if not (last and i == DEPTH - 1):
            fill_patches(state, padded, patches)
        loads[i].wait()
        if i < DEPTH - 1:
            ends = dot((e0, e1, e2)[i][...], fans.astype(jnp.bfloat16))
            ends = [ends[r * RING : (r + 1) * RING] for r in range(DEPTH - i)]
            mine = dot(facing[...], tile)
            moved = update_strips(edge, i, strips, ends, mine, weights[i], side_patches)
            if i < DEPTH - 2:
                fans = update_fans((taps1, taps2)[i], strips, fans, weights[i])
            strips = moved
        if not (last and i == DEPTH - 1):
            new = next_state(tile.astype(jnp.float32), dot(patches[...], weights[i]))
            if i < DEPTH - 1:
                states[i + 1, 0:CELLS, :] = new
            else:
                out[...] = new
                share[...] = dot(rim[...], new).astype(jnp.bfloat16)
    for i in range(DEPTH):
        deliver(i, lambda copy: copy.wait())


def four_sections(step, index, edge, start, gathered, weights, rim, maps, chosen):
    last = step == 1
    vmem = pl.BlockSpec(memory_space=pltpu.VMEM)
    smem = pl.BlockSpec(memory_space=pltpu.SMEM)
    hbm = pl.BlockSpec(memory_space=pl.ANY)
    bf16 = jnp.bfloat16
    state = jax.ShapeDtypeStruct((CELLS + RING, C), bf16)
    outs = [state, state]
    if not last:
        outs += [jax.ShapeDtypeStruct((CELLS, C), bf16), jax.ShapeDtypeStruct((SHARE, C), bf16)]
    return pl.pallas_call(
        lambda *refs: round_kernel(step, last, *refs),
        out_shape=outs,
        in_specs=[smem] * 2 + [vmem] * 2 + [hbm] + [vmem] * 8 + [hbm] * len(chosen),
        out_specs=[hbm] * 2 + [vmem] * (len(outs) - 2),
        scratch_shapes=[
            pltpu.VMEM((DEPTH, CELLS + RING, C), bf16),
            pltpu.VMEM((SIDE + 2, SIDE + 16, C), jnp.float32),
            pltpu.VMEM((CELLS, TAPS * C), bf16),
            pltpu.VMEM(((DEPTH - 1) * RING, TAPS * C), bf16),
            pltpu.VMEM((DEPTH, TAPS * C, C), bf16),
            pltpu.SemaphoreType.DMA((DEPTH,)),
            pltpu.SemaphoreType.DMA((2,)),
        ],
        input_output_aliases={13 + i: i for i in range(len(chosen))},
        compiler_params=pltpu.CompilerParams(vmem_limit_bytes=VMEM_BYTES),
        cost_estimate=pl.CostEstimate(
            flops=2 * DEPTH * CELLS * TAPS * C * C, bytes_accessed=6 << 20, transcendentals=DEPTH * CELLS * C
        ),
        name="four_sections",
    )(index, edge, start, gathered, weights, rim, *maps, *chosen)


def gradient_kernel(state, cotangent, weights, before, level, term, padded, patches):
    fill_patches(state, padded, patches)
    pre_act = dot(patches[...], weights[...])
    gate = sigmoid(pre_act)
    level[...] = (state[0:CELLS, :].astype(jnp.float32) + pre_act * gate).astype(jnp.bfloat16)
    slope = gate * (1.0 + pre_act * (1.0 - gate))
    delta = (cotangent[...].astype(jnp.float32) * slope).astype(jnp.bfloat16)
    added = lax.dot_general(
        patches[...], delta, (((0,), (0,)), ((), ())), preferred_element_type=jnp.float32
    )
    term[...] = (before[...] + added).astype(term.dtype)


def gradient(state, cotangent, weights, before, dtype):
    vmem = pl.BlockSpec(memory_space=pltpu.VMEM)
    return pl.pallas_call(
        gradient_kernel,
        out_shape=(
            jax.ShapeDtypeStruct((CELLS, C), jnp.bfloat16),
            jax.ShapeDtypeStruct((TAPS * C, C), dtype),
        ),
        in_specs=[vmem] * 4,
        out_specs=(vmem,) * 2,
        scratch_shapes=[
            pltpu.VMEM((SIDE + 2, SIDE + 16, C), jnp.float32),
            pltpu.VMEM((CELLS, TAPS * C), jnp.bfloat16),
        ],
        compiler_params=pltpu.CompilerParams(vmem_limit_bytes=VMEM_BYTES),
        cost_estimate=pl.CostEstimate(
            flops=2 * 2 * CELLS * TAPS * C * C, bytes_accessed=3 << 20, transcendentals=CELLS * C
        ),
        name="gradient",
    )(state, cotangent, weights, before)


def share_out(block, axis, groups=None):
    count = lax.axis_size(axis) if groups is None else len(groups[0])
    return lax.all_to_all(
        jnp.broadcast_to(block[None], (count,) + block.shape), axis, 0, 0, axis_index_groups=groups
    )


def sum_terms(term):
    axes = ("dp", "tile")
    count = lax.axis_size(axes)
    rows = term.shape[0] // count
    pieces = lax.all_to_all(term.reshape(count, rows, term.shape[1]), axes, 0, 0)
    piece = jnp.sum(pieces.astype(jnp.float32), axis=0).astype(jnp.bfloat16)
    return share_out(piece, axes).reshape(term.shape).astype(jnp.float32)


def local(inputs, neighbor, edge_of, reverse, weights, cotangent):
    segment = lax.axis_index("segment")
    sample, part = segment // SPLIT, segment % SPLIT
    partner = segment ^ SPLIT
    teams = [[t * SPLIT + p for p in range(SPLIT)] for t in range(2)]
    kernels = lax.all_gather(weights, "segment", axis=0, tiled=True)
    edge, rim, pick, maps = selections(neighbor, edge_of, reverse, lax.axis_index("tile"), part)
    index = jnp.stack([segment, partner]).astype(jnp.int32)
    state = lax.dynamic_index_in_dim(inputs[:, 0], sample, 0, False).reshape(CELLS, C)
    share = dot(rim, state).astype(jnp.bfloat16)
    chosen = ()
    for step in range(2):
        rims = share_out(share, "tile").reshape(-1, C)
        picked = dot(pick, rims).astype(jnp.bfloat16)
        gathered = lax.all_gather(picked, "segment", axis=0, tiled=True, axis_index_groups=teams)
        kept, sent, *more = four_sections(step, index, edge, state, gathered, kernels, rim, maps, chosen)
        chosen = (kept, sent)
        if more:
            state, share = more
    other = lax.ppermute(sent, "segment", [(s, s ^ SPLIT) for s in range(8)])
    cotans = cotangent[0, :, 0].reshape(2, CELLS, C)
    mine = lax.dynamic_index_in_dim(cotans, sample, 0, False)
    theirs = lax.dynamic_index_in_dim(cotans, 1 - sample, 0, False)
    zero = jnp.zeros((TAPS * C, C), jnp.float32)
    level_mine, term = gradient(kept, mine, weights[0], zero, jnp.float32)
    level_other, term = gradient(other, theirs, weights[0], term, jnp.bfloat16)
    total = sum_terms(term)
    low = jnp.where(sample == 0, level_mine, level_other)
    high = jnp.where(sample == 0, level_other, level_mine)
    levels = jnp.stack([low, high]).reshape(1, 2, 1, SIDE, SIDE, C)
    return levels, total[None]


def solution(mesh):
    placed = (
        P("dp", "tile", None, None, None),
        P(),
        P(),
        P(),
        P("segment", None, None),
        P("segment", "dp", "tile", None, None, None),
    )
    return jax.shard_map(
        local,
        mesh=mesh,
        in_specs=placed,
        out_specs=(P("segment", "dp", "tile", None, None, None), P("segment", None, None)),
        check_vma=False,
    )
```

time: 265 us -> 193 us (0.73)
  the two profiles are of different devices: /device:TPU:4 before, /device:TPU:2 now
where the time goes in v3:
time: 193 us
  blocking collectives  72.1 us (37%)
  waiting for transfers between devices  39.6 us (21%)
  Pallas kernels  23.5 us (12%)
  starting transfers between devices  22.6 us (12%)
  between operations  14.7 us (8%)
  local copies, waits for them, and re-layouts  13.5 us (7%)
  other arithmetic  3.88 us (2%)
  matrix products  3.16 us (2%)
    all_to_all x1, blocking collectives, share_out(): lax.all_to_all(jnp.broadcast_to(block[None], (count,) + block.shape), axi...  35.4 us
    all_to_all x2, waiting for transfers between devices, share_out(): lax.all_to_all(jnp.broadcast_to(block[None], (count,) + block.shape), axi...  32.8 us
    all_to_all x1, blocking collectives, sum_terms(): lax.all_to_all(term.reshape(count, rows, term.shape[1]), axes, 0, 0)  24.9 us
    all_to_all x2, starting transfers between devices, share_out(): lax.all_to_all(jnp.broadcast_to(block[None], (count,) + block.shape), axi...  18.8 us
    pallas_call x2, Pallas kernels, four_sections(): pl.pallas_call(lambda *refs: round_kernel(step, last, *refs), out_shape=o...  18.6 us
    all_gather x2, blocking collectives, local(): lax.all_gather(picked, 'segment', axis=0, tiled=True, axis_index_groups=t...  11.8 us
    ppermute x1, waiting for transfers between devices, local(): other = lax.ppermute(sent, 'segment', [(s, s ^ SPLIT) for s in range(8)])  6.09 us
    pallas_call x2, Pallas kernels, gradient(): pl.pallas_call(gradient_kernel, out_shape=(jax.ShapeDtypeStruct((CELLS, C...  4.86 us
  transfers between devices with their start and end apart: 4, of which 3 were waited for; matrix products, arithmetic and copies ran while one was open for 7% of the time, Pallas kernels for 1%

profile of v3, /device:TPU:2, one launch (start us, length us, event | category | flops | bytes accessed | tf_op | source)
XLA Modules:
  0.0 193.0 jit_solution(16217907907458344815)
XLA Ops:
  7.2 1.0 copy-done
  8.5 1.2 broadcast_in_dim.601
  9.8 13.9 %all-to-all-start = ((bf16[32,128,128]{2,1,0:T(8,128)(2,1)}), bf16[32,128,128]{2,1,0:T(8,128)(2,1)}, u32[]{:S(2)}, u32[]{:S(2)}) async-start(bf16[32,128,128]{2,1,0:T(8,128)(2,1)} %broadcast_in_dim.601), calls=%async_computation | async-start | bytes 2097152 | tf_op jit(solution)/shard_map/all_to_all | solution.py:336
  23.7 0.7 all-gather.2.cloned.1.call-update
  34.1 17.1 %all-to-all-done = bf16[32,128,128]{2,1,0:T(8,128)(2,1)} async-done(((bf16[32,128,128]{2,1,0:T(8,128)(2,1)}), bf16[32,128,128]{2,1,0:T(8,128)(2,1)}, u32[]{:S(2)}, u32[]{:S(2)}) %all-to-all-start) | async-done | bytes 1048608 | tf_op jit(solution)/shard_map/all_to_all | solution.py:336
  51.2 2.1 %fusion.5 = bf16[288,128]{1,0:T(8,128)(2,1)S(1)} fusion(bf16[4096,128]{1,0:T(8,128)(2,1)} %bitcast.3, s32[288]{0:T(512)S(1)} %pad_add_fusion.1), kind=kOutput, calls=%fused_computation.7 | convolution fusion | flops 303206400 | bytes 1123456 | tf_op jit(solution)/shard_map/dot_general | solution.py:167
  53.3 5.9 %all_gather.9.refs_3_ = bf16[1152,128]{1,0:T(8,128)(2,1)S(1)} all-gather(bf16[288,128]{1,0:T(8,128)(2,1)S(1)} %fusion.5), channel_id=1, replica_groups={{0,32,64,96},{128,160,192,224},{1,33,65,97},{129,161,193,225},{2,34,66,..., dimensions={0}, use_global_device_ids=true | all-gather | bytes 368640 | tf_op jit(solution)/shard_map/all_gather | solution.py:364
  59.2 1.7 copy-done.1
  60.9 10.5 %four_sections.2 = (bf16[1152,128]{1,0:T(8,128)(2,1)S(1)}, bf16[1152,128]{1,0:T(8,128)(2,1)}, bf16[1024,128]{1,0:T(8,128)(2,1)S(1)}, bf16[128,128]{1,0:T(8,128)(2,1)S(1)}) custom-call(s32[2]{0:T(128)S(1)} %pad_add_fusion.2.refs_0_, s32[4]{0:T(128)S(1)} %get-tuple-element.27.refs_1_, bf16[1024,128]{1,0:T(8,128)(2,1)S(1)} %bitcast.23, ...), custom_call_target="tpu_custom_call" | custom-call | flops 1207959552 | bytes 6291456 | tf_op jit(solution)/shard_map/four_sections/pallas_call | solution.py:276
  71.6 35.4 %all_to_all.20 = bf16[32,128,128]{2,1,0:T(8,128)(2,1)S(1)} all-to-all(bf16[32,128,128]{2,1,0:T(8,128)(2,1)S(1)} %broadcast_in_dim.651), channel_id=1, replica_groups=mesh['dp'=2,'segment'=8,'tile'=32] {'tile'}, dimensions={0} | all-to-all | bytes 2097152 | tf_op jit(solution)/shard_map/all_to_all | solution.py:336
  107.0 0.8 fusion.6
  107.9 5.9 %all_gather.11.refs_3_ = bf16[1152,128]{1,0:T(8,128)(2,1)S(1)} all-gather(bf16[288,128]{1,0:T(8,128)(2,1)S(1)} %fusion.6), channel_id=1, replica_groups={{0,32,64,96},{128,160,192,224},{1,33,65,97},{129,161,193,225},{2,34,66,..., dimensions={0}, use_global_device_ids=true | all-gather | bytes 368640 | tf_op jit(solution)/shard_map/all_gather | solution.py:364
  113.7 8.2 %four_sections.3 = (bf16[1152,128]{1,0:T(8,128)(2,1)S(1)}, bf16[1152,128]{1,0:T(8,128)(2,1)}) custom-call(s32[2]{0:T(128)S(1)} %pad_add_fusion.2.refs_0_, s32[4]{0:T(128)S(1)} %get-tuple-element.27.refs_1_, bf16[1024,128]{1,0:T(8,128)(2,1)S(1)} %get-tuple-element.12.refs_2_, ...), custom_call_target="tpu_custom_call", output_to_operand_aliasing={{0}: (13, {}), {1}: (14, {})} | custom-call | flops 1207959552 | bytes 6291456 | tf_op jit(solution)/shard_map/four_sections/pallas_call | solution.py:276
  121.9 3.8 %collective-permute-start = (bf16[1152,128]{1,0:T(8,128)(2,1)}, bf16[1152,128]{1,0:T(8,128)(2,1)S(1)}, u32[]{:S(2)}, u32[]{:S(2)}) collective-permute-start(bf16[1152,128]{1,0:T(8,128)(2,1)} %get-tuple-element.18), channel_id=1, source_target_pairs={{0,128},{32,160},{64,192},{96,224},{128,0},{160,32},{192,64},{224,... | collective-permute-start | bytes 884744 | tf_op jit(solution)/shard_map/ppermute | solution.py:369
  125.7 1.1 dynamic-slice_bitcast_fusion.1
  126.8 2.4 %gradient.2 = (bf16[1024,128]{1,0:T(8,128)(2,1)S(1)}, f32[1152,128]{1,0:T(8,128)S(1)}) custom-call(bf16[1152,128]{1,0:T(8,128)(2,1)S(1)} %get-tuple-element.16.state, bf16[1024,128]{1,0:T(8,128)(2,1)S(1)} %get-tuple-element.47.cotangent, bf16[1152,128]{1,0:T(8,128)(2,1)S(1)} %bitcast.24, f32[1152,128]{1,0:T(8,128)S(1)} %broadcast_in_dim.652.before), custom_call_target="tpu_custom_call" | custom-call | flops 603979776 | bytes 3145728 | tf_op jit(solution)/shard_map/gradient/pallas_call | solution.py:314
  129.2 6.1 %collective-permute-done.state = bf16[1152,128]{1,0:T(8,128)(2,1)S(1)} collective-permute-done((bf16[1152,128]{1,0:T(8,128)(2,1)}, bf16[1152,128]{1,0:T(8,128)(2,1)S(1)}, u32[]{:S(2)}, u32[]{:S(2)}) %collective-permute-start) | collective-permute-done | bytes 294944 | tf_op jit(solution)/shard_map/ppermute | solution.py:369
  135.3 2.4 %gradient.3 = (bf16[1024,128]{1,0:T(8,128)(2,1)S(1)}, bf16[1152,128]{1,0:T(8,128)(2,1)S(1)}) custom-call(bf16[1152,128]{1,0:T(8,128)(2,1)S(1)} %collective-permute-done.state, bf16[1024,128]{1,0:T(8,128)(2,1)S(1)} %get-tuple-element.48.cotangent, bf16[1152,128]{1,0:T(8,128)(2,1)S(1)} %bitcast.25, f32[1152,128]{1,0:T(8,128)S(1)} %get-tuple-element.19.before), custom_call_target="tpu_custom_call" | custom-call | flops 603979776 | bytes 3145728 | tf_op jit(solution)/shard_map/gradient/pallas_call | solution.py:314
  137.9 24.9 %all_to_all.21 = bf16[64,18,128]{2,1,0:T(8,128)(2,1)S(1)} all-to-all(bf16[64,18,128]{2,1,0:T(8,128)(2,1)S(1)} %reshape.1183), channel_id=1, replica_groups=mesh['dp'=2,'segment'=8,'tile'=32] {'dp','tile'}, dimensions={0} | all-to-all | bytes 589824 | tf_op jit(solution)/shard_map/all_to_all | solution.py:345
  162.9 0.8 broadcast_in_dim.653
  163.7 4.9 %all-to-all-start.3 = ((bf16[64,18,128]{2,1,0:T(8,128)(2,1)}), bf16[64,18,128]{2,1,0:T(8,128)(2,1)S(1)}, u32[]{:S(2)}, u32[]{:S(2)}) async-start(bf16[64,18,128]{2,1,0:T(8,128)(2,1)} %broadcast_in_dim.653), calls=%async_computation.3 | async-start | bytes 786432 | tf_op jit(solution)/shard_map/all_to_all | solution.py:336
  168.7 0.8 pad_maximum_fusion
  169.5 15.7 %all-to-all-done.3 = bf16[64,18,128]{2,1,0:T(8,128)(2,1)S(1)} async-done(((bf16[64,18,128]{2,1,0:T(8,128)(2,1)}), bf16[64,18,128]{2,1,0:T(8,128)(2,1)S(1)}, u32[]{:S(2)}, u32[]{:S(2)}) %all-to-all-start.3) | async-done | bytes 294944 | tf_op jit(solution)/shard_map/all_to_all | solution.py:336
  185.2 0.9 reshape.1184
  (155 shorter events, 10.2 us)
Async XLA Ops:
  7.2 1.0 copy-start
  8.5 16.1 %copy-start.4 = (s32[32,4]{0,1:T(4,128)S(1)}, s32[32,4]{0,1:T(4,128)}, u32[]{:S(2)}) copy-start(s32[32,4]{0,1:T(4,128)} %param.8) | copy-start | bytes 1540
  8.5 16.3 %copy-start.5 = (s32[32,4]{0,1:T(4,128)S(1)}, s32[32,4]{0,1:T(4,128)}, u32[]{:S(2)}) copy-start(s32[32,4]{0,1:T(4,128)} %param.7) | copy-start | bytes 1540
  8.5 16.5 %copy-start.6 = (s32[32,4]{0,1:T(4,128)S(1)}, s32[32,4]{0,1:T(4,128)}, u32[]{:S(2)}) copy-start(s32[32,4]{0,1:T(4,128)} %param.9) | copy-start | bytes 1540
  9.8 41.5 %all-to-all-start = ((bf16[32,128,128]{2,1,0:T(8,128)(2,1)}), bf16[32,128,128]{2,1,0:T(8,128)(2,1)}, u32[]{:S(2)}, u32[]{:S(2)}) async-start(bf16[32,128,128]{2,1,0:T(8,128)(2,1)} %broadcast_in_dim.601), calls=%async_computation | async-start | bytes 2097152 | tf_op jit(solution)/shard_map/all_to_all | solution.py:336
  23.7 35.5 %all-gather.2.cloned.1.call-start = ((), (), s32[]{:S(2)}) async-start(), calls=%async_computation.4 | async-start | bytes 2654208 | tf_op jit(solution)/shard_map/all_gather | solution.py:355
  59.2 1.7 copy-start.1
  107.0 6.7 %copy-start.2 = (bf16[8,1152,128]{2,1,0:T(8,128)(2,1)S(1)}, bf16[8,1152,128]{2,1,0:T(8,128)(2,1)}, u32[]{:S(2)}) copy-start(bf16[8,1152,128]{2,1,0:T(8,128)(2,1)} %all-gather.2.cloned.1.call-done.refs_4_) | copy-start | bytes 7077892
  113.7 13.1 %copy-start.3 = (bf16[1,1152,128]{2,1,0:T(8,128)(2,1)S(1)}, bf16[1,1152,128]{2,1,0:T(8,128)(2,1)}, u32[]{:S(2)}) copy-start(bf16[1,1152,128]{2,1,0:T(8,128)(2,1)} %param.10) | copy-start | bytes 884740
  121.9 13.4 %collective-permute-start = (bf16[1152,128]{1,0:T(8,128)(2,1)}, bf16[1152,128]{1,0:T(8,128)(2,1)S(1)}, u32[]{:S(2)}, u32[]{:S(2)}) collective-permute-start(bf16[1152,128]{1,0:T(8,128)(2,1)} %get-tuple-element.18), channel_id=1, source_target_pairs={{0,128},{32,160},{64,192},{96,224},{128,0},{160,32},{192,64},{224,... | collective-permute-start | bytes 884744 | tf_op jit(solution)/shard_map/ppermute | solution.py:369
  163.7 21.5 %all-to-all-start.3 = ((bf16[64,18,128]{2,1,0:T(8,128)(2,1)}), bf16[64,18,128]{2,1,0:T(8,128)(2,1)S(1)}, u32[]{:S(2)}, u32[]{:S(2)}) async-start(bf16[64,18,128]{2,1,0:T(8,128)(2,1)} %broadcast_in_dim.653), calls=%async_computation.3 | async-start | bytes 786432 | tf_op jit(solution)/shard_map/all_to_all | solution.py:336
Sparse Core Ops, SparseCore 0:
  26.6 28.5 all-gather.1

commit v4 on v3

--- a/solution.py
+++ b/solution.py
@@ -30,10 +30,10 @@
     return (target[:, None] == iota((target.shape[0], columns), 1)).astype(jnp.bfloat16)
 
 
-def lookup(table, index):
-    flat = table.reshape(-1)
-    hit = index[..., None] == jnp.arange(flat.shape[0], dtype=jnp.int32)
-    return jnp.sum(jnp.where(hit, flat, 0), axis=-1)
+def lookup(seams, slot):
+    hit = slot[..., None] == jnp.arange(seams.shape[0], dtype=jnp.int32)
+    found = jnp.sum(jnp.where(hit, seams, 0), axis=-1)
+    return found // 8, found // 2 % 4, found % 2
 
 
 def rim_cell(edge, depth, place):
@@ -49,17 +49,15 @@
     )
 
 
-def walk(tables, tile, edge, end):
-    neighbor, edge_of, reverse = tables
-    slot = tile * 4 + jnp.where(edge % 2 == 0, 3 - 2 * end, 2 * end)
+def walk(seams, tile, edge, end):
     corner = jnp.where((edge == 0) | (edge == 3), 0, 1)
-    corner = jnp.where(lookup(reverse, slot) == 1, 1 - corner, corner)
-    return lookup(neighbor, slot), lookup(edge_of, slot), corner
+    tile, edge, flip = lookup(seams, tile * 4 + jnp.where(edge % 2 == 0, 3 - 2 * end, 2 * end))
+    return tile, edge, jnp.where(flip == 1, 1 - corner, corner)
 
 
 def spread(columns, counts):
     return jnp.concatenate(
-        [jnp.broadcast_to(col[:, None], (FANS, n)) for col, n in zip(columns, counts)], axis=1
+        [jnp.broadcast_to(col[..., None], col.shape + (n,)) for col, n in zip(columns, counts)], axis=-1
     )
 
 
@@ -80,27 +78,34 @@
     return x + along, c + down
 
 
-def selections(neighbor, edge_of, reverse, tile, part):
-    tables = (neighbor, edge_of, reverse)
-    own = tile * 4 + jnp.arange(4, dtype=jnp.int32)
-    nbr, edge, flip = lookup(neighbor, own), lookup(edge_of, own), lookup(reverse, own)
-    tiles = neighbor.shape[0]
+def selections(neighbor, edge_of, reverse, tile, part, columns):
+    seams = (neighbor * 8 + edge_of * 2 + reverse).reshape(-1)
     row = jnp.arange(SHARE, dtype=jnp.int32)
     share = rim_cell(row // EDGE, row // PART % DEPTH, part * PART + row % PART)
     rim = onehot(share, CELLS)
+    targets = jnp.arange(neighbor.shape[0] // columns, dtype=jnp.int32)[:, None] * columns + tile % columns
     fan = jnp.arange(FANS, dtype=jnp.int32)
-    chain = [(lookup(nbr, fan // 2), lookup(edge, fan // 2), fan % 2)]
+    nbr, edge, flip = lookup(seams, targets * 4 + fan // 2)
+    chain = [(nbr, edge, jnp.broadcast_to(fan % 2, nbr.shape))]
     for j in range(1, DEPTH):
-        chain.append(walk(tables, *chain[-1]))
+        chain.append(walk(seams, *chain[-1]))
     around, edges, ends = zip(*chain[1:])
-    strips = lookup(nbr, row // EDGE) * SHARE + lookup(edge, row // EDGE) * EDGE + row % EDGE
     counts = [len(block) for block in BLOCKS]
     x = static([cell[0] for block in BLOCKS for cell in block])
     c = static([cell[1] for block in BLOCKS for cell in block])
-    place = jnp.where(spread(ends, counts) == 1, SIDE - 1 - x, x)
-    cells = spread(around, counts) * SHARE + spread(edges, counts) * EDGE + c * PART + place % PART
-    cells = jnp.where(place // PART == part, cells, -1)
-    pick = onehot(jnp.concatenate([strips, cells.reshape(-1)]), tiles * SHARE)
+    along = jnp.where(spread(ends, counts) == 1, SIDE - 1 - x, x)
+    inner = spread(edges, counts) * EDGE + c * PART + along % PART
+    inner = jnp.where(along // PART == part, inner, -SHARE * columns)
+    strip = [nbr[:, 0::2], edge[:, 0::2]]
+    strip = [jnp.concatenate([jnp.broadcast_to(v[:, d : d + 1], (v.shape[0], EDGE)) for d in range(4)], 1) for v in strip]
+    source = jnp.concatenate([strip[0], spread(around, counts).reshape(-1, FANS * SLOTS)], axis=1)
+    place = jnp.concatenate([strip[1] * EDGE + row % EDGE, inner.reshape(-1, FANS * SLOTS)], axis=1)
+    place = jnp.where(source // columns == tile // columns, source % columns * SHARE + place, -1)
+    pick = onehot(place.reshape(-1), columns * SHARE)
+    mine = (targets == tile).astype(jnp.int32)
+    edge, flip = jnp.sum(edge * mine, axis=0)[0::2], jnp.sum(flip * mine, axis=0)[0::2]
+    edges = [jnp.sum(v * mine, axis=0) for v in edges]
+    ends = [jnp.sum(v * mine, axis=0) for v in ends]
     d, place = row // SIDE, row % SIDE
     end = jnp.where(place == 0, 0, jnp.where(place == SIDE - 1, 1, -1))
     beyond = []
@@ -129,7 +134,8 @@
     base = (DEPTH - 1) * RING + fan3 * 8
     second = jnp.where(c < 0, x * RING + at_end, jnp.where(x < 0, base + 6 + c, base + 2 * x + c))
     second = onehot(jnp.where((c < 0) & (x < 0), -1, second).reshape(-1), (DEPTH - 1) * RING + FANS * 8)
-    turned = jnp.where(lookup(flip, d) == 1, SIDE - 1 - place, place)
+    flip = jnp.concatenate([jnp.broadcast_to(flip[k : k + 1], (SIDE,)) for k in range(4)])
+    turned = jnp.where(flip == 1, SIDE - 1 - place, place)
     facing = onehot(rim_cell(d, 0, turned), CELLS)
     turn = onehot(d * SIDE + turned, RING)
     return edge, rim, pick, (*beyond, first, second, facing, turn)
@@ -276,7 +282,7 @@
     return pl.pallas_call(
         lambda *refs: round_kernel(step, last, *refs),
         out_shape=outs,
-        in_specs=[smem] * 2 + [vmem] * 2 + [hbm] + [vmem] * 8 + [hbm] * len(chosen),
+        in_specs=[smem] * 2 + [vmem] * 2 + [pl.BlockSpec(memory_space=pltpu.HBM)] + [vmem] * 8 + [hbm] * len(chosen),
         out_specs=[hbm] * 2 + [vmem] * (len(outs) - 2),
         scratch_shapes=[
             pltpu.VMEM((DEPTH, CELLS + RING, C), bf16),
@@ -339,12 +345,12 @@
 
 
 def sum_terms(term):
-    axes = ("dp", "tile")
-    count = lax.axis_size(axes)
+    count = lax.axis_size("tile")
     rows = term.shape[0] // count
-    pieces = lax.all_to_all(term.reshape(count, rows, term.shape[1]), axes, 0, 0)
+    pieces = lax.all_to_all(term.reshape(count, rows, term.shape[1]), "tile", 0, 0)
     piece = jnp.sum(pieces.astype(jnp.float32), axis=0).astype(jnp.bfloat16)
-    return share_out(piece, axes).reshape(term.shape).astype(jnp.float32)
+    pieces = share_out(piece, ("dp", "tile")).reshape((lax.axis_size("dp"),) + term.shape)
+    return jnp.sum(pieces.astype(jnp.float32), axis=0)
 
 
 def local(inputs, neighbor, edge_of, reverse, weights, cotangent):
@@ -353,14 +359,21 @@
     partner = segment ^ SPLIT
     teams = [[t * SPLIT + p for p in range(SPLIT)] for t in range(2)]
     kernels = lax.all_gather(weights, "segment", axis=0, tiled=True)
-    edge, rim, pick, maps = selections(neighbor, edge_of, reverse, lax.axis_index("tile"), part)
+    tiles = neighbor.shape[0]
+    rows = 4 if tiles % 8 == 0 else 2
+    columns = tiles // rows
+    along_row = [[r * columns + c for c in range(columns)] for r in range(rows)]
+    along_column = [[r * columns + c for r in range(rows)] for c in range(columns)]
+    edge, rim, pick, maps = selections(neighbor, edge_of, reverse, lax.axis_index("tile"), part, columns)
     index = jnp.stack([segment, partner]).astype(jnp.int32)
     state = lax.dynamic_index_in_dim(inputs[:, 0], sample, 0, False).reshape(CELLS, C)
     share = dot(rim, state).astype(jnp.bfloat16)
     chosen = ()
     for step in range(2):
-        rims = share_out(share, "tile").reshape(-1, C)
-        picked = dot(pick, rims).astype(jnp.bfloat16)
+        rims = share_out(share, "tile", along_row).reshape(-1, C)
+        picked = dot(pick, rims).astype(jnp.bfloat16).reshape(rows, PICK, C)
+        picked = lax.all_to_all(picked, "tile", 0, 0, axis_index_groups=along_column)
+        picked = jnp.sum(picked.astype(jnp.float32), axis=0).astype(jnp.bfloat16)
         gathered = lax.all_gather(picked, "segment", axis=0, tiled=True, axis_index_groups=teams)
         kept, sent, *more = four_sections(step, index, edge, state, gathered, kernels, rim, maps, chosen)
         chosen = (kept, sent)

time: 193 us -> 199 us (1.031)
  the two profiles are of different devices: /device:TPU:2 before, /device:TPU:18 now
where the time goes in v4:
time: 199 us; the launch traced here: 198 us
  blocking collectives  62.4 us (31%)
  waiting for transfers between devices  31.2 us (16%)
  starting transfers between devices  29.1 us (15%)
  local copies, waits for them, and re-layouts  27.2 us (14%)
  Pallas kernels  23.4 us (12%)
  between operations  14.9 us (7%)
  other arithmetic  6.79 us (3%)
  matrix products  2.89 us (1%)
    all_to_all x2, waiting for transfers between devices, share_out(): lax.all_to_all(jnp.broadcast_to(block[None], (count,) + block.shape), axi...  20.6 us
    all_to_all x1, blocking collectives, share_out(): lax.all_to_all(jnp.broadcast_to(block[None], (count,) + block.shape), axi...  19.8 us
    all_to_all x2, starting transfers between devices, share_out(): lax.all_to_all(jnp.broadcast_to(block[None], (count,) + block.shape), axi...  19.6 us
    pallas_call x2, Pallas kernels, four_sections(): pl.pallas_call(lambda *refs: round_kernel(step, last, *refs), out_shape=o...  18.6 us
    all_to_all x1, blocking collectives, sum_terms(): lax.all_to_all(term.reshape(count, rows, term.shape[1]), 'tile', 0, 0)  18 us
    unnamed x60, local copies, waits for them, and re-layouts  13 us
    all_gather x2, blocking collectives, local(): lax.all_gather(picked, 'segment', axis=0, tiled=True, axis_index_groups=t...  12.4 us
    all_to_all x1, blocking collectives, local(): lax.all_to_all(picked, 'tile', 0, 0, axis_index_groups=along_column)  12.2 us
  transfers between devices with their start and end apart: 5, of which 4 were waited for; matrix products, arithmetic and copies ran while one was open for 9% of the time, Pallas kernels for 1%

profile of v4, /device:TPU:18, one launch (start us, length us, event | category | flops | bytes accessed | tf_op | source)
XLA Modules:
  0.0 197.9 jit_solution(8259719400312930476)
XLA Ops:
  7.3 1.0 copy-done
  9.3 10.3 %all-to-all-start = ((bf16[8,128,128]{2,1,0:T(8,128)(2,1)}), bf16[8,128,128]{2,1,0:T(8,128)(2,1)S(1)}, u32[]{:S(2)}, u32[]{:S(2)}) async-start(bf16[8,128,128]{2,1,0:T(8,128)(2,1)} %broadcast_in_dim.634), calls=%async_computation | async-start | bytes 524288 | tf_op jit(solution)/shard_map/all_to_all | solution.py:342
  35.0 1.7 fusion.2
  36.6 5.2 %all-to-all-start.1 = ((bf16[4,288,128]{2,1,0:T(8,128)(2,1)}), bf16[4,288,128]{2,1,0:T(8,128)(2,1)S(1)}, u32[]{:S(2)}, u32[]{:S(2)}) async-start(bf16[4,288,128]{2,1,0:T(8,128)(2,1)} %bitcast.4), calls=%async_computation.1 | async-start | bytes 589824 | tf_op jit(solution)/shard_map/all_to_all | solution.py:375
  42.2 5.8 %all-to-all-done.1 = bf16[4,288,128]{2,1,0:T(8,128)(2,1)S(1)} async-done(((bf16[4,288,128]{2,1,0:T(8,128)(2,1)}), bf16[4,288,128]{2,1,0:T(8,128)(2,1)S(1)}, u32[]{:S(2)}, u32[]{:S(2)}) %all-to-all-start.1) | async-done | bytes 294944 | tf_op jit(solution)/shard_map/all_to_all | solution.py:375
  48.0 6.3 %all_gather.9.refs_3_ = bf16[1152,128]{1,0:T(8,128)(2,1)S(1)} all-gather(bf16[288,128]{1,0:T(8,128)(2,1)S(1)} %reduce_sum.140), channel_id=1, replica_groups={{0,32,64,96},{128,160,192,224},{1,33,65,97},{129,161,193,225},{2,34,66,..., dimensions={0}, use_global_device_ids=true | all-gather | bytes 368640 | tf_op jit(solution)/shard_map/all_gather | solution.py:377
  54.8 1.7 copy-done.1
  56.4 10.5 %four_sections.2 = (bf16[1152,128]{1,0:T(8,128)(2,1)S(1)}, bf16[1152,128]{1,0:T(8,128)(2,1)}, bf16[1024,128]{1,0:T(8,128)(2,1)S(1)}, bf16[128,128]{1,0:T(8,128)(2,1)S(1)}) custom-call(s32[2]{0:T(128)S(1)} %pad_add_fusion.3.refs_0_, s32[4]{0:T(128)S(1)} %slice.48.refs_1_, bf16[1024,128]{1,0:T(8,128)(2,1)S(1)} %bitcast.30, ...), custom_call_target="tpu_custom_call" | custom-call | flops 1207959552 | bytes 6291456 | tf_op jit(solution)/shard_map/four_sections/pallas_call | solution.py:282
  67.0 19.8 %all_to_all.30 = bf16[8,128,128]{2,1,0:T(8,128)(2,1)S(1)} all-to-all(bf16[8,128,128]{2,1,0:T(8,128)(2,1)S(1)} %broadcast_in_dim.690), channel_id=1, replica_groups={{0,1,2,3,4,5,6,7},{8,9,10,11,12,13,14,15},{16,17,18,19,20,21,22,23},{24..., dimensions={0} | all-to-all | bytes 524288 | tf_op jit(solution)/shard_map/all_to_all | solution.py:342
  87.8 12.2 %all_to_all.31 = bf16[4,288,128]{2,1,0:T(8,128)(2,1)} all-to-all(bf16[4,288,128]{2,1,0:T(8,128)(2,1)S(1)} %bitcast.37), channel_id=1, replica_groups={{0,8,16,24},{1,9,17,25},{2,10,18,26},{3,11,19,27},{4,12,20,28},{5,13,21..., dimensions={0} | all-to-all | bytes 589824 | tf_op jit(solution)/shard_map/all_to_all | solution.py:375
  100.0 1.6 reduce_sum.146
  101.6 6.1 %all_gather.11.refs_3_ = bf16[1152,128]{1,0:T(8,128)(2,1)S(1)} all-gather(bf16[288,128]{1,0:T(8,128)(2,1)} %reduce_sum.146), channel_id=1, replica_groups={{0,32,64,96},{128,160,192,224},{1,33,65,97},{129,161,193,225},{2,34,66,..., dimensions={0}, use_global_device_ids=true | all-gather | bytes 368640 | tf_op jit(solution)/shard_map/all_gather | solution.py:377
  107.7 1.2 copy-done.4
  112.3 1.0 copy-done.14
  115.4 8.2 %four_sections.3 = (bf16[1152,128]{1,0:T(8,128)(2,1)S(1)}, bf16[1152,128]{1,0:T(8,128)(2,1)}) custom-call(s32[2]{0:T(128)S(1)} %copy-done.22, s32[4]{0:T(128)S(1)} %copy-done.24, bf16[1024,128]{1,0:T(8,128)(2,1)S(1)} %copy-done.20, bf16[1152,128]{1,0:T(8,128)(2,1)S(1)} %all_gather.11.refs_3_, ...), custom_call_target="tpu_custom_call", output_to_operand_aliasing={{0}: (13, {}), {1}: (14, {})} | custom-call | flops 1207959552 | bytes 6291456 | tf_op jit(solution)/shard_map/four_sections/pallas_call | solution.py:282
  124.3 4.2 %collective-permute-start = (bf16[1152,128]{1,0:T(8,128)(2,1)}, bf16[1152,128]{1,0:T(8,128)(2,1)S(1)}, u32[]{:S(2)}, u32[]{:S(2)}) collective-permute-start(bf16[1152,128]{1,0:T(8,128)(2,1)} %get-tuple-element.18), channel_id=1, source_target_pairs={{0,128},{32,160},{64,192},{96,224},{128,0},{160,32},{192,64},{224,... | collective-permute-start | bytes 884744 | tf_op jit(solution)/shard_map/ppermute | solution.py:382
  128.6 1.1 dynamic-slice_bitcast_fusion.1
  130.7 1.0 copy-done.17
  131.7 2.4 %gradient.2 = (bf16[1024,128]{1,0:T(8,128)(2,1)S(1)}, f32[1152,128]{1,0:T(8,128)S(1)}) custom-call(bf16[1152,128]{1,0:T(8,128)(2,1)S(1)} %copy-done.16, bf16[1024,128]{1,0:T(8,128)(2,1)S(1)} %get-tuple-element.50.cotangent, bf16[1152,128]{1,0:T(8,128)(2,1)S(1)} %bitcast.31, f32[1152,128]{1,0:T(8,128)S(1)} %broadcast_in_dim.691.before), custom_call_target="tpu_custom_call" | custom-call | flops 603979776 | bytes 3145728 | tf_op jit(solution)/shard_map/gradient/pallas_call | solution.py:320
  134.1 3.7 %collective-permute-done.state = bf16[1152,128]{1,0:T(8,128)(2,1)S(1)} collective-permute-done((bf16[1152,128]{1,0:T(8,128)(2,1)}, bf16[1152,128]{1,0:T(8,128)(2,1)S(1)}, u32[]{:S(2)}, u32[]{:S(2)}) %collective-permute-start) | collective-permute-done | bytes 294944 | tf_op jit(solution)/shard_map/ppermute | solution.py:382
  137.7 2.4 %gradient.3 = (bf16[1024,128]{1,0:T(8,128)(2,1)S(1)}, bf16[1152,128]{1,0:T(8,128)(2,1)S(1)}) custom-call(bf16[1152,128]{1,0:T(8,128)(2,1)S(1)} %collective-permute-done.state, bf16[1024,128]{1,0:T(8,128)(2,1)S(1)} %get-tuple-element.51.cotangent, bf16[1152,128]{1,0:T(8,128)(2,1)S(1)} %bitcast.32, f32[1152,128]{1,0:T(8,128)S(1)} %get-tuple-element.19.before), custom_call_target="tpu_custom_call" | custom-call | flops 603979776 | bytes 3145728 | tf_op jit(solution)/shard_map/gradient/pallas_call | solution.py:320
  140.2 18.0 %all_to_all.32 = bf16[32,36,128]{2,1,0:T(8,128)(2,1)S(1)} all-to-all(bf16[32,36,128]{2,1,0:T(8,128)(2,1)S(1)} %reshape.1450), channel_id=1, replica_groups=mesh['dp'=2,'segment'=8,'tile'=32] {'tile'}, dimensions={0} | all-to-all | bytes 589824 | tf_op jit(solution)/shard_map/all_to_all | solution.py:350
  159.2 9.3 %all-to-all-start.5 = ((bf16[64,36,128]{2,1,0:T(8,128)(2,1)}), bf16[64,36,128]{2,1,0:T(8,128)(2,1)S(1)}, u32[]{:S(2)}, u32[]{:S(2)}) async-start(bf16[64,36,128]{2,1,0:T(8,128)(2,1)} %broadcast_in_dim.692), calls=%async_computation.5 | async-start | bytes 1310720 | tf_op jit(solution)/shard_map/all_to_all | solution.py:342
  169.4 20.6 %all-to-all-done.5 = bf16[64,36,128]{2,1,0:T(8,128)(2,1)S(1)} async-done(((bf16[64,36,128]{2,1,0:T(8,128)(2,1)}), bf16[64,36,128]{2,1,0:T(8,128)(2,1)S(1)}, u32[]{:S(2)}, u32[]{:S(2)}) %all-to-all-start.5) | async-done | bytes 589856 | tf_op jit(solution)/shard_map/all_to_all | solution.py:342
  (239 shorter events, 27.9 us)
Async XLA Ops:
  7.2 1.0 copy-start
  7.2 13.4 %copy-start.29 = (s32[32,4]{0,1:T(4,128)S(1)}, s32[32,4]{0,1:T(4,128)}, u32[]{:S(2)}) copy-start(s32[32,4]{0,1:T(4,128)} %param.7) | copy-start | bytes 1540
  7.2 13.4 %copy-start.28 = (s32[32,4]{0,1:T(4,128)S(1)}, s32[32,4]{0,1:T(4,128)}, u32[]{:S(2)}) copy-start(s32[32,4]{0,1:T(4,128)} %param.8) | copy-start | bytes 1540
  7.2 13.4 %copy-start.27 = (s32[32,4]{0,1:T(4,128)S(1)}, s32[32,4]{0,1:T(4,128)}, u32[]{:S(2)}) copy-start(s32[32,4]{0,1:T(4,128)} %param.9) | copy-start | bytes 1540
  9.3 25.7 %all-to-all-start = ((bf16[8,128,128]{2,1,0:T(8,128)(2,1)}), bf16[8,128,128]{2,1,0:T(8,128)(2,1)S(1)}, u32[]{:S(2)}, u32[]{:S(2)}) async-start(bf16[8,128,128]{2,1,0:T(8,128)(2,1)} %broadcast_in_dim.634), calls=%async_computation | async-start | bytes 524288 | tf_op jit(solution)/shard_map/all_to_all | solution.py:342
  19.6 35.2 %all-gather.2.cloned.1.call-start = ((), (), s32[]{:S(2)}) async-start(), calls=%async_computation.6 | async-start | bytes 2654208 | tf_op jit(solution)/shard_map/all_gather | solution.py:361
  34.0 2.6 %copy-start.25 = (s32[1152]{0:T(1024)}, s32[1152]{0:T(1024)S(1)}, u32[]{:S(2)}) copy-start(s32[1152]{0:T(1024)S(1)} %fusion.18) | copy-start | bytes 13828
  34.1 20.6 %copy-start.9 = (bf16[256,16]{1,0:T(8,128)(2,1)}, bf16[256,16]{1,0:T(8,128)(2,1)S(1)}, u32[]{:S(2)}) copy-start(bf16[256,16]{1,0:T(8,128)(2,1)S(1)} %fusion.13.refs_8_) | copy-start | bytes 24580
  34.3 20.5 %copy-start.7 = (bf16[384,64]{1,0:T(8,128)(2,1)}, bf16[384,64]{1,0:T(8,128)(2,1)S(1)}, u32[]{:S(2)}) copy-start(bf16[384,64]{1,0:T(8,128)(2,1)S(1)} %fusion.12.refs_7_) | copy-start | bytes 147460
  34.6 20.1 %copy-start.21 = (s32[2]{0:T(128)}, s32[2]{0:T(128)S(1)}, u32[]{:S(2)}) copy-start(s32[2]{0:T(128)S(1)} %pad_add_fusion.3.refs_0_) | copy-start | bytes 28
  34.7 20.0 %copy-start.23 = (s32[4]{0:T(128)}, s32[4]{0:T(128)S(1)}, u32[]{:S(2)}) copy-start(s32[4]{0:T(128)S(1)} %slice.48.refs_1_) | copy-start | bytes 52
  34.9 19.8 %copy-start.5 = (bf16[512,160]{1,0:T(8,128)(2,1)}, bf16[512,160]{1,0:T(8,128)(2,1)S(1)}, u32[]{:S(2)}) copy-start(bf16[512,160]{1,0:T(8,128)(2,1)S(1)} %fusion.8.refs_6_) | copy-start | bytes 491524
  36.6 11.4 %all-to-all-start.1 = ((bf16[4,288,128]{2,1,0:T(8,128)(2,1)}), bf16[4,288,128]{2,1,0:T(8,128)(2,1)S(1)}, u32[]{:S(2)}, u32[]{:S(2)}) async-start(bf16[4,288,128]{2,1,0:T(8,128)(2,1)} %bitcast.4), calls=%async_computation.1 | async-start | bytes 589824 | tf_op jit(solution)/shard_map/all_to_all | solution.py:375
  41.9 25.0 %copy-start.11 = (bf16[128,128]{1,0:T(8,128)(2,1)}, bf16[128,128]{1,0:T(8,128)(2,1)S(1)}, u32[]{:S(2)}) copy-start(bf16[128,128]{1,0:T(8,128)(2,1)S(1)} %fusion.14.refs_12_) | copy-start | bytes 98308
  42.1 24.8 %copy-start.3 = (bf16[576,672]{1,0:T(8,128)(2,1)}, bf16[576,672]{1,0:T(8,128)(2,1)S(1)}, u32[]{:S(2)}) copy-start(bf16[576,672]{1,0:T(8,128)(2,1)S(1)} %fusion.6.refs_9_) | copy-start | bytes 2322436
  54.8 1.7 copy-start.1
  56.4 30.4 %copy-start.26 = (s32[1152]{0:T(1024)S(1)}, s32[1152]{0:T(1024)}, u32[]{:S(2)}) copy-start(s32[1152]{0:T(1024)} %copy-done.25) | copy-start | bytes 13828
  66.9 19.9 %copy-start.13 = (bf16[1152,128]{1,0:T(8,128)(2,1)}, bf16[1152,128]{1,0:T(8,128)(2,1)S(1)}, u32[]{:S(2)}) copy-start(bf16[1152,128]{1,0:T(8,128)(2,1)S(1)} %get-tuple-element.14.refs_13_) | copy-start | bytes 884740
  66.9 19.9 %copy-start.19 = (bf16[1024,128]{1,0:T(8,128)(2,1)}, bf16[1024,128]{1,0:T(8,128)(2,1)S(1)}, u32[]{:S(2)}) copy-start(bf16[1024,128]{1,0:T(8,128)(2,1)S(1)} %get-tuple-element.12.refs_2_) | copy-start | bytes 786436
  86.8 20.9 %copy-start.2 = (bf16[8,1152,128]{2,1,0:T(8,128)(2,1)S(1)}, bf16[8,1152,128]{2,1,0:T(8,128)(2,1)}, u32[]{:S(2)}) copy-start(bf16[8,1152,128]{2,1,0:T(8,128)(2,1)} %all-gather.2.cloned.1.call-done.refs_4_) | copy-start | bytes 7077892
  107.7 1.2 copy-start.4
  124.3 13.4 %collective-permute-start = (bf16[1152,128]{1,0:T(8,128)(2,1)}, bf16[1152,128]{1,0:T(8,128)(2,1)S(1)}, u32[]{:S(2)}, u32[]{:S(2)}) collective-permute-start(bf16[1152,128]{1,0:T(8,128)(2,1)} %get-tuple-element.18), channel_id=1, source_target_pairs={{0,128},{32,160},{64,192},{96,224},{128,0},{160,32},{192,64},{224,... | collective-permute-start | bytes 884744 | tf_op jit(solution)/shard_map/ppermute | solution.py:382
  128.6 9.2 %copy-start.18 = (bf16[1,1152,128]{2,1,0:T(8,128)(2,1)S(1)}, bf16[1,1152,128]{2,1,0:T(8,128)(2,1)}, u32[]{:S(2)}) copy-start(bf16[1,1152,128]{2,1,0:T(8,128)(2,1)} %param.10) | copy-start | bytes 884740
  159.2 30.8 %all-to-all-start.5 = ((bf16[64,36,128]{2,1,0:T(8,128)(2,1)}), bf16[64,36,128]{2,1,0:T(8,128)(2,1)S(1)}, u32[]{:S(2)}, u32[]{:S(2)}) async-start(bf16[64,36,128]{2,1,0:T(8,128)(2,1)} %broadcast_in_dim.692), calls=%async_computation.5 | async-start | bytes 1310720 | tf_op jit(solution)/shard_map/all_to_all | solution.py:342
  (11 other events, 9.2 us)
Sparse Core Ops, SparseCore 0:
  22.5 32.1 all-gather.1

commit v5 on v4

--- a/solution.py
+++ b/solution.py
@@ -14,12 +14,14 @@
 SPLIT = 4
 PART = SIDE // SPLIT
 EDGE = DEPTH * PART
-SHARE = 4 * EDGE
-BLOCKS = [[(x, c) for x in range(DEPTH + 1 - j) for c in range(DEPTH - j)] for j in range(1, DEPTH)]
-SLOTS = sum(len(block) for block in BLOCKS)
+STRIPS = 4 * EDGE
+BLOCKS = [(1, 0), (1, 1), (1, 2), (2, 0), (2, 1), (3, 0)]
 FANS = 8
-PICK = SHARE + FANS * SLOTS
-VMEM_BYTES = 48 * 1024 * 1024
+SLOTS = len(BLOCKS)
+SHARE = STRIPS + 32
+PICK = STRIPS + FANS * SLOTS
+AROUND = SPLIT * FANS * SLOTS
+VMEM_BYTES = 20 * 1024 * 1024
 
 
 def iota(shape, axis):
@@ -80,9 +82,11 @@
 
 def selections(neighbor, edge_of, reverse, tile, part, columns):
     seams = (neighbor * 8 + edge_of * 2 + reverse).reshape(-1)
-    row = jnp.arange(SHARE, dtype=jnp.int32)
+    row = jnp.arange(STRIPS, dtype=jnp.int32)
     share = rim_cell(row // EDGE, row // PART % DEPTH, part * PART + row % PART)
-    rim = onehot(share, CELLS)
+    corner = jnp.arange(SHARE - STRIPS, dtype=jnp.int32)
+    spot = rim_cell(corner // 6, corner % 3, jnp.where(corner // 3 % 2 == 1, SIDE - 1 - part, part))
+    rim = onehot(jnp.concatenate([share, jnp.where(corner < 24, spot, -1)]), CELLS)
     targets = jnp.arange(neighbor.shape[0] // columns, dtype=jnp.int32)[:, None] * columns + tile % columns
     fan = jnp.arange(FANS, dtype=jnp.int32)
     nbr, edge, flip = lookup(seams, targets * 4 + fan // 2)
@@ -90,12 +94,11 @@
     for j in range(1, DEPTH):
         chain.append(walk(seams, *chain[-1]))
     around, edges, ends = zip(*chain[1:])
-    counts = [len(block) for block in BLOCKS]
-    x = static([cell[0] for block in BLOCKS for cell in block])
-    c = static([cell[1] for block in BLOCKS for cell in block])
-    along = jnp.where(spread(ends, counts) == 1, SIDE - 1 - x, x)
-    inner = spread(edges, counts) * EDGE + c * PART + along % PART
-    inner = jnp.where(along // PART == part, inner, -SHARE * columns)
+    counts = [sum(1 for block in BLOCKS if block[0] == j) for j in range(1, DEPTH)]
+    j = static([block[0] for block in BLOCKS])
+    c = static([block[1] for block in BLOCKS])
+    inner = STRIPS + (spread(edges, counts) * 2 + spread(ends, counts)) * 3 + c
+    inner = jnp.where(part + j <= DEPTH, inner, -SHARE * columns)
     strip = [nbr[:, 0::2], edge[:, 0::2]]
     strip = [jnp.concatenate([jnp.broadcast_to(v[:, d : d + 1], (v.shape[0], EDGE)) for d in range(4)], 1) for v in strip]
     source = jnp.concatenate([strip[0], spread(around, counts).reshape(-1, FANS * SLOTS)], axis=1)
@@ -109,10 +112,10 @@
     d, place = row // SIDE, row % SIDE
     end = jnp.where(place == 0, 0, jnp.where(place == SIDE - 1, 1, -1))
     beyond = []
-    for slots, stride, rows in ((SLOTS, 3, 4), (8, 2, 3), (2, 1, 2)):
+    for slots, stride, rows, count in ((SLOTS, FANS * SLOTS, 4, AROUND), (8, 2, 3, 64), (2, 1, 2, 16)):
         target = (d * 2 + end)[None] * slots + stride * jnp.arange(rows, dtype=jnp.int32)[:, None]
         target = jnp.where(end[None] < 0, -1, target)
-        beyond.append(onehot(target.reshape(-1), FANS * slots))
+        beyond.append(onehot(target.reshape(-1), count))
     fan3 = iota((1, FANS, 1), 1)
     at_end = fan3 // 2 * SIDE + fan3 % 2 * (SIDE - 1)
     x = static([0, 0, 1, 1, 2, 2, 0, 1])
@@ -120,16 +123,17 @@
     near = jnp.arange(8, dtype=jnp.int32) < 6
     x, c = tap_columns(spread(edges[:2], (6, 2)), spread(ends[:2], (6, 2)), near, x, c)
     base = DEPTH * RING + fan3 * SLOTS
+    next_place = FANS * SLOTS
     first = jnp.where(
         c < 0,
         jnp.where(near, x * RING + at_end, base + x),
         jnp.where(
             x < 0,
-            jnp.where(near, base + 12 + 2 * c, base + 18 + c),
-            jnp.where(near, base + 3 * x + c, base + 12 + 2 * x + c),
+            base + next_place * c + jnp.where(near, 3, 5),
+            base + next_place * x + jnp.where(near, 0, 3) + c,
         ),
     )
-    first = onehot(jnp.where((c < 0) & (x < 0), -1, first).reshape(-1), DEPTH * RING + FANS * SLOTS)
+    first = onehot(jnp.where((c < 0) & (x < 0), -1, first).reshape(-1), DEPTH * RING + AROUND)
     x, c = tap_columns(spread(edges[:1], (2,)), spread(ends[:1], (2,)), None, static([0, 1]), static([0, 0]))
     base = (DEPTH - 1) * RING + fan3 * 8
     second = jnp.where(c < 0, x * RING + at_end, jnp.where(x < 0, base + 6 + c, base + 2 * x + c))
@@ -231,9 +235,7 @@
         )
         for r in range(DEPTH)
     ]
-    fans = cells[SHARE:PICK]
-    for q in range(1, SPLIT):
-        fans = fans + cells[q * PICK + SHARE : (q + 1) * PICK]
+    fans = jnp.concatenate([cells[q * PICK + STRIPS : (q + 1) * PICK] for q in range(SPLIT)], axis=0)
 
     def deliver(i, act):
         for slot, target in ((0, kept), (1, sent)):
@@ -302,26 +304,30 @@
     )(index, edge, start, gathered, weights, rim, *maps, *chosen)
 
 
-def gradient_kernel(state, cotangent, weights, before, level, term, padded, patches):
+def gradient_kernel(last, state, cotangent, weights, before, level, term, padded, patches):
     fill_patches(state, padded, patches)
     pre_act = dot(patches[...], weights[...])
     gate = sigmoid(pre_act)
     level[...] = (state[0:CELLS, :].astype(jnp.float32) + pre_act * gate).astype(jnp.bfloat16)
     slope = gate * (1.0 + pre_act * (1.0 - gate))
     delta = (cotangent[...].astype(jnp.float32) * slope).astype(jnp.bfloat16)
-    added = lax.dot_general(
-        patches[...], delta, (((0,), (0,)), ((), ())), preferred_element_type=jnp.float32
-    )
-    term[...] = (before[...] + added).astype(term.dtype)
-
-
-def gradient(state, cotangent, weights, before, dtype):
+    added = before[...] + lax.dot_general(
+        delta, patches[...], (((0,), (0,)), ((), ())), preferred_element_type=jnp.float32
+    )
+    if not last:
+        term[...] = added
+        return
+    for k in range(TAPS):
+        term[k * C : (k + 1) * C, :] = added[:, k * C : (k + 1) * C].T.astype(jnp.bfloat16)
+
+
+def gradient(state, cotangent, weights, before, last):
     vmem = pl.BlockSpec(memory_space=pltpu.VMEM)
     return pl.pallas_call(
-        gradient_kernel,
+        lambda *refs: gradient_kernel(last, *refs),
         out_shape=(
             jax.ShapeDtypeStruct((CELLS, C), jnp.bfloat16),
-            jax.ShapeDtypeStruct((TAPS * C, C), dtype),
+            jax.ShapeDtypeStruct((TAPS * C, C), jnp.bfloat16) if last else jax.ShapeDtypeStruct((C, TAPS * C), jnp.float32),
         ),
         in_specs=[vmem] * 4,
         out_specs=(vmem,) * 2,
@@ -383,9 +389,9 @@
     cotans = cotangent[0, :, 0].reshape(2, CELLS, C)
     mine = lax.dynamic_index_in_dim(cotans, sample, 0, False)
     theirs = lax.dynamic_index_in_dim(cotans, 1 - sample, 0, False)
-    zero = jnp.zeros((TAPS * C, C), jnp.float32)
-    level_mine, term = gradient(kept, mine, weights[0], zero, jnp.float32)
-    level_other, term = gradient(other, theirs, weights[0], term, jnp.bfloat16)
+    zero = jnp.zeros((C, TAPS * C), jnp.float32)
+    level_mine, term = gradient(kept, mine, weights[0], zero, False)
+    level_other, term = gradient(other, theirs, weights[0], term, True)
     total = sum_terms(term)
     low = jnp.where(sample == 0, level_mine, level_other)
     high = jnp.where(sample == 0, level_other, level_mine)

time: 199 us -> 196 us (0.985)
    all_to_all x1, blocking collectives: 12.2 us -> 9.55 us  [local(): lax.all_to_all(picked, 'tile', 0, 0, axis_index_groups=along_column)]
    all_gather x1, waiting for transfers between devices: 0.4 us -> 2.57 us  [local(): kernels = lax.all_gather(weights, 'segment', axis=0, tiled=True)]
    all_to_all x1, waiting for transfers between devices: 5.82 us -> 3.79 us  [local(): lax.all_to_all(picked, 'tile', 0, 0, axis_index_groups=along_column)]
    unnamed x60 -> x48, local copies, waits for them, and re-layouts: 13 us -> 14.2 us
where the time goes in v5:
time: 196 us; the launch traced here: 195 us
  blocking collectives  60.5 us (31%)
  waiting for transfers between devices  32 us (16%)
  local copies, waits for them, and re-layouts  28.1 us (14%)
  starting transfers between devices  27.6 us (14%)
  Pallas kernels  22.6 us (12%)
  between operations  14.9 us (8%)
  other arithmetic  6.66 us (3%)
  matrix products  2.52 us (1%)
    all_to_all x1, blocking collectives, share_out(): lax.all_to_all(jnp.broadcast_to(block[None], (count,) + block.shape), axi...  21 us
    all_to_all x2, waiting for transfers between devices, share_out(): lax.all_to_all(jnp.broadcast_to(block[None], (count,) + block.shape), axi...  19.9 us
    all_to_all x2, starting transfers between devices, share_out(): lax.all_to_all(jnp.broadcast_to(block[None], (count,) + block.shape), axi...  18.9 us
    pallas_call x2, Pallas kernels, four_sections(): pl.pallas_call(lambda *refs: round_kernel(step, last, *refs), out_shape=o...  18.6 us
    all_to_all x1, blocking collectives, sum_terms(): lax.all_to_all(term.reshape(count, rows, term.shape[1]), 'tile', 0, 0)  17.8 us
    unnamed x48, local copies, waits for them, and re-layouts  14.2 us
    all_gather x2, blocking collectives, local(): lax.all_gather(picked, 'segment', axis=0, tiled=True, axis_index_groups=t...  12.1 us
    all_to_all x1, blocking collectives, local(): lax.all_to_all(picked, 'tile', 0, 0, axis_index_groups=along_column)  9.55 us
  transfers between devices with their start and end apart: 5, of which 4 were waited for; matrix products, arithmetic and copies ran while one was open for 9% of the time, Pallas kernels for 1%

profile of v5, /device:TPU:18, one launch (start us, length us, event | category | flops | bytes accessed | tf_op | source)
XLA Modules:
  0.0 194.9 jit_solution(17030779984197882998)
XLA Ops:
  9.3 10.3 %all-to-all-start = ((bf16[8,160,128]{2,1,0:T(8,128)(2,1)}), bf16[8,160,128]{2,1,0:T(8,128)(2,1)S(1)}, u32[]{:S(2)}, u32[]{:S(2)}) async-start(bf16[8,160,128]{2,1,0:T(8,128)(2,1)} %broadcast_in_dim.584), calls=%async_computation | async-start | bytes 655360 | tf_op jit(solution)/shard_map/all_to_all | solution.py:348
  34.6 1.4 fusion.5
  36.1 5.2 %all-to-all-start.1 = ((bf16[4,176,128]{2,1,0:T(8,128)(2,1)}), bf16[4,176,128]{2,1,0:T(8,128)(2,1)S(1)}, u32[]{:S(2)}, u32[]{:S(2)}) async-start(bf16[4,176,128]{2,1,0:T(8,128)(2,1)} %bitcast.6), calls=%async_computation.1 | async-start | bytes 360448 | tf_op jit(solution)/shard_map/all_to_all | solution.py:381
  41.7 3.8 %all-to-all-done.1 = bf16[4,176,128]{2,1,0:T(8,128)(2,1)S(1)} async-done(((bf16[4,176,128]{2,1,0:T(8,128)(2,1)}), bf16[4,176,128]{2,1,0:T(8,128)(2,1)S(1)}, u32[]{:S(2)}, u32[]{:S(2)}) %all-to-all-start.1) | async-done | bytes 180256 | tf_op jit(solution)/shard_map/all_to_all | solution.py:381
  45.5 6.4 %all_gather.9.refs_3_ = bf16[704,128]{1,0:T(8,128)(2,1)S(1)} all-gather(bf16[176,128]{1,0:T(8,128)(2,1)S(1)} %reduce_sum.146), channel_id=1, replica_groups={{0,32,64,96},{128,160,192,224},{1,33,65,97},{129,161,193,225},{2,34,66,..., dimensions={0}, use_global_device_ids=true | all-gather | bytes 225280 | tf_op jit(solution)/shard_map/all_gather | solution.py:383
  51.9 2.6 %all-gather.2.cloned.1.call-done.refs_4_ = bf16[8,1152,128]{2,1,0:T(8,128)(2,1)} async-done(((bf16[1,1152,128]{2,1,0:T(8,128)(2,1)}), bf16[8,1152,128]{2,1,0:T(8,128)(2,1)}) %all-gather.2.cloned.1.call-update) | async-done | bytes 2359312 | tf_op jit(solution)/shard_map/all_gather | solution.py:367
  54.5 1.7 copy-done.1
  56.1 10.4 %four_sections.2 = (bf16[1152,128]{1,0:T(8,128)(2,1)S(1)}, bf16[1152,128]{1,0:T(8,128)(2,1)}, bf16[1024,128]{1,0:T(8,128)(2,1)S(1)}, bf16[160,128]{1,0:T(8,128)(2,1)S(1)}) custom-call(s32[2]{0:T(128)S(1)} %pad_add_fusion.4.refs_0_, s32[4]{0:T(128)S(1)} %slice.48.refs_1_, bf16[1024,128]{1,0:T(8,128)(2,1)S(1)} %bitcast.74, ...), custom_call_target="tpu_custom_call" | custom-call | flops 1207959552 | bytes 6291456 | tf_op jit(solution)/shard_map/four_sections/pallas_call | solution.py:284
  68.9 21.0 %all_to_all.30 = bf16[8,160,128]{2,1,0:T(8,128)(2,1)S(1)} all-to-all(bf16[8,160,128]{2,1,0:T(8,128)(2,1)S(1)} %broadcast_in_dim.640), channel_id=1, replica_groups={{0,1,2,3,4,5,6,7},{8,9,10,11,12,13,14,15},{16,17,18,19,20,21,22,23},{24..., dimensions={0} | all-to-all | bytes 655360 | tf_op jit(solution)/shard_map/all_to_all | solution.py:348
  90.7 9.6 %all_to_all.31 = bf16[4,176,128]{2,1,0:T(8,128)(2,1)} all-to-all(bf16[4,176,128]{2,1,0:T(8,128)(2,1)S(1)} %bitcast.83), channel_id=1, replica_groups={{0,8,16,24},{1,9,17,25},{2,10,18,26},{3,11,19,27},{4,12,20,28},{5,13,21..., dimensions={0} | all-to-all | bytes 360448 | tf_op jit(solution)/shard_map/all_to_all | solution.py:381
  100.3 1.6 reduce_sum.152
  101.9 5.8 %all_gather.11.refs_3_ = bf16[704,128]{1,0:T(8,128)(2,1)S(1)} all-gather(bf16[176,128]{1,0:T(8,128)(2,1)} %reduce_sum.152), channel_id=1, replica_groups={{0,32,64,96},{128,160,192,224},{1,33,65,97},{129,161,193,225},{2,34,66,..., dimensions={0}, use_global_device_ids=true | all-gather | bytes 225280 | tf_op jit(solution)/shard_map/all_gather | solution.py:383
  107.6 1.2 copy-done.4
  112.3 1.0 copy-done.14
  114.2 8.1 %four_sections.3 = (bf16[1152,128]{1,0:T(8,128)(2,1)S(1)}, bf16[1152,128]{1,0:T(8,128)(2,1)}) custom-call(s32[2]{0:T(128)S(1)} %pad_add_fusion.4.refs_0_, s32[4]{0:T(128)S(1)} %slice.48.refs_1_, bf16[1024,128]{1,0:T(8,128)(2,1)S(1)} %copy-done.20, bf16[704,128]{1,0:T(8,128)(2,1)S(1)} %all_gather.11.refs_3_, ...), custom_call_target="tpu_custom_call", output_to_operand_aliasing={{0}: (13, {}), {1}: (14, {})} | custom-call | flops 1207959552 | bytes 6291456 | tf_op jit(solution)/shard_map/four_sections/pallas_call | solution.py:284
  123.1 3.5 %collective-permute-start = (bf16[1152,128]{1,0:T(8,128)(2,1)}, bf16[1152,128]{1,0:T(8,128)(2,1)S(1)}, u32[]{:S(2)}, u32[]{:S(2)}) collective-permute-start(bf16[1152,128]{1,0:T(8,128)(2,1)} %get-tuple-element.18), channel_id=1, source_target_pairs={{0,128},{32,160},{64,192},{96,224},{128,0},{160,32},{192,64},{224,... | collective-permute-start | bytes 884744 | tf_op jit(solution)/shard_map/ppermute | solution.py:388
  126.5 1.1 dynamic-slice_bitcast_fusion.1
  128.6 1.0 copy-done.17
  129.6 2.0 %gradient.2 = (bf16[1024,128]{1,0:T(8,128)(2,1)S(1)}, f32[128,1152]{1,0:T(8,128)S(1)}) custom-call(bf16[1152,128]{1,0:T(8,128)(2,1)S(1)} %copy-done.16, bf16[1024,128]{1,0:T(8,128)(2,1)S(1)} %get-tuple-element.50.refs_1_, bf16[1152,128]{1,0:T(8,128)(2,1)S(1)} %bitcast.75, f32[128,1152]{1,0:T(8,128)S(1)} %broadcast_in_dim.641.refs_3_), custom_call_target="tpu_custom_call" | custom-call | flops 603979776 | bytes 3145728 | tf_op jit(solution)/shard_map/gradient/pallas_call | solution.py:326
  131.6 5.0 %collective-permute-done.refs_0_ = bf16[1152,128]{1,0:T(8,128)(2,1)S(1)} collective-permute-done((bf16[1152,128]{1,0:T(8,128)(2,1)}, bf16[1152,128]{1,0:T(8,128)(2,1)S(1)}, u32[]{:S(2)}, u32[]{:S(2)}) %collective-permute-start) | collective-permute-done | bytes 294944 | tf_op jit(solution)/shard_map/ppermute | solution.py:388
  136.6 2.1 %gradient.3 = (bf16[1024,128]{1,0:T(8,128)(2,1)S(1)}, bf16[1152,128]{1,0:T(8,128)(2,1)S(1)}) custom-call(bf16[1152,128]{1,0:T(8,128)(2,1)S(1)} %collective-permute-done.refs_0_, bf16[1024,128]{1,0:T(8,128)(2,1)S(1)} %get-tuple-element.51.refs_1_, bf16[1152,128]{1,0:T(8,128)(2,1)S(1)} %bitcast.76, f32[128,1152]{1,0:T(8,128)S(1)} %get-tuple-element.19.refs_3_), custom_call_target="tpu_custom_call" | custom-call | flops 603979776 | bytes 3145728 | tf_op jit(solution)/shard_map/gradient/pallas_call | solution.py:326
  138.8 17.8 %all_to_all.32 = bf16[32,36,128]{2,1,0:T(8,128)(2,1)S(1)} all-to-all(bf16[32,36,128]{2,1,0:T(8,128)(2,1)S(1)} %reshape.1479), channel_id=1, replica_groups=mesh['dp'=2,'segment'=8,'tile'=32] {'tile'}, dimensions={0} | all-to-all | bytes 589824 | tf_op jit(solution)/shard_map/all_to_all | solution.py:356
  157.5 8.6 %all-to-all-start.5 = ((bf16[64,36,128]{2,1,0:T(8,128)(2,1)}), bf16[64,36,128]{2,1,0:T(8,128)(2,1)S(1)}, u32[]{:S(2)}, u32[]{:S(2)}) async-start(bf16[64,36,128]{2,1,0:T(8,128)(2,1)} %broadcast_in_dim.642), calls=%async_computation.5 | async-start | bytes 1310720 | tf_op jit(solution)/shard_map/all_to_all | solution.py:348
  167.0 19.9 %all-to-all-done.5 = bf16[64,36,128]{2,1,0:T(8,128)(2,1)S(1)} async-done(((bf16[64,36,128]{2,1,0:T(8,128)(2,1)}), bf16[64,36,128]{2,1,0:T(8,128)(2,1)S(1)}, u32[]{:S(2)}, u32[]{:S(2)}) %all-to-all-start.5) | async-done | bytes 589856 | tf_op jit(solution)/shard_map/all_to_all | solution.py:348
  (225 shorter events, 29.2 us)
Async XLA Ops:
  7.2 1.0 copy-start
  7.2 13.5 %copy-start.23 = (s32[32,4]{0,1:T(4,128)S(1)}, s32[32,4]{0,1:T(4,128)}, u32[]{:S(2)}) copy-start(s32[32,4]{0,1:T(4,128)} %param.7) | copy-start | bytes 1540
  7.2 13.5 %copy-start.22 = (s32[32,4]{0,1:T(4,128)S(1)}, s32[32,4]{0,1:T(4,128)}, u32[]{:S(2)}) copy-start(s32[32,4]{0,1:T(4,128)} %param.8) | copy-start | bytes 1540
  7.2 13.5 %copy-start.21 = (s32[32,4]{0,1:T(4,128)S(1)}, s32[32,4]{0,1:T(4,128)}, u32[]{:S(2)}) copy-start(s32[32,4]{0,1:T(4,128)} %param.9) | copy-start | bytes 1540
  9.3 25.3 %all-to-all-start = ((bf16[8,160,128]{2,1,0:T(8,128)(2,1)}), bf16[8,160,128]{2,1,0:T(8,128)(2,1)S(1)}, u32[]{:S(2)}, u32[]{:S(2)}) async-start(bf16[8,160,128]{2,1,0:T(8,128)(2,1)} %broadcast_in_dim.584), calls=%async_computation | async-start | bytes 655360 | tf_op jit(solution)/shard_map/all_to_all | solution.py:348
  19.6 34.8 %all-gather.2.cloned.1.call-start = ((), (), s32[]{:S(2)}) async-start(), calls=%async_computation.6 | async-start | bytes 2654208 | tf_op jit(solution)/shard_map/all_gather | solution.py:367
  33.8 20.7 %copy-start.11 = (bf16[128,128]{1,0:T(8,128)(2,1)}, bf16[128,128]{1,0:T(8,128)(2,1)S(1)}, u32[]{:S(2)}) copy-start(bf16[128,128]{1,0:T(8,128)(2,1)S(1)} %fusion.14.refs_12_) | copy-start | bytes 98308
  34.0 20.4 %copy-start.9 = (bf16[384,64]{1,0:T(8,128)(2,1)}, bf16[384,64]{1,0:T(8,128)(2,1)S(1)}, u32[]{:S(2)}) copy-start(bf16[384,64]{1,0:T(8,128)(2,1)S(1)} %fusion.12.refs_7_) | copy-start | bytes 147460
  34.1 20.3 %copy-start.7 = (bf16[144,448]{1,0:T(8,128)(2,1)}, bf16[144,448]{1,0:T(8,128)(2,1)S(1)}, u32[]{:S(2)}) copy-start(bf16[144,448]{1,0:T(8,128)(2,1)S(1)} %fusion.11.refs_10_) | copy-start | bytes 387076
  34.5 20.0 %copy-start.5 = (bf16[512,192]{1,0:T(8,128)(2,1)}, bf16[512,192]{1,0:T(8,128)(2,1)S(1)}, u32[]{:S(2)}) copy-start(bf16[512,192]{1,0:T(8,128)(2,1)S(1)} %fusion.8.refs_6_) | copy-start | bytes 589828
  36.1 9.4 %all-to-all-start.1 = ((bf16[4,176,128]{2,1,0:T(8,128)(2,1)}), bf16[4,176,128]{2,1,0:T(8,128)(2,1)S(1)}, u32[]{:S(2)}, u32[]{:S(2)}) async-start(bf16[4,176,128]{2,1,0:T(8,128)(2,1)} %bitcast.6), calls=%async_computation.1 | async-start | bytes 360448 | tf_op jit(solution)/shard_map/all_to_all | solution.py:381
  54.4 1.7 copy-start.1
  66.6 0.9 copy-start.3
  68.9 38.7 %copy-start.2 = (bf16[8,1152,128]{2,1,0:T(8,128)(2,1)S(1)}, bf16[8,1152,128]{2,1,0:T(8,128)(2,1)}, u32[]{:S(2)}) copy-start(bf16[8,1152,128]{2,1,0:T(8,128)(2,1)} %all-gather.2.cloned.1.call-done.refs_4_) | copy-start | bytes 7077892
  107.6 1.2 copy-start.4
  108.8 0.9 copy-start.6
  109.7 0.9 copy-start.8
  112.3 1.0 copy-start.14
  113.3 0.9 copy-start.20
  123.1 13.6 %copy-start.18 = (bf16[1,1152,128]{2,1,0:T(8,128)(2,1)S(1)}, bf16[1,1152,128]{2,1,0:T(8,128)(2,1)}, u32[]{:S(2)}) copy-start(bf16[1,1152,128]{2,1,0:T(8,128)(2,1)} %param.10) | copy-start | bytes 884740
  123.1 13.6 %collective-permute-start = (bf16[1152,128]{1,0:T(8,128)(2,1)}, bf16[1152,128]{1,0:T(8,128)(2,1)S(1)}, u32[]{:S(2)}, u32[]{:S(2)}) collective-permute-start(bf16[1152,128]{1,0:T(8,128)(2,1)} %get-tuple-element.18), channel_id=1, source_target_pairs={{0,128},{32,160},{64,192},{96,224},{128,0},{160,32},{192,64},{224,... | collective-permute-start | bytes 884744 | tf_op jit(solution)/shard_map/ppermute | solution.py:388
  127.7 1.0 copy-start.16
  128.6 1.0 copy-start.17
  157.5 29.5 %all-to-all-start.5 = ((bf16[64,36,128]{2,1,0:T(8,128)(2,1)}), bf16[64,36,128]{2,1,0:T(8,128)(2,1)S(1)}, u32[]{:S(2)}, u32[]{:S(2)}) async-start(bf16[64,36,128]{2,1,0:T(8,128)(2,1)} %broadcast_in_dim.642), calls=%async_computation.5 | async-start | bytes 1310720 | tf_op jit(solution)/shard_map/all_to_all | solution.py:348
  (5 other events, 3.8 us)
Sparse Core Ops, SparseCore 0:
  22.6 31.7 all-gather.1

commit v6 on v5

--- a/solution.py
+++ b/solution.py
@@ -304,9 +304,12 @@
     )(index, edge, start, gathered, weights, rim, *maps, *chosen)
 
 
-def gradient_kernel(last, state, cotangent, weights, before, level, term, padded, patches):
+def gradient_kernel(last, index, state, cotangents, weights, before, level, term, padded, patches, cotangent, sem):
+    load = pltpu.make_async_copy(cotangents.at[index[0]], cotangent, sem)
+    load.start()
     fill_patches(state, padded, patches)
     pre_act = dot(patches[...], weights[...])
+    load.wait()
     gate = sigmoid(pre_act)
     level[...] = (state[0:CELLS, :].astype(jnp.float32) + pre_act * gate).astype(jnp.bfloat16)
     slope = gate * (1.0 + pre_act * (1.0 - gate))
@@ -321,26 +324,50 @@
         term[k * C : (k + 1) * C, :] = added[:, k * C : (k + 1) * C].T.astype(jnp.bfloat16)
 
 
-def gradient(state, cotangent, weights, before, last):
+def gradient(sample, state, cotangents, weights, before, last):
     vmem = pl.BlockSpec(memory_space=pltpu.VMEM)
+    smem = pl.BlockSpec(memory_space=pltpu.SMEM)
+    hbm = pl.BlockSpec(memory_space=pltpu.HBM)
     return pl.pallas_call(
         lambda *refs: gradient_kernel(last, *refs),
         out_shape=(
             jax.ShapeDtypeStruct((CELLS, C), jnp.bfloat16),
             jax.ShapeDtypeStruct((TAPS * C, C), jnp.bfloat16) if last else jax.ShapeDtypeStruct((C, TAPS * C), jnp.float32),
         ),
-        in_specs=[vmem] * 4,
+        in_specs=[smem, vmem, hbm, vmem, vmem],
         out_specs=(vmem,) * 2,
         scratch_shapes=[
             pltpu.VMEM((SIDE + 2, SIDE + 16, C), jnp.float32),
             pltpu.VMEM((CELLS, TAPS * C), jnp.bfloat16),
+            pltpu.VMEM((CELLS, C), jnp.bfloat16),
+            pltpu.SemaphoreType.DMA,
         ],
         compiler_params=pltpu.CompilerParams(vmem_limit_bytes=VMEM_BYTES),
         cost_estimate=pl.CostEstimate(
             flops=2 * 2 * CELLS * TAPS * C * C, bytes_accessed=3 << 20, transcendentals=CELLS * C
         ),
         name="gradient",
-    )(state, cotangent, weights, before)
+    )(sample, state, cotangents, weights, before)
+
+
+def add_parts_kernel(parts, out):
+    total = parts[0].astype(jnp.float32)
+    for i in range(1, parts.shape[0]):
+        total = total + parts[i].astype(jnp.float32)
+    out[...] = total.astype(out.dtype)
+
+
+def add_parts(parts):
+    vmem = pl.BlockSpec(memory_space=pltpu.VMEM)
+    return pl.pallas_call(
+        add_parts_kernel,
+        out_shape=jax.ShapeDtypeStruct(parts.shape[1:], parts.dtype),
+        in_specs=[vmem],
+        out_specs=vmem,
+        compiler_params=pltpu.CompilerParams(vmem_limit_bytes=4 * 1024 * 1024),
+        cost_estimate=pl.CostEstimate(flops=parts.size, bytes_accessed=4 * parts.size, transcendentals=0),
+        name="add_parts",
+    )(parts)
 
 
 def share_out(block, axis, groups=None):
@@ -379,7 +406,7 @@
         rims = share_out(share, "tile", along_row).reshape(-1, C)
         picked = dot(pick, rims).astype(jnp.bfloat16).reshape(rows, PICK, C)
         picked = lax.all_to_all(picked, "tile", 0, 0, axis_index_groups=along_column)
-        picked = jnp.sum(picked.astype(jnp.float32), axis=0).astype(jnp.bfloat16)
+        picked = add_parts(picked)
         gathered = lax.all_gather(picked, "segment", axis=0, tiled=True, axis_index_groups=teams)
         kept, sent, *more = four_sections(step, index, edge, state, gathered, kernels, rim, maps, chosen)
         chosen = (kept, sent)
@@ -387,11 +414,10 @@
             state, share = more
     other = lax.ppermute(sent, "segment", [(s, s ^ SPLIT) for s in range(8)])
     cotans = cotangent[0, :, 0].reshape(2, CELLS, C)
-    mine = lax.dynamic_index_in_dim(cotans, sample, 0, False)
-    theirs = lax.dynamic_index_in_dim(cotans, 1 - sample, 0, False)
+    mine, theirs = sample.reshape(1).astype(jnp.int32), (1 - sample).reshape(1).astype(jnp.int32)
     zero = jnp.zeros((C, TAPS * C), jnp.float32)
-    level_mine, term = gradient(kept, mine, weights[0], zero, False)
-    level_other, term = gradient(other, theirs, weights[0], term, True)
+    level_mine, term = gradient(mine, kept, cotans, weights[0], zero, False)
+    level_other, term = gradient(theirs, other, cotans, weights[0], term, True)
     total = sum_terms(term)
     low = jnp.where(sample == 0, level_mine, level_other)
     high = jnp.where(sample == 0, level_other, level_mine)

time: 196 us -> 186 us (0.949)
  local copies, waits for them, and re-layouts: 28.1 us -> 18.6 us
    unnamed x48 -> x20, local copies, waits for them, and re-layouts: 14.2 us -> 5.66 us
where the time goes in v6:
time: 186 us; the launch traced here: 185 us
  blocking collectives  60 us (32%)
  waiting for transfers between devices  33.4 us (18%)
  starting transfers between devices  27.3 us (15%)
  Pallas kernels  23.2 us (12%)
  local copies, waits for them, and re-layouts  18.6 us (10%)
  between operations  14.8 us (8%)
  other arithmetic  5.1 us (3%)
  matrix products  2.52 us (1%)
    all_to_all x1, blocking collectives, share_out(): lax.all_to_all(jnp.broadcast_to(block[None], (count,) + block.shape), axi...  21 us
    all_to_all x2, waiting for transfers between devices, share_out(): lax.all_to_all(jnp.broadcast_to(block[None], (count,) + block.shape), axi...  20.6 us
    all_to_all x2, starting transfers between devices, share_out(): lax.all_to_all(jnp.broadcast_to(block[None], (count,) + block.shape), axi...  18.6 us
    pallas_call x2, Pallas kernels, four_sections(): pl.pallas_call(lambda *refs: round_kernel(step, last, *refs), out_shape=o...  18.5 us
    all_to_all x1, blocking collectives, sum_terms(): lax.all_to_all(term.reshape(count, rows, term.shape[1]), 'tile', 0, 0)  17.8 us
    all_gather x2, blocking collectives, local(): lax.all_gather(picked, 'segment', axis=0, tiled=True, axis_index_groups=t...  11.8 us
    all_to_all x1, blocking collectives, local(): lax.all_to_all(picked, 'tile', 0, 0, axis_index_groups=along_column)  9.43 us
    ppermute x1, waiting for transfers between devices, local(): other = lax.ppermute(sent, 'segment', [(s, s ^ SPLIT) for s in range(8)])  5.75 us
  transfers between devices with their start and end apart: 5, of which 4 were waited for; matrix products, arithmetic and copies ran while one was open for 9% of the time, Pallas kernels for 1%

profile of v6, /device:TPU:18, one launch (start us, length us, event | category | flops | bytes accessed | tf_op | source)
XLA Modules:
  0.0 185.1 jit_solution(12921783922363380571)
XLA Ops:
  7.3 0.9 copy-done
  9.3 10.3 %all-to-all-start = ((bf16[8,160,128]{2,1,0:T(8,128)(2,1)}), bf16[8,160,128]{2,1,0:T(8,128)(2,1)S(1)}, u32[]{:S(2)}, u32[]{:S(2)}) async-start(bf16[8,160,128]{2,1,0:T(8,128)(2,1)} %broadcast_in_dim.584), calls=%async_computation | async-start | bytes 655360 | tf_op jit(solution)/shard_map/all_to_all | solution.py:375
  34.8 1.4 fusion.5
  36.2 5.2 %all-to-all-start.1 = ((bf16[4,176,128]{2,1,0:T(8,128)(2,1)}), bf16[4,176,128]{2,1,0:T(8,128)(2,1)S(1)}, u32[]{:S(2)}, u32[]{:S(2)}) async-start(bf16[4,176,128]{2,1,0:T(8,128)(2,1)} %bitcast.7), calls=%async_computation.1 | async-start | bytes 360448 | tf_op jit(solution)/shard_map/all_to_all | solution.py:408
  41.8 3.8 %all-to-all-done.1.parts = bf16[4,176,128]{2,1,0:T(8,128)(2,1)S(1)} async-done(((bf16[4,176,128]{2,1,0:T(8,128)(2,1)}), bf16[4,176,128]{2,1,0:T(8,128)(2,1)S(1)}, u32[]{:S(2)}, u32[]{:S(2)}) %all-to-all-start.1) | async-done | bytes 180256 | tf_op jit(solution)/shard_map/all_to_all | solution.py:408
  45.6 6.2 %all_gather.9.refs_3_ = bf16[704,128]{1,0:T(8,128)(2,1)S(1)} all-gather(bf16[176,128]{1,0:T(8,128)(2,1)S(1)} %add_parts.2), channel_id=1, replica_groups={{0,32,64,96},{128,160,192,224},{1,33,65,97},{129,161,193,225},{2,34,66,..., dimensions={0}, use_global_device_ids=true | all-gather | bytes 225280 | tf_op jit(solution)/shard_map/all_gather | solution.py:410
  51.9 2.6 %all-gather.2.cloned.1.call-done.refs_4_ = bf16[8,1152,128]{2,1,0:T(8,128)(2,1)} async-done(((bf16[1,1152,128]{2,1,0:T(8,128)(2,1)}), bf16[8,1152,128]{2,1,0:T(8,128)(2,1)}) %all-gather.2.cloned.1.call-update) | async-done | bytes 2359312 | tf_op jit(solution)/shard_map/all_gather | solution.py:394
  54.4 1.7 copy-done.1
  56.1 10.4 %four_sections.2 = (bf16[1152,128]{1,0:T(8,128)(2,1)S(1)}, bf16[1152,128]{1,0:T(8,128)(2,1)}, bf16[1024,128]{1,0:T(8,128)(2,1)S(1)}, bf16[160,128]{1,0:T(8,128)(2,1)S(1)}) custom-call(s32[2]{0:T(128)S(1)} %pad_add_fusion.4.refs_0_, s32[4]{0:T(128)S(1)} %slice.48.refs_1_, bf16[1024,128]{1,0:T(8,128)(2,1)S(1)} %bitcast.72, ...), custom_call_target="tpu_custom_call" | custom-call | flops 1207959552 | bytes 6291456 | tf_op jit(solution)/shard_map/four_sections/pallas_call | solution.py:284
  66.6 21.0 %all_to_all.30 = bf16[8,160,128]{2,1,0:T(8,128)(2,1)S(1)} all-to-all(bf16[8,160,128]{2,1,0:T(8,128)(2,1)S(1)} %broadcast_in_dim.640), channel_id=1, replica_groups={{0,1,2,3,4,5,6,7},{8,9,10,11,12,13,14,15},{16,17,18,19,20,21,22,23},{24..., dimensions={0} | all-to-all | bytes 655360 | tf_op jit(solution)/shard_map/all_to_all | solution.py:375
  88.4 9.4 %all_to_all.31.parts = bf16[4,176,128]{2,1,0:T(8,128)(2,1)S(1)} all-to-all(bf16[4,176,128]{2,1,0:T(8,128)(2,1)S(1)} %bitcast.82), channel_id=1, replica_groups={{0,8,16,24},{1,9,17,25},{2,10,18,26},{3,11,19,27},{4,12,20,28},{5,13,21..., dimensions={0} | all-to-all | bytes 360448 | tf_op jit(solution)/shard_map/all_to_all | solution.py:408
  97.9 5.6 %all_gather.11.refs_3_ = bf16[704,128]{1,0:T(8,128)(2,1)S(1)} all-gather(bf16[176,128]{1,0:T(8,128)(2,1)S(1)} %add_parts.3), channel_id=1, replica_groups={{0,32,64,96},{128,160,192,224},{1,33,65,97},{129,161,193,225},{2,34,66,..., dimensions={0}, use_global_device_ids=true | all-gather | bytes 225280 | tf_op jit(solution)/shard_map/all_gather | solution.py:410
  103.4 8.1 %four_sections.3 = (bf16[1152,128]{1,0:T(8,128)(2,1)S(1)}, bf16[1152,128]{1,0:T(8,128)(2,1)}) custom-call(s32[2]{0:T(128)S(1)} %pad_add_fusion.4.refs_0_, s32[4]{0:T(128)S(1)} %slice.48.refs_1_, bf16[1024,128]{1,0:T(8,128)(2,1)S(1)} %get-tuple-element.12.refs_2_, ...), custom_call_target="tpu_custom_call", output_to_operand_aliasing={{0}: (13, {}), {1}: (14, {})} | custom-call | flops 1207959552 | bytes 6291456 | tf_op jit(solution)/shard_map/four_sections/pallas_call | solution.py:284
  111.5 3.5 %collective-permute-start = (bf16[1152,128]{1,0:T(8,128)(2,1)}, bf16[1152,128]{1,0:T(8,128)(2,1)S(1)}, u32[]{:S(2)}, u32[]{:S(2)}) collective-permute-start(bf16[1152,128]{1,0:T(8,128)(2,1)} %get-tuple-element.18), channel_id=1, source_target_pairs={{0,128},{32,160},{64,192},{96,224},{128,0},{160,32},{192,64},{224,... | collective-permute-start | bytes 884744 | tf_op jit(solution)/shard_map/ppermute | solution.py:415
  115.1 1.0 copy-done.3
  116.0 1.0 copy-done.5
  117.1 2.3 %gradient.2 = (bf16[1024,128]{1,0:T(8,128)(2,1)S(1)}, f32[128,1152]{1,0:T(8,128)S(1)}) custom-call(s32[1]{0:T(128)} %bitcast.refs_0_, bf16[1152,128]{1,0:T(8,128)(2,1)S(1)} %get-tuple-element.16.refs_1_, bf16[2,1024,128]{2,1,0:T(8,128)(2,1)S(1)} %bitcast.75, bf16[1152,128]{1,0:T(8,128)(2,1)S(1)} %bitcast.73, f32[128,1152]{1,0:T(8,128)S(1)} %broadcast_in_dim.641.refs_4_), custom_call_target="tpu_custom_call" | custom-call | flops 603979776 | bytes 3145728 | tf_op jit(solution)/shard_map/gradient/pallas_call | solution.py:331
  119.4 5.7 %collective-permute-done.refs_1_ = bf16[1152,128]{1,0:T(8,128)(2,1)S(1)} collective-permute-done((bf16[1152,128]{1,0:T(8,128)(2,1)}, bf16[1152,128]{1,0:T(8,128)(2,1)S(1)}, u32[]{:S(2)}, u32[]{:S(2)}) %collective-permute-start) | collective-permute-done | bytes 294944 | tf_op jit(solution)/shard_map/ppermute | solution.py:415
  125.1 1.0 copy-done.6
  126.2 2.3 %gradient.3 = (bf16[1024,128]{1,0:T(8,128)(2,1)S(1)}, bf16[1152,128]{1,0:T(8,128)(2,1)S(1)}) custom-call(s32[1]{0:T(128)} %bitcast.19.refs_0_, bf16[1152,128]{1,0:T(8,128)(2,1)S(1)} %collective-permute-done.refs_1_, bf16[2,1024,128]{2,1,0:T(8,128)(2,1)S(1)} %bitcast.76, bf16[1152,128]{1,0:T(8,128)(2,1)S(1)} %bitcast.74, ...), custom_call_target="tpu_custom_call" | custom-call | flops 603979776 | bytes 3145728 | tf_op jit(solution)/shard_map/gradient/pallas_call | solution.py:331
  128.6 17.8 %all_to_all.32 = bf16[32,36,128]{2,1,0:T(8,128)(2,1)S(1)} all-to-all(bf16[32,36,128]{2,1,0:T(8,128)(2,1)S(1)} %reshape.1487), channel_id=1, replica_groups=mesh['dp'=2,'segment'=8,'tile'=32] {'tile'}, dimensions={0} | all-to-all | bytes 589824 | tf_op jit(solution)/shard_map/all_to_all | solution.py:383
  147.3 8.3 %all-to-all-start.5 = ((bf16[64,36,128]{2,1,0:T(8,128)(2,1)}), bf16[64,36,128]{2,1,0:T(8,128)(2,1)S(1)}, u32[]{:S(2)}, u32[]{:S(2)}) async-start(bf16[64,36,128]{2,1,0:T(8,128)(2,1)} %broadcast_in_dim.642), calls=%async_computation.5 | async-start | bytes 1310720 | tf_op jit(solution)/shard_map/all_to_all | solution.py:375
  156.6 20.6 %all-to-all-done.5 = bf16[64,36,128]{2,1,0:T(8,128)(2,1)S(1)} async-done(((bf16[64,36,128]{2,1,0:T(8,128)(2,1)}), bf16[64,36,128]{2,1,0:T(8,128)(2,1)S(1)}, u32[]{:S(2)}, u32[]{:S(2)}) %all-to-all-start.5) | async-done | bytes 589856 | tf_op jit(solution)/shard_map/all_to_all | solution.py:375
  177.3 0.9 reduce_sum.128
  (202 shorter events, 19.0 us)
Async XLA Ops:
  7.2 1.0 copy-start
  7.2 13.5 %copy-start.9 = (s32[32,4]{0,1:T(4,128)S(1)}, s32[32,4]{0,1:T(4,128)}, u32[]{:S(2)}) copy-start(s32[32,4]{0,1:T(4,128)} %param.7) | copy-start | bytes 1540
  7.2 13.5 %copy-start.8 = (s32[32,4]{0,1:T(4,128)S(1)}, s32[32,4]{0,1:T(4,128)}, u32[]{:S(2)}) copy-start(s32[32,4]{0,1:T(4,128)} %param.8) | copy-start | bytes 1540
  7.2 13.5 %copy-start.7 = (s32[32,4]{0,1:T(4,128)S(1)}, s32[32,4]{0,1:T(4,128)}, u32[]{:S(2)}) copy-start(s32[32,4]{0,1:T(4,128)} %param.9) | copy-start | bytes 1540
  9.3 25.4 %all-to-all-start = ((bf16[8,160,128]{2,1,0:T(8,128)(2,1)}), bf16[8,160,128]{2,1,0:T(8,128)(2,1)S(1)}, u32[]{:S(2)}, u32[]{:S(2)}) async-start(bf16[8,160,128]{2,1,0:T(8,128)(2,1)} %broadcast_in_dim.584), calls=%async_computation | async-start | bytes 655360 | tf_op jit(solution)/shard_map/all_to_all | solution.py:375
  19.6 34.8 %all-gather.2.cloned.1.call-start = ((), (), s32[]{:S(2)}) async-start(), calls=%async_computation.6 | async-start | bytes 2654208 | tf_op jit(solution)/shard_map/all_gather | solution.py:394
  36.2 9.4 %all-to-all-start.1 = ((bf16[4,176,128]{2,1,0:T(8,128)(2,1)}), bf16[4,176,128]{2,1,0:T(8,128)(2,1)S(1)}, u32[]{:S(2)}, u32[]{:S(2)}) async-start(bf16[4,176,128]{2,1,0:T(8,128)(2,1)} %bitcast.7), calls=%async_computation.1 | async-start | bytes 360448 | tf_op jit(solution)/shard_map/all_to_all | solution.py:408
  54.4 1.7 copy-start.1
  66.5 36.9 %copy-start.2 = (bf16[8,1152,128]{2,1,0:T(8,128)(2,1)S(1)}, bf16[8,1152,128]{2,1,0:T(8,128)(2,1)}, u32[]{:S(2)}) copy-start(bf16[8,1152,128]{2,1,0:T(8,128)(2,1)} %all-gather.2.cloned.1.call-done.refs_4_) | copy-start | bytes 7077892
  111.5 13.6 %copy-start.4 = (bf16[1,1152,128]{2,1,0:T(8,128)(2,1)S(1)}, bf16[1,1152,128]{2,1,0:T(8,128)(2,1)}, u32[]{:S(2)}) copy-start(bf16[1,1152,128]{2,1,0:T(8,128)(2,1)} %param.10) | copy-start | bytes 884740
  111.5 13.6 %collective-permute-start = (bf16[1152,128]{1,0:T(8,128)(2,1)}, bf16[1152,128]{1,0:T(8,128)(2,1)S(1)}, u32[]{:S(2)}, u32[]{:S(2)}) collective-permute-start(bf16[1152,128]{1,0:T(8,128)(2,1)} %get-tuple-element.18), channel_id=1, source_target_pairs={{0,128},{32,160},{64,192},{96,224},{128,0},{160,32},{192,64},{224,... | collective-permute-start | bytes 884744 | tf_op jit(solution)/shard_map/ppermute | solution.py:415
  115.1 1.0 copy-start.3
  116.0 1.0 copy-start.5
  125.1 1.0 copy-start.6
  147.3 29.8 %all-to-all-start.5 = ((bf16[64,36,128]{2,1,0:T(8,128)(2,1)}), bf16[64,36,128]{2,1,0:T(8,128)(2,1)S(1)}, u32[]{:S(2)}, u32[]{:S(2)}) async-start(bf16[64,36,128]{2,1,0:T(8,128)(2,1)} %broadcast_in_dim.642), calls=%async_computation.5 | async-start | bytes 1310720 | tf_op jit(solution)/shard_map/all_to_all | solution.py:375
Sparse Core Ops, SparseCore 0:
  22.6 31.7 all-gather.1

commit v7 on v6

v7 whole, which is shorter than its diff:
```python
import jax
import jax.numpy as jnp
import numpy as np
from jax import lax
from jax.experimental import pallas as pl
from jax.experimental.pallas import tpu as pltpu
from jax.sharding import PartitionSpec as P

SIDE = 32
CELLS = SIDE * SIDE
RING = 4 * SIDE
C = 128
TAPS = 9
DEPTH = 8
SPLIT = 4
PART = SIDE // SPLIT
EDGE = DEPTH * PART
SHARE = 4 * EDGE
FANS = 8
VMEM_BYTES = 26 * 1024 * 1024


def round_up(value, step):
    return -(-value // step) * step


def block_cells(depth):
    return [
        (j, c, x) for j in range(1, depth) for c in range(depth - j) for x in range(depth - j + 1)
    ]


SLOTS = [(j, c, x) for j in range(1, DEPTH) for c in range(DEPTH - j) for x in range((DEPTH - j) // SPLIT + 1)]
SLOT_ROWS = round_up(len(SLOTS), 8)
PICK = SHARE + FANS * SLOT_ROWS
FAN_ROWS = round_up(len(block_cells(DEPTH)) + 8, 16)


def iota(shape, axis):
    return lax.broadcasted_iota(jnp.int32, shape, axis)


def onehot(target, columns):
    return (target[:, None] == iota((target.shape[0], columns), 1)).astype(jnp.bfloat16)


def lookup(seams, slot):
    hit = slot[..., None] == jnp.arange(seams.shape[0], dtype=jnp.int32)
    found = jnp.sum(jnp.where(hit, seams, 0), axis=-1)
    return found // 8, found // 2 % 4, found % 2


def rim_cell(edge, depth, place):
    last = SIDE - 1
    return jnp.where(
        edge == 0,
        depth * SIDE + place,
        jnp.where(
            edge == 1,
            place * SIDE + last - depth,
            jnp.where(edge == 2, (last - depth) * SIDE + place, place * SIDE + depth),
        ),
    )


def walk(seams, tile, edge, end):
    corner = jnp.where((edge == 0) | (edge == 3), 0, 1)
    tile, edge, flip = lookup(seams, tile * 4 + jnp.where(edge % 2 == 0, 3 - 2 * end, 2 * end))
    return tile, edge, jnp.where(flip == 1, 1 - corner, corner)


def spread(columns, steps):
    picked = [columns[max(j, 1) - 1] for j in steps]
    return jnp.stack(picked, axis=-1)


def pad_cells(cells, count):
    cells = cells + [(0, 0, 0)] * (count - len(cells))
    return [np.array(column, np.int32) for column in zip(*cells)]


def fan_taps(depth, edges, ends):
    cells, targets = block_cells(depth), block_cells(depth - 1)
    rows = round_up(len(targets), 16)
    after = round_up(len(cells), 8)
    j, c, x = pad_cells(targets, rows)
    k = iota((1, TAPS, 1), 1)
    dy, dx = k // 3 - 1, k % 3 - 1
    edge, end = spread(edges, j)[:, None], spread(ends, j)[:, None]
    down = jnp.where(edge == 0, dy, jnp.where(edge == 2, -dy, jnp.where(edge == 3, dx, -dx)))
    along = jnp.where(edge % 2 == 0, dx, dy)
    along = jnp.where(end == 1, -along, along)
    x, c = x + along, c + down
    first = np.array([sum(1 for cell in cells if cell[0] < step) for step in range(depth + 1)], np.int32)
    width = depth + 1 - np.arange(depth + 1, dtype=np.int32)
    inside = first[j] + c * width[j] + x
    before = jnp.where(j == 1, after + x, first[np.maximum(j - 1, 0)] + x * width[np.maximum(j - 1, 0)])
    beyond = first[np.minimum(j + 1, depth)] + c
    column = jnp.where(c < 0, jnp.where(x < 0, -1, before), jnp.where(x < 0, beyond, inside))
    column = jnp.where(j == 0, -1, column)
    return onehot(column.reshape(-1), round_up(after + 8, 16))


def selections(neighbor, edge_of, reverse, tile, part, columns):
    seams = (neighbor * 8 + edge_of * 2 + reverse).reshape(-1)
    row = jnp.arange(SHARE, dtype=jnp.int32)
    rim = onehot(rim_cell(row // EDGE, row // PART % DEPTH, row % PART * SPLIT + part), CELLS)
    targets = jnp.arange(neighbor.shape[0] // columns, dtype=jnp.int32)[:, None] * columns + tile % columns
    fan = jnp.arange(FANS, dtype=jnp.int32)
    nbr, edge, flip = lookup(seams, targets * 4 + fan // 2)
    chain = [(nbr, edge, jnp.broadcast_to(fan % 2, nbr.shape))]
    for j in range(1, DEPTH):
        chain.append(walk(seams, *chain[-1]))
    around, edges, ends = zip(*chain[1:])
    j, c, x = pad_cells(SLOTS, SLOT_ROWS)
    end = spread(ends, j)
    place = x * SPLIT + jnp.where(end == 1, SPLIT - 1 - part, part)
    inner = spread(edges, j) * EDGE + c * PART + jnp.where(end == 1, PART - 1 - x, x)
    inner = jnp.where((j > 0) & (place + j <= DEPTH), inner, -SHARE * columns)
    strip = [nbr[:, 0::2], edge[:, 0::2]]
    strip = [jnp.concatenate([jnp.broadcast_to(v[:, d : d + 1], (v.shape[0], EDGE)) for d in range(4)], 1) for v in strip]
    source = jnp.concatenate([strip[0], spread(around, j).reshape(-1, FANS * SLOT_ROWS)], axis=1)
    place = jnp.concatenate([strip[1] * EDGE + row % EDGE, inner.reshape(-1, FANS * SLOT_ROWS)], axis=1)
    place = jnp.where(source // columns == tile // columns, source % columns * SHARE + place, -1)
    pick = onehot(place.reshape(-1), columns * SHARE)
    mine = (targets == tile).astype(jnp.int32)
    edge, flip = jnp.sum(edge * mine, axis=0)[0::2], jnp.sum(flip * mine, axis=0)[0::2]
    edges = [jnp.sum(v * mine, axis=0) for v in edges]
    ends = [jnp.sum(v * mine, axis=0) for v in ends]
    cells = block_cells(DEPTH)
    j, c, x = pad_cells(cells, FAN_ROWS)
    slot = np.array([SLOTS.index((a, b, d // SPLIT)) for a, b, d in cells] + [0] * (FAN_ROWS - len(cells)), np.int32)
    member = jnp.where(spread(ends, j) == 1, SPLIT - 1 - x % SPLIT, x % SPLIT)
    gather = onehot(jnp.where(j > 0, member * SLOT_ROWS + slot, -1).reshape(-1), SPLIT * SLOT_ROWS)
    taps = [fan_taps(depth, edges, ends) for depth in range(DEPTH, 2, -1)]
    row = np.arange(RING)
    d, place = row // SIDE, row % SIDE
    order = onehot(jnp.asarray(place % SPLIT * 4 * PART + d * PART + place // SPLIT, jnp.int32), RING)
    fan, depth = np.arange(FANS * 8) // 8, np.arange(FANS * 8) % 8
    tips = onehot(jnp.asarray(depth * RING + fan // 2 * SIDE + fan % 2 * (SIDE - 1), jnp.int32), DEPTH * RING)
    end = np.where(place == 0, 0, np.where(place == SIDE - 1, 1, -1))
    target = np.where(end < 0, -1, (d * 2 + end) * 8 + np.arange(DEPTH)[:, None])
    beyond = onehot(jnp.asarray(target.reshape(-1), jnp.int32), FANS * 8)
    flip = jnp.concatenate([jnp.broadcast_to(flip[k : k + 1], (SIDE,)) for k in range(4)])
    turned = jnp.where(flip == 1, SIDE - 1 - place, place)
    facing = onehot(rim_cell(d, 0, turned), CELLS)
    turn = onehot(d * SIDE + turned, RING)
    return edge, rim, pick, (gather, order, tips, beyond, facing, turn, *taps)


def sigmoid(value):
    return 1.0 / (1.0 + jnp.exp(-value))


def fill_patches(state, padded, patches):
    padded[1 : SIDE + 1, 8 : SIDE + 8, :] = (
        state[0:CELLS, :].astype(jnp.float32).reshape(SIDE, SIDE, C)
    )
    halo = state[CELLS : CELLS + RING, :].astype(jnp.float32)
    empty = jnp.zeros((8, C), jnp.float32)
    for row, first in ((0, 0), (SIDE + 1, 2 * SIDE)):
        padded[row, 0:8, :] = empty
        padded[row, 8 : SIDE + 8, :] = halo[first : first + SIDE]
        padded[row, SIDE + 8 : SIDE + 16, :] = empty
    padded[1 : SIDE + 1, SIDE + 8, :] = halo[SIDE : 2 * SIDE]
    padded[1 : SIDE + 1, 7, :] = halo[3 * SIDE : 4 * SIDE]
    for dx in range(3):
        shifted = padded[:, 7 + dx : 7 + dx + SIDE, :].astype(jnp.bfloat16)
        shifted = shifted.reshape((SIDE + 2) * SIDE, C)
        for dy in range(3):
            k = dy * 3 + dx
            patches[:, k * C : (k + 1) * C] = shifted[dy * SIDE : dy * SIDE + CELLS]


def next_state(state, pre_act):
    return (state + pre_act * sigmoid(pre_act)).astype(jnp.bfloat16)


def dot(a, b):
    return jnp.dot(a, b, preferred_element_type=jnp.float32)


def update_strips(edge, strips, ends, mine, weights, side_patches):
    rows = len(strips) - 1
    place = iota((RING, C), 0) % SIDE
    moved = []
    for cells, beyond in [(mine, jnp.zeros_like(mine))] + list(zip(strips, ends)):
        below = jnp.where(place == 0, beyond, pltpu.roll(cells, 1, 0))
        above = jnp.where(place == SIDE - 1, beyond, pltpu.roll(cells, RING - 1, 0))
        moved.append([v.astype(jnp.bfloat16) for v in (below, cells, above)])
    for d in range(4):
        e = edge[d]
        for a in range(3):
            across = jnp.where((e == 0) | (e == 3), a, 2 - a)
            for b in range(3):
                tap = jnp.where(e % 2 == 0, 3 * across + b, 3 * b + across)
                lanes = pl.ds(pl.multiple_of(tap * C, C), C)
                for r in range(rows):
                    first = r * RING + d * SIDE
                    side_patches[first : first + SIDE, lanes] = moved[r + a][b][d * SIDE : (d + 1) * SIDE]
    before = jnp.concatenate(strips[:rows], axis=0)
    after = next_state(before, dot(side_patches[0 : rows * RING, :], weights)).astype(jnp.float32)
    return [after[r * RING : (r + 1) * RING] for r in range(rows)]


def update_fans(taps, fans, tips, weights, fan_patches):
    columns = taps.shape[1]
    rows = taps.shape[0] // (FANS * TAPS)
    centers = []
    for f in range(FANS):
        known = fans[f]
        pool = [known, tips[f * 8 : (f + 1) * 8]]
        spare = columns - known.shape[0] - 8
        if spare:
            pool.append(jnp.zeros((spare, C), jnp.float32))
        pool = jnp.concatenate(pool, axis=0).astype(jnp.bfloat16)
        found = dot(taps[f * TAPS * rows : (f + 1) * TAPS * rows, :], pool)
        for k in range(TAPS):
            fan_patches[f * rows : (f + 1) * rows, k * C : (k + 1) * C] = found[k * rows : (k + 1) * rows].astype(
                jnp.bfloat16
            )
        centers.append(found[4 * rows : 5 * rows])
    pre_act = dot(fan_patches[0 : FANS * rows, :], weights)
    after = next_state(jnp.concatenate(centers, axis=0), pre_act).astype(jnp.float32)
    return [after[f * rows : (f + 1) * rows] for f in range(FANS)]


def sections_kernel(*refs):
    index, edge, start, gathered, weights, gather, order, tips_of, beyond, facing, turn = refs[:11]
    taps, refs = refs[11 : 11 + DEPTH - 2], refs[11 + DEPTH - 2 :]
    kept, sent, states, padded, patches, side_patches, fan_patches, sems = refs

    def deliver(i, act):
        for slot, target in ((0, kept), (1, sent)):

            @pl.when(index[slot] == i)
            def _():
                act(pltpu.make_async_copy(states.at[i], target, sems.at[slot]))

    states[0, 0:CELLS, :] = start[...]
    strips = []
    for r in range(DEPTH):
        found = [
            gathered[q * PICK + d * EDGE + r * PART : q * PICK + d * EDGE + (r + 1) * PART, :].astype(jnp.float32)
            for q in range(SPLIT)
            for d in range(4)
        ]
        strips.append(dot(order[...], jnp.concatenate(found, axis=0).astype(jnp.bfloat16)))
    fans = []
    for f in range(FANS):
        first = SHARE + f * SLOT_ROWS
        found = [
            gathered[q * PICK + first : q * PICK + first + SLOT_ROWS, :].astype(jnp.float32) for q in range(SPLIT)
        ]
        found = jnp.concatenate(found, axis=0).astype(jnp.bfloat16)
        fans.append(dot(gather[f * FAN_ROWS : (f + 1) * FAN_ROWS, :], found))
    for i in range(DEPTH):
        state = states.at[i]
        state[CELLS : CELLS + RING, :] = dot(turn[...], strips[0].astype(jnp.bfloat16)).astype(jnp.bfloat16)
        deliver(i, lambda copy: copy.start())
        if i == DEPTH - 1:
            break
        known = DEPTH - i
        tile = state[0:CELLS, :]
        fill_patches(state, padded, patches)
        outer = jnp.concatenate([fan[0:8] for fan in fans], axis=0).astype(jnp.bfloat16)
        ends = dot(beyond[0 : known * RING, :], outer)
        ends = [ends[r * RING : (r + 1) * RING] for r in range(known)]
        mine = dot(facing[...], tile)
        moved = update_strips(edge, strips, ends, mine, weights[i], side_patches)
        if known > 2:
            cells = round_up(len(block_cells(known)), 8)
            pool = jnp.concatenate([v.astype(jnp.bfloat16) for v in strips], axis=0)
            tips = dot(tips_of[:, 0 : known * RING], pool)
            fans = update_fans(taps[i], [fan[0:cells] for fan in fans], tips, weights[i], fan_patches)
        strips = moved
        states[i + 1, 0:CELLS, :] = next_state(tile.astype(jnp.float32), dot(patches[...], weights[i]))
    for i in range(DEPTH):
        deliver(i, lambda copy: copy.wait())


def all_sections(index, edge, start, gathered, weights, maps):
    vmem = pl.BlockSpec(memory_space=pltpu.VMEM)
    smem = pl.BlockSpec(memory_space=pltpu.SMEM)
    hbm = pl.BlockSpec(memory_space=pl.ANY)
    bf16 = jnp.bfloat16
    state = jax.ShapeDtypeStruct((CELLS + RING, C), bf16)
    fan_rows = FANS * round_up(len(block_cells(DEPTH - 1)), 16)
    return pl.pallas_call(
        sections_kernel,
        out_shape=(state, state),
        in_specs=[smem] * 2 + [vmem] * (3 + len(maps)),
        out_specs=(hbm, hbm),
        scratch_shapes=[
            pltpu.VMEM((DEPTH, CELLS + RING, C), bf16),
            pltpu.VMEM((SIDE + 2, SIDE + 16, C), jnp.float32),
            pltpu.VMEM((CELLS, TAPS * C), bf16),
            pltpu.VMEM(((DEPTH - 1) * RING, TAPS * C), bf16),
            pltpu.VMEM((fan_rows, TAPS * C), bf16),
            pltpu.SemaphoreType.DMA((2,)),
        ],
        compiler_params=pltpu.CompilerParams(vmem_limit_bytes=VMEM_BYTES),
        cost_estimate=pl.CostEstimate(
            flops=3 * DEPTH * CELLS * TAPS * C * C, bytes_accessed=16 << 20, transcendentals=DEPTH * CELLS * C
        ),
        name="all_sections",
    )(index, edge, start, gathered, weights, *maps)


def gradient_kernel(last, index, state, cotangents, weights, before, level, term, padded, patches, cotangent, sem):
    load = pltpu.make_async_copy(cotangents.at[index[0]], cotangent, sem)
    load.start()
    fill_patches(state, padded, patches)
    pre_act = dot(patches[...], weights[...])
    load.wait()
    gate = sigmoid(pre_act)
    level[...] = (state[0:CELLS, :].astype(jnp.float32) + pre_act * gate).astype(jnp.bfloat16)
    slope = gate * (1.0 + pre_act * (1.0 - gate))
    delta = (cotangent[...].astype(jnp.float32) * slope).astype(jnp.bfloat16)
    added = before[...] + lax.dot_general(
        delta, patches[...], (((0,), (0,)), ((), ())), preferred_element_type=jnp.float32
    )
    if not last:
        term[...] = added
        return
    for k in range(TAPS):
        term[k * C : (k + 1) * C, :] = added[:, k * C : (k + 1) * C].T.astype(jnp.bfloat16)


def gradient(sample, state, cotangents, weights, before, last):
    vmem = pl.BlockSpec(memory_space=pltpu.VMEM)
    smem = pl.BlockSpec(memory_space=pltpu.SMEM)
    hbm = pl.BlockSpec(memory_space=pltpu.HBM)
    return pl.pallas_call(
        lambda *refs: gradient_kernel(last, *refs),
        out_shape=(
            jax.ShapeDtypeStruct((CELLS, C), jnp.bfloat16),
            jax.ShapeDtypeStruct((TAPS * C, C), jnp.bfloat16) if last else jax.ShapeDtypeStruct((C, TAPS * C), jnp.float32),
        ),
        in_specs=[smem, vmem, hbm, vmem, vmem],
        out_specs=(vmem,) * 2,
        scratch_shapes=[
            pltpu.VMEM((SIDE + 2, SIDE + 16, C), jnp.float32),
            pltpu.VMEM((CELLS, TAPS * C), jnp.bfloat16),
            pltpu.VMEM((CELLS, C), jnp.bfloat16),
            pltpu.SemaphoreType.DMA,
        ],
        compiler_params=pltpu.CompilerParams(vmem_limit_bytes=VMEM_BYTES),
        cost_estimate=pl.CostEstimate(
            flops=2 * 2 * CELLS * TAPS * C * C, bytes_accessed=3 << 20, transcendentals=CELLS * C
        ),
        name="gradient",
    )(sample, state, cotangents, weights, before)


def add_parts_kernel(parts, out):
    total = parts[0].astype(jnp.float32)
    for i in range(1, parts.shape[0]):
        total = total + parts[i].astype(jnp.float32)
    out[...] = total.astype(out.dtype)


def add_parts(parts):
    vmem = pl.BlockSpec(memory_space=pltpu.VMEM)
    return pl.pallas_call(
        add_parts_kernel,
        out_shape=jax.ShapeDtypeStruct(parts.shape[1:], parts.dtype),
        in_specs=[vmem],
        out_specs=vmem,
        compiler_params=pltpu.CompilerParams(vmem_limit_bytes=4 * 1024 * 1024),
        cost_estimate=pl.CostEstimate(flops=parts.size, bytes_accessed=4 * parts.size, transcendentals=0),
        name="add_parts",
    )(parts)


def share_out(block, axis, groups=None):
    count = lax.axis_size(axis) if groups is None else len(groups[0])
    return lax.all_to_all(
        jnp.broadcast_to(block[None], (count,) + block.shape), axis, 0, 0, axis_index_groups=groups
    )


def sum_terms(term):
    count = lax.axis_size("tile")
    rows = term.shape[0] // count
    pieces = lax.all_to_all(term.reshape(count, rows, term.shape[1]), "tile", 0, 0)
    piece = jnp.sum(pieces.astype(jnp.float32), axis=0).astype(jnp.bfloat16)
    pieces = share_out(piece, ("dp", "tile")).reshape((lax.axis_size("dp"),) + term.shape)
    return jnp.sum(pieces.astype(jnp.float32), axis=0)


def local(inputs, neighbor, edge_of, reverse, weights, cotangent):
    segment = lax.axis_index("segment")
    sample, part = segment // SPLIT, segment % SPLIT
    partner = segment ^ SPLIT
    teams = [[t * SPLIT + p for p in range(SPLIT)] for t in range(2)]
    kernels = lax.all_gather(weights, "segment", axis=0, tiled=True)
    tiles = neighbor.shape[0]
    rows = 4 if tiles % 8 == 0 else 2
    columns = tiles // rows
    along_row = [[r * columns + c for c in range(columns)] for r in range(rows)]
    along_column = [[r * columns + c for r in range(rows)] for c in range(columns)]
    edge, rim, pick, maps = selections(neighbor, edge_of, reverse, lax.axis_index("tile"), part, columns)
    index = jnp.stack([segment, partner]).astype(jnp.int32)
    state = lax.dynamic_index_in_dim(inputs[:, 0], sample, 0, False).reshape(CELLS, C)
    share = dot(rim, state).astype(jnp.bfloat16)
    rims = share_out(share, "tile", along_row).reshape(-1, C)
    picked = dot(pick, rims).astype(jnp.bfloat16).reshape(rows, PICK, C)
    picked = lax.all_to_all(picked, "tile", 0, 0, axis_index_groups=along_column)
    picked = add_parts(picked)
    gathered = lax.all_gather(picked, "segment", axis=0, tiled=True, axis_index_groups=teams)
    kept, sent = all_sections(index, edge, state, gathered, kernels, maps)
    other = lax.ppermute(sent, "segment", [(s, s ^ SPLIT) for s in range(8)])
    cotans = cotangent[0, :, 0].reshape(2, CELLS, C)
    mine, theirs = sample.reshape(1).astype(jnp.int32), (1 - sample).reshape(1).astype(jnp.int32)
    zero = jnp.zeros((C, TAPS * C), jnp.float32)
    level_mine, term = gradient(mine, kept, cotans, weights[0], zero, False)
    level_other, term = gradient(theirs, other, cotans, weights[0], term, True)
    total = sum_terms(term)
    low = jnp.where(sample == 0, level_mine, level_other)
    high = jnp.where(sample == 0, level_other, level_mine)
    levels = jnp.stack([low, high]).reshape(1, 2, 1, SIDE, SIDE, C)
    return levels, total[None]


def solution(mesh):
    placed = (
        P("dp", "tile", None, None, None),
        P(),
        P(),
        P(),
        P("segment", None, None),
        P("segment", "dp", "tile", None, None, None),
    )
    return jax.shard_map(
        local,
        mesh=mesh,
        in_specs=placed,
        out_specs=(P("segment", "dp", "tile", None, None, None), P("segment", None, None)),
        check_vma=False,
    )
```

time: 186 us -> 216 us (1.16); the launches traced: 185 us -> 211 us
  blocking collectives: 60 us -> 30.9 us
  local copies, waits for them, and re-layouts: 18.6 us -> 43 us
  other arithmetic: 5.1 us -> 21.6 us
  Pallas kernels: 23.2 us -> 27.1 us
  waiting for transfers between devices: 33.4 us -> 37.1 us
  matrix products: 2.52 us -> 5.53 us
  starting transfers between devices: 27.3 us -> 29.5 us
    all_to_all x2 -> x0, blocking collectives: 30.4 us -> none  [the longest x1 21 us: share_out(): lax.all_to_all(jnp.broadcast_to(block[None], (count,) + block.shape), axi...]
    convert_element_type x8 -> x12, other arithmetic: 0.96 us -> 16.8 us  [onehot(): (target[:, None] == iota((target.shape[0], columns), 1)).astype(jnp.bfloa...]
    unnamed x20 -> x176, local copies, waits for them, and re-layouts: 5.66 us -> 18.5 us
    all_to_all x1, waiting for transfers between devices: 3.79 us -> 12.6 us  [local(): lax.all_to_all(picked, 'tile', 0, 0, axis_index_groups=along_column)]
    all_to_all x1, blocking collectives: 17.8 us -> 23.6 us  [sum_terms(): lax.all_to_all(term.reshape(count, rows, term.shape[1]), 'tile', 0, 0)]
    all_gather x2 -> x1, blocking collectives: 11.8 us -> 7.29 us  [local(): lax.all_gather(picked, 'segment', axis=0, tiled=True, axis_index_groups=t...]
    broadcast_in_dim x46 -> x126, local copies, waits for them, and re-layouts: 3.7 us -> 7.93 us  [the longest x32 2.27 us: fan_taps(): jnp.where(edge == 3, dx, -dx)]
    pallas_call x2 -> x1, Pallas kernels: 18.5 us -> 22.4 us  [all_sections(): pl.pallas_call(sections_kernel, out_shape=(state, state), in_specs=[smem]...]
  transfers between devices with their start and end apart: 5 -> 5, of which waited for: 4 -> 3; matrix products, arithmetic and copies ran while one was open for 9% -> 23% of each run, Pallas kernels for 1% -> 1%
where the time goes in v7:
time: 216 us; the launch traced here: 211 us
  local copies, waits for them, and re-layouts  43 us (20%)
  waiting for transfers between devices  37.1 us (17%)
  blocking collectives  30.9 us (14%)
  starting transfers between devices  29.5 us (14%)
  Pallas kernels  27.1 us (13%)
  other arithmetic  21.6 us (10%)
  between operations  16.7 us (8%)
  matrix products  5.53 us (3%)
    all_to_all x1, blocking collectives, sum_terms(): lax.all_to_all(term.reshape(count, rows, term.shape[1]), 'tile', 0, 0)  23.6 us
    pallas_call x1, Pallas kernels, all_sections(): pl.pallas_call(sections_kernel, out_shape=(state, state), in_specs=[smem]...  22.4 us
    all_to_all x2, waiting for transfers between devices, share_out(): lax.all_to_all(jnp.broadcast_to(block[None], (count,) + block.shape), axi...  19.9 us
    all_to_all x2, starting transfers between devices, share_out(): lax.all_to_all(jnp.broadcast_to(block[None], (count,) + block.shape), axi...  19.7 us
    unnamed x176, local copies, waits for them, and re-layouts  18.5 us
    convert_element_type x12, other arithmetic, onehot(): (target[:, None] == iota((target.shape[0], columns), 1)).astype(jnp.bfloa...  16.8 us
    all_to_all x1, waiting for transfers between devices, local(): lax.all_to_all(picked, 'tile', 0, 0, axis_index_groups=along_column)  12.6 us
    all_gather x1, blocking collectives, local(): lax.all_gather(picked, 'segment', axis=0, tiled=True, axis_index_groups=t...  7.29 us
  transfers between devices with their start and end apart: 5, of which 3 were waited for; matrix products, arithmetic and copies ran while one was open for 23% of the time, Pallas kernels for 1%

profile of v7, /device:TPU:18, one launch (start us, length us, event | category | flops | bytes accessed | tf_op | source)
XLA Modules:
  0.0 211.5 jit_solution(8952329350017893134)
XLA Ops:
  10.2 10.4 %all-to-all-start = ((bf16[8,256,128]{2,1,0:T(8,128)(2,1)}), bf16[8,256,128]{2,1,0:T(8,128)(2,1)S(1)}, u32[]{:S(2)}, u32[]{:S(2)}) async-start(bf16[8,256,128]{2,1,0:T(8,128)(2,1)} %broadcast_in_dim.966), calls=%async_computation | async-start | bytes 1048576 | tf_op jit(solution)/shard_map/all_to_all | solution.py:378
  28.9 5.3 %fusion.2.refs_11_ = bf16[8064,176]{1,0:T(8,128)(2,1)} fusion(s32[8064]{0:T(1024)S(1)} %select_select_fusion), kind=kLoop, calls=%fused_computation.4 | loop fusion | flops 2838528 | bytes 2870784 | tf_op jit(solution)/shard_map/convert_element_type | solution.py:44
  48.9 1.0 fusion.8.refs_15_
  59.2 2.6 %fusion.4.refs_12_ = bf16[5760,128]{1,0:T(8,128)(2,1)S(1)} fusion(s32[5760]{0:T(1024)S(1)} %select_select_fusion.1), kind=kLoop, calls=%fused_computation.7 | loop fusion | flops 1474560 | bytes 1497600 | tf_op jit(solution)/shard_map/convert_element_type | solution.py:44
  61.9 1.8 fusion.7.refs_14_
  63.7 5.2 %fusion.3 = bf16[2816,128]{1,0:T(8,128)(2,1)} fusion(bf16[2048,128]{1,0:T(8,128)(2,1)S(1)} %bitcast.253, s32[2816]{0:T(1024)S(1)} %fusion.22), kind=kOutput, calls=%fused_computation.5 | convolution fusion | flops 1482522624 | bytes 1256448 | tf_op jit(solution)/shard_map/dot_general | solution.py:180
  68.9 5.4 %all-to-all-start.1 = ((bf16[4,704,128]{2,1,0:T(8,128)(2,1)}), bf16[4,704,128]{2,1,0:T(8,128)(2,1)S(1)}, u32[]{:S(2)}, u32[]{:S(2)}) async-start(bf16[4,704,128]{2,1,0:T(8,128)(2,1)} %bitcast.251), calls=%async_computation.1 | async-start | bytes 1441792 | tf_op jit(solution)/shard_map/all_to_all | solution.py:409
  74.5 2.3 %fusion.5.refs_13_ = bf16[3456,80]{1,0:T(8,128)(2,1)} fusion(s32[3456]{0:T(1024)S(1)} %select_select_fusion.2), kind=kLoop, calls=%fused_computation.9 | loop fusion | flops 552960 | bytes 566784 | tf_op jit(solution)/shard_map/convert_element_type | solution.py:44
  76.8 12.6 %all-to-all-done.1.parts = bf16[4,704,128]{2,1,0:T(8,128)(2,1)S(1)} async-done(((bf16[4,704,128]{2,1,0:T(8,128)(2,1)}), bf16[4,704,128]{2,1,0:T(8,128)(2,1)S(1)}, u32[]{:S(2)}, u32[]{:S(2)}) %all-to-all-start.1) | async-done | bytes 720928 | tf_op jit(solution)/shard_map/all_to_all | solution.py:409
  89.5 7.3 %all_gather.6.refs_3_ = bf16[2816,128]{1,0:T(8,128)(2,1)S(1)} all-gather(bf16[704,128]{1,0:T(8,128)(2,1)S(1)} %add_parts.1), channel_id=1, replica_groups={{0,32,64,96},{128,160,192,224},{1,33,65,97},{129,161,193,225},{2,34,66,..., dimensions={0}, use_global_device_ids=true | all-gather | bytes 901120 | tf_op jit(solution)/shard_map/all_gather | solution.py:411
  96.8 2.2 %copy-done.1 = bf16[8064,176]{1,0:T(8,128)(2,1)S(1)} copy-done((bf16[8064,176]{1,0:T(8,128)(2,1)S(1)}, bf16[8064,176]{1,0:T(8,128)(2,1)}, u32[]{:S(2)}) %copy-start.1) | copy-done | bytes 2838552
  98.9 1.2 copy-done.2
  100.1 1.1 copy-done.3
  106.8 1.7 copy-done.13
  108.5 22.4 %all_sections.1 = (bf16[1152,128]{1,0:T(8,128)(2,1)S(1)}, bf16[1152,128]{1,0:T(8,128)(2,1)}) custom-call(s32[2]{0:T(128)S(1)} %pad_add_fusion.1.refs_0_, s32[4]{0:T(128)S(1)} %slice.48.refs_1_, bf16[1024,128]{1,0:T(8,128)(2,1)S(1)} %bitcast.246, bf16[2816,128]{1,0:T(8,128)(2,1)S(1)} %all_gather.6.refs_3_, bf16[8,1152,128]{2,1,0:T(8,128)(2,1)S(1)} %copy-done.13, ...), custom_call_target="tpu_custom_call" | custom-call | flops 3623878656 | bytes 16777216 | tf_op jit(solution)/shard_map/all_sections/pallas_call | solution.py:289
  131.6 4.4 %collective-permute-start = (bf16[1152,128]{1,0:T(8,128)(2,1)}, bf16[1152,128]{1,0:T(8,128)(2,1)S(1)}, u32[]{:S(2)}, u32[]{:S(2)}) collective-permute-start(bf16[1152,128]{1,0:T(8,128)(2,1)} %get-tuple-element.10), channel_id=1, source_target_pairs={{0,128},{32,160},{64,192},{96,224},{128,0},{160,32},{192,64},{224,... | collective-permute-start | bytes 884744 | tf_op jit(solution)/shard_map/ppermute | solution.py:413
  137.1 1.0 copy-done.14
  139.1 2.3 %gradient.2 = (bf16[1024,128]{1,0:T(8,128)(2,1)S(1)}, f32[128,1152]{1,0:T(8,128)S(1)}) custom-call(s32[1]{0:T(128)} %bitcast.refs_0_, bf16[1152,128]{1,0:T(8,128)(2,1)S(1)} %copy-done.17, bf16[2,1024,128]{2,1,0:T(8,128)(2,1)S(1)} %bitcast.247, bf16[1152,128]{1,0:T(8,128)(2,1)S(1)} %bitcast.243, f32[128,1152]{1,0:T(8,128)S(1)} %broadcast_in_dim.1112.refs_4_), custom_call_target="tpu_custom_call" | custom-call | flops 603979776 | bytes 3145728 | tf_op jit(solution)/shard_map/gradient/pallas_call | solution.py:334
  141.3 3.9 %collective-permute-done.refs_1_ = bf16[1152,128]{1,0:T(8,128)(2,1)S(1)} collective-permute-done((bf16[1152,128]{1,0:T(8,128)(2,1)}, bf16[1152,128]{1,0:T(8,128)(2,1)S(1)}, u32[]{:S(2)}, u32[]{:S(2)}) %collective-permute-start) | collective-permute-done | bytes 294944 | tf_op jit(solution)/shard_map/ppermute | solution.py:413
  145.2 1.0 copy-done.15
  146.3 2.3 %gradient.3 = (bf16[1024,128]{1,0:T(8,128)(2,1)S(1)}, bf16[1152,128]{1,0:T(8,128)(2,1)S(1)}) custom-call(s32[1]{0:T(128)} %bitcast.33.refs_0_, bf16[1152,128]{1,0:T(8,128)(2,1)S(1)} %collective-permute-done.refs_1_, bf16[2,1024,128]{2,1,0:T(8,128)(2,1)S(1)} %bitcast.248, bf16[1152,128]{1,0:T(8,128)(2,1)S(1)} %bitcast.244, ...), custom_call_target="tpu_custom_call" | custom-call | flops 603979776 | bytes 3145728 | tf_op jit(solution)/shard_map/gradient/pallas_call | solution.py:334
  148.7 23.6 %all_to_all.20 = bf16[32,36,128]{2,1,0:T(8,128)(2,1)S(1)} all-to-all(bf16[32,36,128]{2,1,0:T(8,128)(2,1)S(1)} %reshape.17778), channel_id=1, replica_groups=mesh['dp'=2,'segment'=8,'tile'=32] {'tile'}, dimensions={0} | all-to-all | bytes 589824 | tf_op jit(solution)/shard_map/all_to_all | solution.py:386
  173.3 9.2 %all-to-all-start.3 = ((bf16[64,36,128]{2,1,0:T(8,128)(2,1)}), bf16[64,36,128]{2,1,0:T(8,128)(2,1)S(1)}, u32[]{:S(2)}, u32[]{:S(2)}) async-start(bf16[64,36,128]{2,1,0:T(8,128)(2,1)} %broadcast_in_dim.1113), calls=%async_computation.3 | async-start | bytes 1310720 | tf_op jit(solution)/shard_map/all_to_all | solution.py:378
  183.4 19.9 %all-to-all-done.3 = bf16[64,36,128]{2,1,0:T(8,128)(2,1)S(1)} async-done(((bf16[64,36,128]{2,1,0:T(8,128)(2,1)}), bf16[64,36,128]{2,1,0:T(8,128)(2,1)S(1)}, u32[]{:S(2)}, u32[]{:S(2)}) %all-to-all-start.3) | async-done | bytes 589856 | tf_op jit(solution)/shard_map/all_to_all | solution.py:378
  (536 shorter events, 44.8 us)
Async XLA Ops:
  7.2 14.4 %copy-start.21 = (s32[32,4]{0,1:T(4,128)S(1)}, s32[32,4]{0,1:T(4,128)}, u32[]{:S(2)}) copy-start(s32[32,4]{0,1:T(4,128)} %param.80) | copy-start | bytes 1540
  7.2 14.4 %copy-start.20 = (s32[32,4]{0,1:T(4,128)S(1)}, s32[32,4]{0,1:T(4,128)}, u32[]{:S(2)}) copy-start(s32[32,4]{0,1:T(4,128)} %param.81) | copy-start | bytes 1540
  7.2 14.4 %copy-start.19 = (s32[32,4]{0,1:T(4,128)S(1)}, s32[32,4]{0,1:T(4,128)}, u32[]{:S(2)}) copy-start(s32[32,4]{0,1:T(4,128)} %param.82) | copy-start | bytes 1540
  10.2 17.6 %copy-start.63 = (s32[112]{0:T(128)S(1)}, s32[112]{0:T(128)}, u32[]{:S(2)}) copy-start(s32[112]{0:T(128)} %constant.725.clone) | copy-start | bytes 1348
  10.2 17.8 %copy-start.62 = (s32[112]{0:T(128)S(1)}, s32[112]{0:T(128)}, u32[]{:S(2)}) copy-start(s32[112]{0:T(128)} %constant.724.clone) | copy-start | bytes 1348
  10.2 53.5 %all-to-all-start = ((bf16[8,256,128]{2,1,0:T(8,128)(2,1)}), bf16[8,256,128]{2,1,0:T(8,128)(2,1)S(1)}, u32[]{:S(2)}, u32[]{:S(2)}) async-start(bf16[8,256,128]{2,1,0:T(8,128)(2,1)} %broadcast_in_dim.966), calls=%async_computation | async-start | bytes 1048576 | tf_op jit(solution)/shard_map/all_to_all | solution.py:378
  20.7 76.1 %all-gather.2.cloned.1.call-start = ((), (), s32[]{:S(2)}) async-start(), calls=%async_computation.4 | async-start | bytes 2654208 | tf_op jit(solution)/shard_map/all_gather | solution.py:397
  43.0 7.8 %copy-start.29 = (s32[16]{0:T(128)S(1)}, s32[16]{0:T(128)}, u32[]{:S(2)}) copy-start(s32[16]{0:T(128)} %constant.769.clone) | copy-start | bytes 196
  43.0 7.9 %copy-start.28 = (s32[16]{0:T(128)S(1)}, s32[16]{0:T(128)}, u32[]{:S(2)}) copy-start(s32[16]{0:T(128)} %constant.773.clone) | copy-start | bytes 196
  43.0 8.0 %copy-start.27 = (s32[16]{0:T(128)S(1)}, s32[16]{0:T(128)}, u32[]{:S(2)}) copy-start(s32[16]{0:T(128)} %constant.770.clone) | copy-start | bytes 196
  43.2 7.9 %copy-start.72 = (pred[16]{0:T(512)(128)(4,1)S(1)}, pred[16]{0:T(512)(128)(4,1)}, u32[]{:S(2)}) copy-start(pred[16]{0:T(512)(128)(4,1)} %constant.774.clone) | copy-start | bytes 52
  46.5 9.9 %copy-start.67 = (s32[128]{0:T(128)S(1)}, s32[128]{0:T(128)}, u32[]{:S(2)}) copy-start(s32[128]{0:T(128)} %constant.778.clone) | copy-start | bytes 1540
  46.5 9.9 %copy-start.68 = (s32[128]{0:T(128)S(1)}, s32[128]{0:T(128)}, u32[]{:S(2)}) copy-start(s32[128]{0:T(128)} %constant.779.clone) | copy-start | bytes 1540
  46.5 9.9 %copy-start.69 = (s32[128]{0:T(128)S(1)}, s32[128]{0:T(128)}, u32[]{:S(2)}) copy-start(s32[128]{0:T(128)} %constant.783.clone) | copy-start | bytes 1540
  46.5 10.0 %copy-start.64 = (pred[128]{0:T(512)(128)(4,1)S(1)}, pred[128]{0:T(512)(128)(4,1)}, u32[]{:S(2)}) copy-start(pred[128]{0:T(512)(128)(4,1)} %constant.780.clone) | copy-start | bytes 388
  46.5 10.0 %copy-start.65 = (pred[128]{0:T(512)(128)(4,1)S(1)}, pred[128]{0:T(512)(128)(4,1)}, u32[]{:S(2)}) copy-start(pred[128]{0:T(512)(128)(4,1)} %constant.781.clone) | copy-start | bytes 388
  46.5 10.0 %copy-start.66 = (pred[128]{0:T(512)(128)(4,1)S(1)}, pred[128]{0:T(512)(128)(4,1)}, u32[]{:S(2)}) copy-start(pred[128]{0:T(512)(128)(4,1)} %constant.782.clone) | copy-start | bytes 388
  47.3 10.1 %copy-start.18 = (s32[1024]{0:T(1024)S(1)}, s32[1024]{0:T(1024)}, u32[]{:S(2)}) copy-start(s32[1024]{0:T(1024)} %constant.777.clone) | copy-start | bytes 12292
  47.7 10.7 %copy-start.26 = (s32[64]{0:T(128)S(1)}, s32[64]{0:T(128)}, u32[]{:S(2)}) copy-start(s32[64]{0:T(128)} %constant.776.clone) | copy-start | bytes 772
  63.7 10.6 %copy-start.25 = (s32[128]{0:T(128)S(1)}, s32[128]{0:T(128)}, u32[]{:S(2)}) copy-start(s32[128]{0:T(128)} %constant.775.clone) | copy-start | bytes 1540
  68.9 20.5 %all-to-all-start.1 = ((bf16[4,704,128]{2,1,0:T(8,128)(2,1)}), bf16[4,704,128]{2,1,0:T(8,128)(2,1)S(1)}, u32[]{:S(2)}, u32[]{:S(2)}) async-start(bf16[4,704,128]{2,1,0:T(8,128)(2,1)} %bitcast.251), calls=%async_computation.1 | async-start | bytes 1441792 | tf_op jit(solution)/shard_map/all_to_all | solution.py:409
  131.6 13.6 %copy-start.5 = (bf16[1,1152,128]{2,1,0:T(8,128)(2,1)S(1)}, bf16[1,1152,128]{2,1,0:T(8,128)(2,1)}, u32[]{:S(2)}) copy-start(bf16[1,1152,128]{2,1,0:T(8,128)(2,1)} %param.83) | copy-start | bytes 884740
  131.6 13.6 %collective-permute-start = (bf16[1152,128]{1,0:T(8,128)(2,1)}, bf16[1152,128]{1,0:T(8,128)(2,1)S(1)}, u32[]{:S(2)}, u32[]{:S(2)}) collective-permute-start(bf16[1152,128]{1,0:T(8,128)(2,1)} %get-tuple-element.10), channel_id=1, source_target_pairs={{0,128},{32,160},{64,192},{96,224},{128,0},{160,32},{192,64},{224,... | collective-permute-start | bytes 884744 | tf_op jit(solution)/shard_map/ppermute | solution.py:413
  173.3 30.1 %all-to-all-start.3 = ((bf16[64,36,128]{2,1,0:T(8,128)(2,1)}), bf16[64,36,128]{2,1,0:T(8,128)(2,1)S(1)}, u32[]{:S(2)}, u32[]{:S(2)}) async-start(bf16[64,36,128]{2,1,0:T(8,128)(2,1)} %broadcast_in_dim.1113), calls=%async_computation.3 | async-start | bytes 1310720 | tf_op jit(solution)/shard_map/all_to_all | solution.py:378
  (69 other events, 344.7 us)
Sparse Core Ops, SparseCore 0:
  23.6 31.3 all-gather.1

commit v8 on v7

--- a/solution.py
+++ b/solution.py
@@ -17,7 +17,8 @@
 EDGE = DEPTH * PART
 SHARE = 4 * EDGE
 FANS = 8
-VMEM_BYTES = 26 * 1024 * 1024
+VMEM_BYTES = 60 * 1024 * 1024
+GRADIENT_VMEM_BYTES = 20 * 1024 * 1024
 
 
 def round_up(value, step):
@@ -34,6 +35,62 @@
 SLOT_ROWS = round_up(len(SLOTS), 8)
 PICK = SHARE + FANS * SLOT_ROWS
 FAN_ROWS = round_up(len(block_cells(DEPTH)) + 8, 16)
+BLOCKS = DEPTH - 1
+
+
+def fan_layout(depth):
+    step = 1 if depth == DEPTH else 16
+    rows, starts = {}, [0]
+    for j in range(1, depth):
+        block = [cell for cell in block_cells(depth) if cell[0] == j]
+        rows.update({cell: starts[-1] + n for n, cell in enumerate(block)})
+        starts.append(round_up(starts[-1] + len(block), step))
+    return rows, starts, round_up(starts[-1], 8)
+
+
+def fan_taps(depth):
+    source, _, after = fan_layout(depth)
+    target, _, rows = fan_layout(depth - 1)
+    table = np.zeros((TAPS * rows, round_up(after + 8, 16)), np.float32)
+    for (j, c, x), row in target.items():
+        for down in (-1, 0, 1):
+            for along in (-1, 0, 1):
+                deep, place = c + down, x + along
+                if deep < 0 and place < 0:
+                    continue
+                if deep >= 0 and place >= 0:
+                    column = source[j, deep, place]
+                elif place < 0:
+                    column = source[j + 1, 0, deep]
+                else:
+                    column = after + place if j == 1 else source[j - 1, place, 0]
+                table[((down + 1) * 3 + along + 1) * rows + row, column] = 1
+    return table
+
+
+def member_rows(end):
+    table = np.zeros((FAN_ROWS, SPLIT * SLOT_ROWS), np.float32)
+    for (j, c, x), row in fan_layout(DEPTH)[0].items():
+        member = SPLIT - 1 - x % SPLIT if end else x % SPLIT
+        table[row, member * SLOT_ROWS + SLOTS.index((j, c, x // SPLIT))] = 1
+    return table
+
+
+def constant_maps():
+    row = np.arange(RING)
+    d, place = row // SIDE, row % SIDE
+    order = np.zeros((RING, RING), np.float32)
+    order[row, place % SPLIT * 4 * PART + d * PART + place // SPLIT] = 1
+    tips = np.zeros((FANS * 8, DEPTH * RING), np.float32)
+    beyond = np.zeros((DEPTH * RING, FANS * 8), np.float32)
+    for fan in range(FANS):
+        for depth in range(DEPTH):
+            column = depth * RING + fan // 2 * SIDE + fan % 2 * (SIDE - 1)
+            tips[fan * 8 + depth, column] = 1
+            beyond[column, fan * 8 + depth] = 1
+    taps = [fan_taps(depth) for depth in range(DEPTH, 2, -1)]
+    tables = [order, tips, beyond, member_rows(0), member_rows(1), *taps]
+    return [jnp.asarray(table.astype(jnp.bfloat16)) for table in tables]
 
 
 def iota(shape, axis):
@@ -70,35 +127,12 @@
 
 
 def spread(columns, steps):
-    picked = [columns[max(j, 1) - 1] for j in steps]
-    return jnp.stack(picked, axis=-1)
+    return sum(jnp.where(steps == j, column[..., None], 0) for j, column in enumerate(columns, 1))
 
 
 def pad_cells(cells, count):
     cells = cells + [(0, 0, 0)] * (count - len(cells))
     return [np.array(column, np.int32) for column in zip(*cells)]
-
-
-def fan_taps(depth, edges, ends):
-    cells, targets = block_cells(depth), block_cells(depth - 1)
-    rows = round_up(len(targets), 16)
-    after = round_up(len(cells), 8)
-    j, c, x = pad_cells(targets, rows)
-    k = iota((1, TAPS, 1), 1)
-    dy, dx = k // 3 - 1, k % 3 - 1
-    edge, end = spread(edges, j)[:, None], spread(ends, j)[:, None]
-    down = jnp.where(edge == 0, dy, jnp.where(edge == 2, -dy, jnp.where(edge == 3, dx, -dx)))
-    along = jnp.where(edge % 2 == 0, dx, dy)
-    along = jnp.where(end == 1, -along, along)
-    x, c = x + along, c + down
-    first = np.array([sum(1 for cell in cells if cell[0] < step) for step in range(depth + 1)], np.int32)
-    width = depth + 1 - np.arange(depth + 1, dtype=np.int32)
-    inside = first[j] + c * width[j] + x
-    before = jnp.where(j == 1, after + x, first[np.maximum(j - 1, 0)] + x * width[np.maximum(j - 1, 0)])
-    beyond = first[np.minimum(j + 1, depth)] + c
-    column = jnp.where(c < 0, jnp.where(x < 0, -1, before), jnp.where(x < 0, beyond, inside))
-    column = jnp.where(j == 0, -1, column)
-    return onehot(column.reshape(-1), round_up(after + 8, 16))
 
 
 def selections(neighbor, edge_of, reverse, tile, part, columns):
@@ -117,35 +151,28 @@
     place = x * SPLIT + jnp.where(end == 1, SPLIT - 1 - part, part)
     inner = spread(edges, j) * EDGE + c * PART + jnp.where(end == 1, PART - 1 - x, x)
     inner = jnp.where((j > 0) & (place + j <= DEPTH), inner, -SHARE * columns)
-    strip = [nbr[:, 0::2], edge[:, 0::2]]
-    strip = [jnp.concatenate([jnp.broadcast_to(v[:, d : d + 1], (v.shape[0], EDGE)) for d in range(4)], 1) for v in strip]
+    strip = [sum(jnp.where(row // EDGE == d, v[:, 2 * d : 2 * d + 1], 0) for d in range(4)) for v in (nbr, edge)]
     source = jnp.concatenate([strip[0], spread(around, j).reshape(-1, FANS * SLOT_ROWS)], axis=1)
     place = jnp.concatenate([strip[1] * EDGE + row % EDGE, inner.reshape(-1, FANS * SLOT_ROWS)], axis=1)
     place = jnp.where(source // columns == tile // columns, source % columns * SHARE + place, -1)
     pick = onehot(place.reshape(-1), columns * SHARE)
+    return rim, pick, (targets, edge, flip, edges, ends)
+
+
+def own_selections(tile, targets, edge, flip, edges, ends):
     mine = (targets == tile).astype(jnp.int32)
     edge, flip = jnp.sum(edge * mine, axis=0)[0::2], jnp.sum(flip * mine, axis=0)[0::2]
     edges = [jnp.sum(v * mine, axis=0) for v in edges]
     ends = [jnp.sum(v * mine, axis=0) for v in ends]
-    cells = block_cells(DEPTH)
-    j, c, x = pad_cells(cells, FAN_ROWS)
-    slot = np.array([SLOTS.index((a, b, d // SPLIT)) for a, b, d in cells] + [0] * (FAN_ROWS - len(cells)), np.int32)
-    member = jnp.where(spread(ends, j) == 1, SPLIT - 1 - x % SPLIT, x % SPLIT)
-    gather = onehot(jnp.where(j > 0, member * SLOT_ROWS + slot, -1).reshape(-1), SPLIT * SLOT_ROWS)
-    taps = [fan_taps(depth, edges, ends) for depth in range(DEPTH, 2, -1)]
-    row = np.arange(RING)
-    d, place = row // SIDE, row % SIDE
-    order = onehot(jnp.asarray(place % SPLIT * 4 * PART + d * PART + place // SPLIT, jnp.int32), RING)
-    fan, depth = np.arange(FANS * 8) // 8, np.arange(FANS * 8) % 8
-    tips = onehot(jnp.asarray(depth * RING + fan // 2 * SIDE + fan % 2 * (SIDE - 1), jnp.int32), DEPTH * RING)
-    end = np.where(place == 0, 0, np.where(place == SIDE - 1, 1, -1))
-    target = np.where(end < 0, -1, (d * 2 + end) * 8 + np.arange(DEPTH)[:, None])
-    beyond = onehot(jnp.asarray(target.reshape(-1), jnp.int32), FANS * 8)
-    flip = jnp.concatenate([jnp.broadcast_to(flip[k : k + 1], (SIDE,)) for k in range(4)])
+    d, place = jnp.arange(RING, dtype=jnp.int32) // SIDE, jnp.arange(RING, dtype=jnp.int32) % SIDE
+    flip = sum(jnp.where(d == k, flip[k], 0) for k in range(4))
     turned = jnp.where(flip == 1, SIDE - 1 - place, place)
     facing = onehot(rim_cell(d, 0, turned), CELLS)
     turn = onehot(d * SIDE + turned, RING)
-    return edge, rim, pick, (gather, order, tips, beyond, facing, turn, *taps)
+    edges, ends = jnp.stack(edges, axis=1), jnp.stack(ends, axis=1)
+    down = jnp.where(edges % 2 == 0, 3, 1) * jnp.where((edges == 0) | (edges == 3), 1, -1)
+    along = jnp.where(edges % 2 == 0, 1, 3) * jnp.where(ends == 1, -1, 1)
+    return jnp.concatenate([edge] + [v.reshape(-1) for v in (down, along, ends)]), (facing, turn)
 
 
 def sigmoid(value):
@@ -180,7 +207,7 @@
     return jnp.dot(a, b, preferred_element_type=jnp.float32)
 
 
-def update_strips(edge, strips, ends, mine, weights, side_patches):
+def update_strips(seams, strips, ends, mine, weights, side_patches):
     rows = len(strips) - 1
     place = iota((RING, C), 0) % SIDE
     moved = []
@@ -189,7 +216,7 @@
         above = jnp.where(place == SIDE - 1, beyond, pltpu.roll(cells, RING - 1, 0))
         moved.append([v.astype(jnp.bfloat16) for v in (below, cells, above)])
     for d in range(4):
-        e = edge[d]
+        e = seams[2 + d]
         for a in range(3):
             across = jnp.where((e == 0) | (e == 3), a, 2 - a)
             for b in range(3):
@@ -203,9 +230,9 @@
     return [after[r * RING : (r + 1) * RING] for r in range(rows)]
 
 
-def update_fans(taps, fans, tips, weights, fan_patches):
+def update_fans(seams, depth, taps, fans, tips, weights, fan_patches):
     columns = taps.shape[1]
-    rows = taps.shape[0] // (FANS * TAPS)
+    _, starts, rows = fan_layout(depth - 1)
     centers = []
     for f in range(FANS):
         known = fans[f]
@@ -214,11 +241,15 @@
         if spare:
             pool.append(jnp.zeros((spare, C), jnp.float32))
         pool = jnp.concatenate(pool, axis=0).astype(jnp.bfloat16)
-        found = dot(taps[f * TAPS * rows : (f + 1) * TAPS * rows, :], pool)
-        for k in range(TAPS):
-            fan_patches[f * rows : (f + 1) * rows, k * C : (k + 1) * C] = found[k * rows : (k + 1) * rows].astype(
-                jnp.bfloat16
-            )
+        found = dot(taps[...], pool)
+        moved = found.astype(jnp.bfloat16)
+        for j in range(depth - 2):
+            down, along = seams[6 + f * BLOCKS + j], seams[6 + (FANS + f) * BLOCKS + j]
+            first, last = starts[j], starts[j + 1]
+            for tap in range(TAPS):
+                to = 4 + (tap // 3 - 1) * down + (tap % 3 - 1) * along
+                lanes = pl.ds(pl.multiple_of(to * C, C), C)
+                fan_patches[f * rows + first : f * rows + last, lanes] = moved[tap * rows + first : tap * rows + last]
         centers.append(found[4 * rows : 5 * rows])
     pre_act = dot(fan_patches[0 : FANS * rows, :], weights)
     after = next_state(jnp.concatenate(centers, axis=0), pre_act).astype(jnp.float32)
@@ -226,14 +257,21 @@
 
 
 def sections_kernel(*refs):
-    index, edge, start, gathered, weights, gather, order, tips_of, beyond, facing, turn = refs[:11]
-    taps, refs = refs[11 : 11 + DEPTH - 2], refs[11 + DEPTH - 2 :]
-    kept, sent, states, padded, patches, side_patches, fan_patches, sems = refs
+    count = 10 + DEPTH - 2
+    seams, sources, refs = refs[0], refs[1 : 1 + count], refs[1 + count :]
+    (kept, sent), held, refs = refs[:2], refs[2 : 2 + count], refs[2 + count :]
+    states, padded, patches, side_patches, fan_patches, load_sems, sems = refs
+    loads = [pltpu.make_async_copy(a, b, load_sems.at[n]) for n, (a, b) in enumerate(zip(sources, held))]
+    for load in loads:
+        load.start()
+    for load in loads[:9]:
+        load.wait()
+    start, gathered, facing, turn, order, tips_of, beyond, entered_low, entered_high, weights, *taps = held
 
     def deliver(i, act):
         for slot, target in ((0, kept), (1, sent)):
 
-            @pl.when(index[slot] == i)
+            @pl.when(seams[slot] == i)
             def _():
                 act(pltpu.make_async_copy(states.at[i], target, sems.at[slot]))
 
@@ -246,14 +284,19 @@
             for d in range(4)
         ]
         strips.append(dot(order[...], jnp.concatenate(found, axis=0).astype(jnp.bfloat16)))
-    fans = []
+    fans, starts = [], fan_layout(DEPTH)[1]
     for f in range(FANS):
         first = SHARE + f * SLOT_ROWS
         found = [
             gathered[q * PICK + first : q * PICK + first + SLOT_ROWS, :].astype(jnp.float32) for q in range(SPLIT)
         ]
         found = jnp.concatenate(found, axis=0).astype(jnp.bfloat16)
-        fans.append(dot(gather[f * FAN_ROWS : (f + 1) * FAN_ROWS, :], found))
+        low, high = dot(entered_low[...], found), dot(entered_high[...], found)
+        row = iota((FAN_ROWS, C), 0)
+        end = jnp.zeros((FAN_ROWS, C), jnp.int32)
+        for j in range(BLOCKS):
+            end = jnp.where(row >= starts[j], seams[6 + (2 * FANS + f) * BLOCKS + j], end)
+        fans.append(jnp.where(end == 1, high, low))
     for i in range(DEPTH):
         state = states.at[i]
         state[CELLS : CELLS + RING, :] = dot(turn[...], strips[0].astype(jnp.bfloat16)).astype(jnp.bfloat16)
@@ -263,40 +306,46 @@
         known = DEPTH - i
         tile = state[0:CELLS, :]
         fill_patches(state, padded, patches)
+        if i == 0:
+            loads[9].wait()
         outer = jnp.concatenate([fan[0:8] for fan in fans], axis=0).astype(jnp.bfloat16)
         ends = dot(beyond[0 : known * RING, :], outer)
         ends = [ends[r * RING : (r + 1) * RING] for r in range(known)]
         mine = dot(facing[...], tile)
-        moved = update_strips(edge, strips, ends, mine, weights[i], side_patches)
+        moved = update_strips(seams, strips, ends, mine, weights[i], side_patches)
         if known > 2:
-            cells = round_up(len(block_cells(known)), 8)
+            cells = fan_layout(known)[2]
             pool = jnp.concatenate([v.astype(jnp.bfloat16) for v in strips], axis=0)
             tips = dot(tips_of[:, 0 : known * RING], pool)
-            fans = update_fans(taps[i], [fan[0:cells] for fan in fans], tips, weights[i], fan_patches)
+            loads[10 + i].wait()
+            fans = update_fans(seams, known, taps[i], [fan[0:cells] for fan in fans], tips, weights[i], fan_patches)
         strips = moved
         states[i + 1, 0:CELLS, :] = next_state(tile.astype(jnp.float32), dot(patches[...], weights[i]))
     for i in range(DEPTH):
         deliver(i, lambda copy: copy.wait())
 
 
-def all_sections(index, edge, start, gathered, weights, maps):
-    vmem = pl.BlockSpec(memory_space=pltpu.VMEM)
+def all_sections(seams, start, gathered, weights, maps):
     smem = pl.BlockSpec(memory_space=pltpu.SMEM)
     hbm = pl.BlockSpec(memory_space=pl.ANY)
     bf16 = jnp.bfloat16
+    fixed = constant_maps()
+    arrays = [start, gathered, *maps, *fixed[:5], weights, *fixed[5:]]
     state = jax.ShapeDtypeStruct((CELLS + RING, C), bf16)
-    fan_rows = FANS * round_up(len(block_cells(DEPTH - 1)), 16)
+    fan_rows = FANS * fan_layout(DEPTH - 1)[2]
     return pl.pallas_call(
         sections_kernel,
         out_shape=(state, state),
-        in_specs=[smem] * 2 + [vmem] * (3 + len(maps)),
+        in_specs=[smem] + [hbm] * len(arrays),
         out_specs=(hbm, hbm),
-        scratch_shapes=[
+        scratch_shapes=[pltpu.VMEM(a.shape, a.dtype) for a in arrays]
+        + [
             pltpu.VMEM((DEPTH, CELLS + RING, C), bf16),
             pltpu.VMEM((SIDE + 2, SIDE + 16, C), jnp.float32),
             pltpu.VMEM((CELLS, TAPS * C), bf16),
             pltpu.VMEM(((DEPTH - 1) * RING, TAPS * C), bf16),
             pltpu.VMEM((fan_rows, TAPS * C), bf16),
+            pltpu.SemaphoreType.DMA((len(arrays),)),
             pltpu.SemaphoreType.DMA((2,)),
         ],
         compiler_params=pltpu.CompilerParams(vmem_limit_bytes=VMEM_BYTES),
@@ -304,7 +353,7 @@
             flops=3 * DEPTH * CELLS * TAPS * C * C, bytes_accessed=16 << 20, transcendentals=DEPTH * CELLS * C
         ),
         name="all_sections",
-    )(index, edge, start, gathered, weights, *maps)
+    )(seams, *arrays)
 
 
 def gradient_kernel(last, index, state, cotangents, weights, before, level, term, padded, patches, cotangent, sem):
@@ -345,7 +394,7 @@
             pltpu.VMEM((CELLS, C), jnp.bfloat16),
             pltpu.SemaphoreType.DMA,
         ],
-        compiler_params=pltpu.CompilerParams(vmem_limit_bytes=VMEM_BYTES),
+        compiler_params=pltpu.CompilerParams(vmem_limit_bytes=GRADIENT_VMEM_BYTES),
         cost_estimate=pl.CostEstimate(
             flops=2 * 2 * CELLS * TAPS * C * C, bytes_accessed=3 << 20, transcendentals=CELLS * C
         ),
@@ -400,7 +449,9 @@
     columns = tiles // rows
     along_row = [[r * columns + c for c in range(columns)] for r in range(rows)]
     along_column = [[r * columns + c for r in range(rows)] for c in range(columns)]
-    edge, rim, pick, maps = selections(neighbor, edge_of, reverse, lax.axis_index("tile"), part, columns)
+    tile = lax.axis_index("tile")
+    rim, pick, found = selections(neighbor, edge_of, reverse, tile, part, columns)
+    seams, maps = own_selections(tile, *found)
     index = jnp.stack([segment, partner]).astype(jnp.int32)
     state = lax.dynamic_index_in_dim(inputs[:, 0], sample, 0, False).reshape(CELLS, C)
     share = dot(rim, state).astype(jnp.bfloat16)
@@ -409,7 +460,7 @@
     picked = lax.all_to_all(picked, "tile", 0, 0, axis_index_groups=along_column)
     picked = add_parts(picked)
     gathered = lax.all_gather(picked, "segment", axis=0, tiled=True, axis_index_groups=teams)
-    kept, sent = all_sections(index, edge, state, gathered, kernels, maps)
+    kept, sent = all_sections(jnp.concatenate([index, seams]), state, gathered, kernels, maps)
     other = lax.ppermute(sent, "segment", [(s, s ^ SPLIT) for s in range(8)])
     cotans = cotangent[0, :, 0].reshape(2, CELLS, C)
     mine, theirs = sample.reshape(1).astype(jnp.int32), (1 - sample).reshape(1).astype(jnp.int32)

time: 216 us -> 175 us (0.81)
  the two profiles are of different devices: /device:TPU:18 before, /device:TPU:22 now
where the time goes in v8:
time: 175 us
  waiting for transfers between devices  46.8 us (27%)
  Pallas kernels  33.3 us (19%)
  starting transfers between devices  27.9 us (16%)
  blocking collectives  27 us (15%)
  between operations  14.8 us (8%)
  local copies, waits for them, and re-layouts  10.9 us (6%)
  other arithmetic  8.37 us (5%)
  matrix products  5.49 us (3%)
    all_to_all x2, waiting for transfers between devices, share_out(): lax.all_to_all(jnp.broadcast_to(block[None], (count,) + block.shape), axi...  28.8 us
    pallas_call x1, Pallas kernels, all_sections(): pl.pallas_call(sections_kernel, out_shape=(state, state), in_specs=[smem]...  28.6 us
    all_to_all x2, starting transfers between devices, share_out(): lax.all_to_all(jnp.broadcast_to(block[None], (count,) + block.shape), axi...  19.6 us
    all_to_all x1, blocking collectives, sum_terms(): lax.all_to_all(term.reshape(count, rows, term.shape[1]), 'tile', 0, 0)  18.8 us
    all_to_all x1, waiting for transfers between devices, local(): lax.all_to_all(picked, 'tile', 0, 0, axis_index_groups=along_column)  10.2 us
    all_gather x1, blocking collectives, local(): lax.all_gather(picked, 'segment', axis=0, tiled=True, axis_index_groups=t...  8.21 us
    ppermute x1, waiting for transfers between devices, local(): other = lax.ppermute(sent, 'segment', [(s, s ^ SPLIT) for s in range(8)])  7.09 us
    dot_general x2, matrix products, dot(): return jnp.dot(a, b, preferred_element_type=jnp.float32)  5.49 us
  transfers between devices with their start and end apart: 5, of which 4 were waited for; matrix products, arithmetic and copies ran while one was open for 11% of the time, Pallas kernels for 1%

profile of v8, /device:TPU:22, one launch (start us, length us, event | category | flops | bytes accessed | tf_op | source)
XLA Modules:
  0.0 174.5 jit_solution(6131061650491155969)
XLA Ops:
  7.4 0.8 copy-done
  8.6 0.9 broadcast_in_dim.734
  9.5 10.3 %all-to-all-start = ((bf16[8,256,128]{2,1,0:T(8,128)(2,1)}), bf16[8,256,128]{2,1,0:T(8,128)(2,1)S(1)}, u32[]{:S(2)}, u32[]{:S(2)}) async-start(bf16[8,256,128]{2,1,0:T(8,128)(2,1)} %broadcast_in_dim.734), calls=%async_computation | async-start | bytes 1048576 | tf_op jit(solution)/shard_map/all_to_all | solution.py:427
  29.1 8.2 %all-to-all-done = bf16[8,256,128]{2,1,0:T(8,128)(2,1)S(1)} async-done(((bf16[8,256,128]{2,1,0:T(8,128)(2,1)}), bf16[8,256,128]{2,1,0:T(8,128)(2,1)S(1)}, u32[]{:S(2)}, u32[]{:S(2)}) %all-to-all-start) | async-done | bytes 524320 | tf_op jit(solution)/shard_map/all_to_all | solution.py:427
  37.3 5.1 %fusion.2 = bf16[2816,128]{1,0:T(8,128)(2,1)} fusion(bf16[2048,128]{1,0:T(8,128)(2,1)S(1)} %bitcast.39, s32[2816]{0:T(1024)S(1)} %fusion.9), kind=kOutput, calls=%fused_computation.3 | convolution fusion | flops 1482522624 | bytes 1256448 | tf_op jit(solution)/shard_map/dot_general | solution.py:207
  42.4 5.2 %all-to-all-start.1 = ((bf16[4,704,128]{2,1,0:T(8,128)(2,1)}), bf16[4,704,128]{2,1,0:T(8,128)(2,1)S(1)}, u32[]{:S(2)}, u32[]{:S(2)}) async-start(bf16[4,704,128]{2,1,0:T(8,128)(2,1)} %bitcast.19), calls=%async_computation.1 | async-start | bytes 1441792 | tf_op jit(solution)/shard_map/all_to_all | solution.py:460
  47.6 0.7 concatenate.14.refs_0_
  49.0 2.6 %multiply_add_fusion.1 = (s32[128]{0:T(128)S(1)}, s32[128]{0:T(128)S(1)}) fusion(s32[]{:T(128)} %bitcast.23, s32[]{:T(128)} %bitcast.22, s32[]{:T(128)} %bitcast.21, s32[]{:T(128)} %bitcast.20), kind=kLoop, calls=%fused_computation.313 | loop fusion | flops 3584 | bytes 1040 | tf_op jit(solution)/shard_map/add | solution.py:171
  51.6 0.7 fusion.5.refs_4_
  52.2 0.8 fusion.4.refs_3_
  53.1 10.2 %all-to-all-done.1.parts = bf16[4,704,128]{2,1,0:T(8,128)(2,1)S(1)} async-done(((bf16[4,704,128]{2,1,0:T(8,128)(2,1)}), bf16[4,704,128]{2,1,0:T(8,128)(2,1)S(1)}, u32[]{:S(2)}, u32[]{:S(2)}) %all-to-all-start.1) | async-done | bytes 720928 | tf_op jit(solution)/shard_map/all_to_all | solution.py:460
  63.3 8.2 %all_gather.6.refs_2_ = bf16[2816,128]{1,0:T(8,128)(2,1)} all-gather(bf16[704,128]{1,0:T(8,128)(2,1)S(1)} %add_parts.1), channel_id=1, replica_groups={{0,32,64,96},{128,160,192,224},{1,33,65,97},{129,161,193,225},{2,34,66,..., dimensions={0}, use_global_device_ids=true | all-gather | bytes 901120 | tf_op jit(solution)/shard_map/all_gather | solution.py:462
  71.5 28.6 %all_sections.1 = (bf16[1152,128]{1,0:T(8,128)(2,1)}, bf16[1152,128]{1,0:T(8,128)(2,1)}) custom-call(s32[174]{0:T(256)} %concatenate.14.refs_0_, bf16[1024,128]{1,0:T(8,128)(2,1)} %bitcast.41, bf16[2816,128]{1,0:T(8,128)(2,1)} %all_gather.6.refs_2_, bf16[128,1024]{1,0:T(8,128)(2,1)} %fusion.4.refs_3_, bf16[128,128]{1,0:T(8,128)(2,1)} %fusion.5.refs_4_, ...), custom_call_target="tpu_custom_call" | custom-call | flops 3623878656 | bytes 16777216 | tf_op jit(solution)/shard_map/all_sections/pallas_call | solution.py:336
  100.1 3.0 %collective-permute-start = (bf16[1152,128]{1,0:T(8,128)(2,1)}, bf16[1152,128]{1,0:T(8,128)(2,1)S(1)}, u32[]{:S(2)}, u32[]{:S(2)}) collective-permute-start(bf16[1152,128]{1,0:T(8,128)(2,1)} %get-tuple-element.10), channel_id=1, source_target_pairs={{0,128},{32,160},{64,192},{96,224},{128,0},{160,32},{192,64},{224,... | collective-permute-start | bytes 884744 | tf_op jit(solution)/shard_map/ppermute | solution.py:464
  103.2 1.0 copy-done.3
  104.2 2.3 %gradient.2 = (bf16[1024,128]{1,0:T(8,128)(2,1)S(1)}, f32[128,1152]{1,0:T(8,128)S(1)}) custom-call(s32[1]{0:T(128)} %bitcast.refs_0_, bf16[1152,128]{1,0:T(8,128)(2,1)S(1)} %copy-done.3, bf16[2,1024,128]{2,1,0:T(8,128)(2,1)S(1)} %bitcast.34, bf16[1152,128]{1,0:T(8,128)(2,1)S(1)} %bitcast.32, f32[128,1152]{1,0:T(8,128)S(1)} %broadcast_in_dim.739.refs_4_), custom_call_target="tpu_custom_call" | custom-call | flops 603979776 | bytes 3145728 | tf_op jit(solution)/shard_map/gradient/pallas_call | solution.py:383
  106.5 7.1 %collective-permute-done.refs_1_ = bf16[1152,128]{1,0:T(8,128)(2,1)S(1)} collective-permute-done((bf16[1152,128]{1,0:T(8,128)(2,1)}, bf16[1152,128]{1,0:T(8,128)(2,1)S(1)}, u32[]{:S(2)}, u32[]{:S(2)}) %collective-permute-start) | collective-permute-done | bytes 294944 | tf_op jit(solution)/shard_map/ppermute | solution.py:464
  113.6 2.4 %gradient.3 = (bf16[1024,128]{1,0:T(8,128)(2,1)S(1)}, bf16[1152,128]{1,0:T(8,128)(2,1)S(1)}) custom-call(s32[1]{0:T(128)} %bitcast.26.refs_0_, bf16[1152,128]{1,0:T(8,128)(2,1)S(1)} %collective-permute-done.refs_1_, bf16[2,1024,128]{2,1,0:T(8,128)(2,1)S(1)} %bitcast.35, bf16[1152,128]{1,0:T(8,128)(2,1)S(1)} %bitcast.33, ...), custom_call_target="tpu_custom_call" | custom-call | flops 603979776 | bytes 3145728 | tf_op jit(solution)/shard_map/gradient/pallas_call | solution.py:383
  116.0 18.8 %all_to_all.20 = bf16[32,36,128]{2,1,0:T(8,128)(2,1)S(1)} all-to-all(bf16[32,36,128]{2,1,0:T(8,128)(2,1)S(1)} %reshape.958), channel_id=1, replica_groups=mesh['dp'=2,'segment'=8,'tile'=32] {'tile'}, dimensions={0} | all-to-all | bytes 589824 | tf_op jit(solution)/shard_map/all_to_all | solution.py:435
  134.9 0.9 broadcast_in_dim.740
  135.8 9.3 %all-to-all-start.3 = ((bf16[64,36,128]{2,1,0:T(8,128)(2,1)}), bf16[64,36,128]{2,1,0:T(8,128)(2,1)S(1)}, u32[]{:S(2)}, u32[]{:S(2)}) async-start(bf16[64,36,128]{2,1,0:T(8,128)(2,1)} %broadcast_in_dim.740), calls=%async_computation.3 | async-start | bytes 1310720 | tf_op jit(solution)/shard_map/all_to_all | solution.py:427
  145.2 0.8 pad_maximum_fusion
  146.0 20.6 %all-to-all-done.3 = bf16[64,36,128]{2,1,0:T(8,128)(2,1)S(1)} async-done(((bf16[64,36,128]{2,1,0:T(8,128)(2,1)}), bf16[64,36,128]{2,1,0:T(8,128)(2,1)S(1)}, u32[]{:S(2)}, u32[]{:S(2)}) %all-to-all-start.3) | async-done | bytes 589856 | tf_op jit(solution)/shard_map/all_to_all | solution.py:427
  166.7 0.9 reduce_sum.262
  (169 shorter events, 10.4 us)
Async XLA Ops:
  7.2 16.9 %copy-start.20 = (pred[56]{0:T(512)(128)(4,1)S(1)}, pred[56]{0:T(512)(128)(4,1)}, u32[]{:S(2)}) copy-start(pred[56]{0:T(512)(128)(4,1)} %constant.561.clone) | copy-start | bytes 172
  7.2 17.0 %copy-start.19 = (pred[56]{0:T(512)(128)(4,1)S(1)}, pred[56]{0:T(512)(128)(4,1)}, u32[]{:S(2)}) copy-start(pred[56]{0:T(512)(128)(4,1)} %constant.562.clone) | copy-start | bytes 172
  7.2 17.1 %copy-start.18 = (pred[56]{0:T(512)(128)(4,1)S(1)}, pred[56]{0:T(512)(128)(4,1)}, u32[]{:S(2)}) copy-start(pred[56]{0:T(512)(128)(4,1)} %constant.563.clone) | copy-start | bytes 172
  7.2 17.2 %copy-start.17 = (pred[56]{0:T(512)(128)(4,1)S(1)}, pred[56]{0:T(512)(128)(4,1)}, u32[]{:S(2)}) copy-start(pred[56]{0:T(512)(128)(4,1)} %constant.564.clone) | copy-start | bytes 172
  7.2 17.3 %copy-start.16 = (pred[56]{0:T(512)(128)(4,1)S(1)}, pred[56]{0:T(512)(128)(4,1)}, u32[]{:S(2)}) copy-start(pred[56]{0:T(512)(128)(4,1)} %constant.565.clone) | copy-start | bytes 172
  7.2 17.4 %copy-start.15 = (pred[56]{0:T(512)(128)(4,1)S(1)}, pred[56]{0:T(512)(128)(4,1)}, u32[]{:S(2)}) copy-start(pred[56]{0:T(512)(128)(4,1)} %constant.566.clone) | copy-start | bytes 172
  7.3 17.5 %copy-start.14 = (pred[56]{0:T(512)(128)(4,1)S(1)}, pred[56]{0:T(512)(128)(4,1)}, u32[]{:S(2)}) copy-start(pred[56]{0:T(512)(128)(4,1)} %constant.567.clone) | copy-start | bytes 172
  7.3 20.5 %copy-start.12 = (s32[56]{0:T(128)S(1)}, s32[56]{0:T(128)}, u32[]{:S(2)}) copy-start(s32[56]{0:T(128)} %constant.568.clone) | copy-start | bytes 676
  7.3 20.5 %copy-start.11 = (s32[56]{0:T(128)S(1)}, s32[56]{0:T(128)}, u32[]{:S(2)}) copy-start(s32[56]{0:T(128)} %constant.572.clone) | copy-start | bytes 676
  7.3 20.6 %copy-start.10 = (s32[56]{0:T(128)S(1)}, s32[56]{0:T(128)}, u32[]{:S(2)}) copy-start(s32[56]{0:T(128)} %constant.569.clone) | copy-start | bytes 676
  7.3 20.7 %copy-start.9 = (s32[56]{0:T(128)S(1)}, s32[56]{0:T(128)}, u32[]{:S(2)}) copy-start(s32[56]{0:T(128)} %constant.570.clone) | copy-start | bytes 676
  7.3 20.8 %copy-start.8 = (s32[56]{0:T(128)S(1)}, s32[56]{0:T(128)}, u32[]{:S(2)}) copy-start(s32[56]{0:T(128)} %constant.571.clone) | copy-start | bytes 676
  7.3 20.9 %copy-start.13 = (pred[56]{0:T(512)(128)(4,1)S(1)}, pred[56]{0:T(512)(128)(4,1)}, u32[]{:S(2)}) copy-start(pred[56]{0:T(512)(128)(4,1)} %constant.573.clone) | copy-start | bytes 172
  7.3 13.2 %copy-start.7 = (s32[32,4]{0,1:T(4,128)S(1)}, s32[32,4]{0,1:T(4,128)}, u32[]{:S(2)}) copy-start(s32[32,4]{0,1:T(4,128)} %param.45) | copy-start | bytes 1540
  7.4 13.2 %copy-start.6 = (s32[32,4]{0,1:T(4,128)S(1)}, s32[32,4]{0,1:T(4,128)}, u32[]{:S(2)}) copy-start(s32[32,4]{0,1:T(4,128)} %param.46) | copy-start | bytes 1540
  7.4 13.2 %copy-start.5 = (s32[32,4]{0,1:T(4,128)S(1)}, s32[32,4]{0,1:T(4,128)}, u32[]{:S(2)}) copy-start(s32[32,4]{0,1:T(4,128)} %param.47) | copy-start | bytes 1540
  8.2 34.2 %copy-start.4 = (bf16[1,1,32,32,128]{4,3,2,1,0:T(8,128)(2,1)}, bf16[1,1,32,32,128]{4,3,2,1,0:T(8,128)(2,1)S(1)}, u32[]{:S(2)}) copy-start(bf16[1,1,32,32,128]{4,3,2,1,0:T(8,128)(2,1)S(1)} %constant_dynamic-slice_fusion) | copy-start | bytes 786436
  9.5 27.8 %all-to-all-start = ((bf16[8,256,128]{2,1,0:T(8,128)(2,1)}), bf16[8,256,128]{2,1,0:T(8,128)(2,1)S(1)}, u32[]{:S(2)}, u32[]{:S(2)}) async-start(bf16[8,256,128]{2,1,0:T(8,128)(2,1)} %broadcast_in_dim.734), calls=%async_computation | async-start | bytes 1048576 | tf_op jit(solution)/shard_map/all_to_all | solution.py:427
  19.8 51.8 %all-gather.2.cloned.1.call-start = ((), (), s32[]{:S(2)}) async-start(), calls=%async_computation.4 | async-start | bytes 2654208 | tf_op jit(solution)/shard_map/all_gather | solution.py:446
  42.4 20.8 %all-to-all-start.1 = ((bf16[4,704,128]{2,1,0:T(8,128)(2,1)}), bf16[4,704,128]{2,1,0:T(8,128)(2,1)S(1)}, u32[]{:S(2)}, u32[]{:S(2)}) async-start(bf16[4,704,128]{2,1,0:T(8,128)(2,1)} %bitcast.19), calls=%async_computation.1 | async-start | bytes 1441792 | tf_op jit(solution)/shard_map/all_to_all | solution.py:460
  71.5 31.7 %copy-start.1 = (bf16[1,1152,128]{2,1,0:T(8,128)(2,1)S(1)}, bf16[1,1152,128]{2,1,0:T(8,128)(2,1)}, u32[]{:S(2)}) copy-start(bf16[1,1152,128]{2,1,0:T(8,128)(2,1)} %param.48) | copy-start | bytes 884740
  71.5 31.7 %copy-start.2 = (bf16[1,2,1,32,32,128]{5,4,3,2,1,0:T(8,128)(2,1)S(1)}, bf16[1,2,1,32,32,128]{5,4,3,2,1,0:T(8,128)(2,1)}, u32[]{:S(2)}) copy-start(bf16[1,2,1,32,32,128]{5,4,3,2,1,0:T(8,128)(2,1)} %param.49) | copy-start | bytes 1572868
  100.1 13.4 %collective-permute-start = (bf16[1152,128]{1,0:T(8,128)(2,1)}, bf16[1152,128]{1,0:T(8,128)(2,1)S(1)}, u32[]{:S(2)}, u32[]{:S(2)}) collective-permute-start(bf16[1152,128]{1,0:T(8,128)(2,1)} %get-tuple-element.10), channel_id=1, source_target_pairs={{0,128},{32,160},{64,192},{96,224},{128,0},{160,32},{192,64},{224,... | collective-permute-start | bytes 884744 | tf_op jit(solution)/shard_map/ppermute | solution.py:464
  135.8 30.8 %all-to-all-start.3 = ((bf16[64,36,128]{2,1,0:T(8,128)(2,1)}), bf16[64,36,128]{2,1,0:T(8,128)(2,1)S(1)}, u32[]{:S(2)}, u32[]{:S(2)}) async-start(bf16[64,36,128]{2,1,0:T(8,128)(2,1)} %broadcast_in_dim.740), calls=%async_computation.3 | async-start | bytes 1310720 | tf_op jit(solution)/shard_map/all_to_all | solution.py:427
  (2 other events, 2.0 us)
Sparse Core Ops, SparseCore 0:
  22.7 31.1 all-gather.1
